TPU v7x, 32 devices: a whole 2x2x4 slice. The times are simulated.
32 devices in a mesh: shard: 4 (over z), context: 4 (over y, core), tensor: 2 (over x).
Axes of the slice: x: 2, y: 2, z: 4, core: 2. Of those that a mesh axis runs over, the one named last changes fastest.
Arguments:
- tokens: bfloat16 [4, 2048, 2048], P('shard', 'context'), may hold values from -6 to 6
- layer_input: bfloat16 [4, 2048, 256], P('shard', 'context'), may hold values from -6 to 6
- segments: int32 [4, 2048], P('shard'), may hold values from 0 to 65, as said below
- adapter_ids: int32 [4], P('shard'), may hold values from 0 to 7
- cotangent: bfloat16 [4, 2048, 2048], P('shard', 'context'), may hold values from -6 to 6
- w_query: bfloat16 [2048, 2048], P('shard', 'tensor'), may hold values from -0.125 to 0.125
- w_key: bfloat16 [2048, 512], P('shard', 'tensor'), may hold values from -0.125 to 0.125
- w_value: bfloat16 [2048, 512], P('shard', 'tensor'), may hold values from -0.125 to 0.125
- w_output: bfloat16 [2048, 2048], P('tensor', 'shard'), may hold values from -0.125 to 0.125
- w_gate: bfloat16 [2048, 8192], P('shard', 'tensor'), may hold values from -0.125 to 0.125
- w_up: bfloat16 [2048, 8192], P('shard', 'tensor'), may hold values from -0.125 to 0.125
- w_down: bfloat16 [8192, 2048], P('tensor', 'shard'), may hold values from -0.0625 to 0.0625
- laurel_left: bfloat16 [2048, 64], P('shard'), may hold values from -0.125 to 0.125
- laurel_right: bfloat16 [64, 2048], P(None, 'shard'), may hold values from -0.75 to 0.75
- input_gate: bfloat16 [2048, 256], P('shard'), may hold values from -0.125 to 0.125
- input_proj: bfloat16 [256, 2048], P(None, 'shard'), may hold values from -0.375 to 0.375
- gain_in: float32 [2048], replicated, may hold values from 0.25 to 1.75
- gain_attn: float32 [2048], replicated, may hold values from 0.25 to 1.75
- gain_laurel: float32 [2048], replicated, may hold values from 0.25 to 1.75
- gain_pre: float32 [2048], replicated, may hold values from 0.25 to 1.75
- gain_post: float32 [2048], replicated, may hold values from 0.25 to 1.75
- gain_layer: float32 [2048], replicated, may hold values from 0.25 to 1.75
- gain_query: float32 [256], replicated, may hold values from 0.25 to 1.75
- gain_key: float32 [256], replicated, may hold values from 0.25 to 1.75
- adapt_attn_in: bfloat16 [8, 2048, 48], replicated, may hold values from -0.125 to 0.125
- adapt_query_out: bfloat16 [8, 16, 2048], P(None, None, 'tensor'), may hold values from -0.59765625 to 0.59765625
- adapt_kv_out: bfloat16 [8, 2, 16, 512], P(None, None, None, 'tensor'), may hold values from -0.59765625 to 0.59765625
- adapt_out_in: bfloat16 [8, 2048, 16], P(None, 'tensor'), may hold values from -0.125 to 0.125
- adapt_out_out: bfloat16 [8, 16, 2048], replicated, may hold values from -0.59765625 to 0.59765625
- adapt_ffn_in: bfloat16 [8, 2048, 32], replicated, may hold values from -0.125 to 0.125
- adapt_gu_out: bfloat16 [8, 2, 16, 8192], P(None, None, None, 'tensor'), may hold values from -0.59765625 to 0.59765625
- adapt_down_in: bfloat16 [8, 8192, 16], P(None, 'tensor'), may hold values from -0.0625 to 0.0625
- adapt_down_out: bfloat16 [8, 16, 2048], replicated, may hold values from -0.59765625 to 0.59765625
Outputs:
- layer_output: bfloat16 [4, 2048, 2048], P('shard', 'context')
- input_grad: bfloat16 [4, 2048, 2048], P('shard', 'context')
- grad_attn_in: float32 [8, 2048, 48], replicated
- grad_query_out: float32 [8, 16, 2048], replicated
- grad_kv_out: float32 [8, 2, 16, 512], replicated
- grad_out_in: float32 [8, 2048, 16], replicated
- grad_out_out: float32 [8, 16, 2048], replicated
- grad_ffn_in: float32 [8, 2048, 32], replicated
- grad_gu_out: float32 [8, 2, 16, 8192], replicated
- grad_down_in: float32 [8, 8192, 16], replicated
- grad_down_out: float32 [8, 16, 2048], replicated
Inputs may be any that keep to these rules, and one draw needn't show every extreme that they name: `segments`: segment numbers start at 0 in every sequence and never fall from one position to the next; each number marks one document; every sequence holds 66 documents.
All inputs are finite; a program needn't handle non-finite values.
Results may differ from a plain program's by a relative error of at most 0.019.
Values may be sent and summed in bfloat16 or wider, within the bound.
A program may use at most 320 MiB of HBM per device.

v0:
```python
from functools import partial
import math

import jax
import jax.numpy as jnp
from jax import lax
from jax.sharding import PartitionSpec as P

WINDOW = 512


EPSILON = 1e-06
HIGHEST = lax.Precision.HIGHEST
ROOT_HALF = 0.7071067811865476


def shifted(array, axis, by):
    count = lax.axis_size(axis)
    pairs = [(i, i + by) for i in range(count) if 0 <= i + by < count]
    return lax.ppermute(array, axis, pairs)


def rms_norm(values, scaling):
    return values * lax.rsqrt(jnp.mean(values * values, axis=-1, keepdims=True) + EPSILON) * scaling


def gelu_tanh(values):
    return jax.nn.gelu(values, approximate=True)


def rotate_half(values, cosine, sine_table):
    middle = values.shape[-1] // 2
    former = values[..., :middle]
    latter = values[..., middle:]
    return jnp.concatenate(
        [former * cosine - latter * sine_table, latter * cosine + former * sine_table], axis=-1
    )


def doc_positions(segment_ids):
    counter = jnp.broadcast_to(
        jnp.arange(segment_ids.shape[-1], dtype=jnp.int32), segment_ids.shape
    )
    boundary = jnp.concatenate(
        [
            jnp.ones(segment_ids.shape[:-1] + (1,), dtype=jnp.bool_),
            segment_ids[..., 1:] != segment_ids[..., :-1],
        ],
        axis=-1,
    )
    starts = lax.cummax(jnp.where(boundary, counter, 0), axis=segment_ids.ndim - 1)
    return counter - starts


def rope_tables(positions, head_size):
    frequency = jnp.exp(
        jnp.arange(head_size // 2, dtype=jnp.float32) * (-2.0 * math.log(10000.0) / head_size)
    )
    angles = positions.astype(jnp.float32)[..., None] * frequency
    return (jnp.cos(angles), jnp.sin(angles))


def matmul(left_op, right_op):
    return jnp.dot(left_op, right_op, preferred_element_type=jnp.float32)


def matmul_t(left_op, right_op):
    return lax.dot_general(
        left_op, right_op, (((1,), (1,)), ((), ())), preferred_element_type=jnp.float32
    )


def select_table(onehot, adapter_table):
    return jnp.einsum("sa,a...->s...", onehot, adapter_table.astype(jnp.float32), precision=HIGHEST)


def adapt_in(activations, picked, seq_count):
    shaped = activations.reshape(seq_count, -1, activations.shape[-1])
    return jnp.einsum("slk,skr->slr", shaped, picked, preferred_element_type=jnp.float32).reshape(
        activations.shape[0], -1
    )


def adapt_out(code_rows, picked, seq_count):
    shaped = code_rows.reshape(seq_count, -1, code_rows.shape[-1])
    return jnp.einsum("slr,sre->sle", shaped, picked, precision=HIGHEST).reshape(
        code_rows.shape[0], -1
    )


def adapt_out_t(gradient, picked, seq_count):
    shaped = gradient.reshape(seq_count, -1, gradient.shape[-1])
    return jnp.einsum("sle,sre->slr", shaped, picked, precision=HIGHEST).reshape(
        gradient.shape[0], -1
    )


def adapt_in_t(code_rows, picked, seq_count):
    shaped = code_rows.reshape(seq_count, -1, code_rows.shape[-1])
    return jnp.einsum(
        "slr,skr->slk", shaped, picked.astype(jnp.float32), precision=HIGHEST
    ).reshape(code_rows.shape[0], -1)


def outer_rows(activations, code_rows, seq_count):
    left_rows = activations.reshape(seq_count, -1, activations.shape[-1]).astype(jnp.float32)
    right_rows = code_rows.reshape(seq_count, -1, code_rows.shape[-1])
    return jnp.einsum("slk,slr->skr", left_rows, right_rows, precision=HIGHEST)


def place_part(part_grad, axis_pos, slot_index, part_count):
    full_shape = list(part_grad.shape)
    full_shape[axis_pos] = part_grad.shape[axis_pos] * part_count
    return lax.dynamic_update_slice_in_dim(
        jnp.zeros(full_shape, jnp.float32),
        part_grad,
        slot_index * part_grad.shape[axis_pos],
        axis_pos,
    )


def body(
    tokens,
    layer_input,
    segments,
    adapter_ids,
    cotangent,
    w_query,
    w_key,
    w_value,
    w_output,
    w_gate,
    w_up,
    w_down,
    laurel_left,
    laurel_right,
    input_gate,
    input_proj,
    gain_in,
    gain_attn,
    gain_laurel,
    gain_pre,
    gain_post,
    gain_layer,
    gain_query,
    gain_key,
    adapt_attn_in,
    adapt_query_out,
    adapt_kv_out,
    adapt_out_in,
    adapt_out_out,
    adapt_ffn_in,
    adapt_gu_out,
    adapt_down_in,
    adapt_down_out,
):
    seq_count, local_len, width_model = tokens.shape
    token_count = seq_count * local_len
    head_size = gain_query.shape[0]
    rank_size = adapt_query_out.shape[1]
    query_heads = adapt_query_out.shape[2] // head_size
    kv_heads = adapt_kv_out.shape[3] // head_size
    group_size = query_heads // kv_heads
    tensor_count = lax.axis_size("tensor")
    tensor_slot = lax.axis_index("tensor")
    context_slot = lax.axis_index("context")
    (
        full_query,
        full_key,
        full_value,
        full_output,
        full_gate,
        full_up,
        full_down,
        full_left,
        full_right,
        full_layer_gate,
        full_layer_proj,
    ) = (
        lax.all_gather(w_query, "shard", axis=0, tiled=True),
        lax.all_gather(w_key, "shard", axis=0, tiled=True),
        lax.all_gather(w_value, "shard", axis=0, tiled=True),
        lax.all_gather(w_output, "shard", axis=1, tiled=True),
        lax.all_gather(w_gate, "shard", axis=0, tiled=True),
        lax.all_gather(w_up, "shard", axis=0, tiled=True),
        lax.all_gather(w_down, "shard", axis=1, tiled=True),
        lax.all_gather(laurel_left, "shard", axis=0, tiled=True),
        lax.all_gather(laurel_right, "shard", axis=1, tiled=True),
        lax.all_gather(input_gate, "shard", axis=0, tiled=True),
        lax.all_gather(input_proj, "shard", axis=1, tiled=True),
    )
    adapter_count = adapt_attn_in.shape[0]
    onehot = (adapter_ids[:, None] == jnp.arange(adapter_count, dtype=jnp.int32)[None, :]).astype(
        jnp.float32
    )
    pick_attn_in = select_table(onehot, adapt_attn_in).astype(jnp.bfloat16)
    pick_query_out = select_table(onehot, adapt_query_out)
    pick_kv_out = select_table(onehot, adapt_kv_out)
    pick_out_in = select_table(onehot, adapt_out_in).astype(jnp.bfloat16)
    pick_out_out = select_table(onehot, adapt_out_out)
    pick_ffn_in = select_table(onehot, adapt_ffn_in).astype(jnp.bfloat16)
    pick_gu_out = select_table(onehot, adapt_gu_out)
    pick_down_in = select_table(onehot, adapt_down_in).astype(jnp.bfloat16)
    pick_down_out = select_table(onehot, adapt_down_out)
    start_pos = context_slot * local_len
    own_pos = lax.dynamic_slice_in_dim(doc_positions(segments), start_pos, local_len, 1).reshape(
        token_count
    )
    cosine, sine_table = rope_tables(own_pos, head_size)
    cosine = cosine[:, None, :]
    sine_table = sine_table[:, None, :]
    inputs_f = tokens.reshape(token_count, width_model).astype(jnp.float32)
    normed, normed_back = jax.vjp(partial(rms_norm, scaling=gain_in), inputs_f)
    normed_b = normed.astype(jnp.bfloat16)
    code_attn = adapt_in(normed_b, pick_attn_in, seq_count)
    query_lin = matmul(normed_b, full_query) + adapt_out(
        code_attn[:, :rank_size], pick_query_out, seq_count
    )
    key_lin = matmul(normed_b, full_key) + adapt_out(
        code_attn[:, rank_size : 2 * rank_size], pick_kv_out[:, 0], seq_count
    )
    value_lin = matmul(normed_b, full_value) + adapt_out(
        code_attn[:, 2 * rank_size :], pick_kv_out[:, 1], seq_count
    )

    def prepare(query_in, key_in, value_in):
        query_rot = rotate_half(
            rms_norm(query_in.reshape(token_count, query_heads, head_size), gain_query),
            cosine,
            sine_table,
        )
        key_rot = rotate_half(
            rms_norm(key_in.reshape(token_count, kv_heads, head_size), gain_key), cosine, sine_table
        )
        value_nrm = rms_norm(value_in.reshape(token_count, kv_heads, head_size), 1.0)
        return (query_rot, key_rot, value_nrm)

    (query_rot, key_rot, value_nrm), prepare_back = jax.vjp(prepare, query_lin, key_lin, value_lin)
    query_b = query_rot.astype(jnp.bfloat16).reshape(
        seq_count, local_len, kv_heads, group_size, head_size
    )
    kv_own = (
        jnp.stack([key_rot, value_nrm])
        .astype(jnp.bfloat16)
        .reshape(2, seq_count, local_len, kv_heads, head_size)
    )
    kv_prior = shifted(kv_own, "context", 1)
    kv_all = jnp.concatenate([kv_prior, kv_own], axis=2)
    query_pos = start_pos + jnp.arange(local_len, dtype=jnp.int32)
    key_pos = start_pos - local_len + jnp.arange(2 * local_len, dtype=jnp.int32)
    seg_query = lax.dynamic_slice_in_dim(segments, start_pos, local_len, 1)
    seg_prior = lax.dynamic_slice_in_dim(
        segments, jnp.maximum(start_pos - local_len, 0), local_len, 1
    )
    seg_keys = jnp.concatenate([seg_prior, seg_query], axis=1)
    distance = query_pos[:, None] - key_pos[None, :]
    window_ok = (distance >= 0) & (distance < WINDOW) & (key_pos >= 0)[None, :]
    allowed = (seg_query[:, :, None] == seg_keys[:, None, :]) & window_ok[None]
    allowed = allowed[:, None, None]
    score_scale = 1.0 / math.sqrt(head_size)

    def masked_scores():
        raw_scores = (
            jnp.einsum("slkgd,smkd->skglm", query_b, kv_all[0], preferred_element_type=jnp.float32)
            * score_scale
        )
        return jnp.where(allowed, raw_scores, -1e30)

    scores = masked_scores()
    row_max = jnp.max(scores, axis=-1, keepdims=True)
    exponent = jnp.exp(scores - row_max)
    row_total = jnp.sum(exponent, axis=-1, keepdims=True)
    log_total = row_max + jnp.log(row_total)
    attn_probs = (exponent / row_total).astype(jnp.bfloat16)
    attended = jnp.einsum(
        "skglm,smkd->slkgd", attn_probs, kv_all[1], preferred_element_type=jnp.float32
    )
    attended_b = attended.reshape(token_count, query_heads * head_size).astype(jnp.bfloat16)
    code_out = adapt_in(attended_b, pick_out_in, seq_count)
    attn_part = matmul(attended_b, full_output) + adapt_out(code_out, pick_out_out, seq_count)
    attn_proj = lax.psum(attn_part.astype(jnp.bfloat16), "tensor").astype(jnp.float32)
    laurel_mid = matmul(normed_b, full_left).astype(jnp.bfloat16)
    laurel_end = matmul(laurel_mid, full_right)

    def combine(inputs_in, normed_in, attn_in, laurel_in):
        return (
            inputs_in + rms_norm(attn_in, gain_attn) + normed_in + rms_norm(laurel_in, gain_laurel)
        ) * ROOT_HALF

    combined, combine_back = jax.vjp(combine, inputs_f, normed, attn_proj, laurel_end)
    ffn_input, pre_ffn_back = jax.vjp(partial(rms_norm, scaling=gain_pre), combined)
    ffn_input_b = ffn_input.astype(jnp.bfloat16)
    code_ffn = adapt_in(ffn_input_b, pick_ffn_in, seq_count)
    gate_lin = matmul(ffn_input_b, full_gate) + adapt_out(
        code_ffn[:, :rank_size], pick_gu_out[:, 0], seq_count
    )
    up_lin = matmul(ffn_input_b, full_up) + adapt_out(
        code_ffn[:, rank_size:], pick_gu_out[:, 1], seq_count
    )

    def activate(gate_in, up_in):
        return gelu_tanh(gate_in) * up_in

    hidden_act, activate_back = jax.vjp(activate, gate_lin, up_lin)
    hidden_b = hidden_act.astype(jnp.bfloat16)
    code_down = adapt_in(hidden_b, pick_down_in, seq_count)
    down_part = matmul(hidden_b, full_down) + adapt_out(code_down, pick_down_out, seq_count)
    down_proj = lax.psum(down_part.astype(jnp.bfloat16), "tensor").astype(jnp.float32)

    def after_step(combined_in, down_in):
        return combined_in + rms_norm(down_in, gain_post)

    after_ffn, after_back = jax.vjp(after_step, combined, down_proj)
    layer_gate = matmul(after_ffn.astype(jnp.bfloat16), full_layer_gate)
    per_layer = layer_input.reshape(token_count, -1).astype(jnp.float32)

    def mix_layer(gate_in):
        return gelu_tanh(gate_in) * per_layer

    layer_mix, mix_back = jax.vjp(mix_layer, layer_gate)
    layer_proj = matmul(layer_mix.astype(jnp.bfloat16), full_layer_proj)

    def finish(after_in, proj_in):
        return after_in + rms_norm(proj_in, gain_layer)

    output_f, finish_back = jax.vjp(finish, after_ffn, layer_proj)
    grad_output = cotangent.reshape(token_count, width_model).astype(jnp.float32)
    grad_after, grad_lproj = finish_back(grad_output)
    (grad_lgate,) = mix_back(matmul_t(grad_lproj.astype(jnp.bfloat16), full_layer_proj))
    grad_after = grad_after + matmul_t(grad_lgate.astype(jnp.bfloat16), full_layer_gate)
    grad_comb, grad_down = after_back(grad_after)
    grad_down_b = grad_down.astype(jnp.bfloat16)
    grad_down_r = grad_down_b.astype(jnp.float32)
    code_down_back = adapt_out_t(grad_down_r, pick_down_out, seq_count)
    term_down_out = outer_rows(code_down, grad_down_r, seq_count)
    term_down_in = outer_rows(hidden_b, code_down_back, seq_count)
    grad_hidden = matmul_t(grad_down_b, full_down) + adapt_in_t(
        code_down_back, pick_down_in, seq_count
    )
    grad_gate, grad_up = activate_back(grad_hidden)
    grad_gate_b = grad_gate.astype(jnp.bfloat16)
    grad_up_b = grad_up.astype(jnp.bfloat16)
    grad_gate_r = grad_gate_b.astype(jnp.float32)
    grad_up_r = grad_up_b.astype(jnp.float32)
    code_ffn_back = jnp.concatenate(
        [
            adapt_out_t(grad_gate_r, pick_gu_out[:, 0], seq_count),
            adapt_out_t(grad_up_r, pick_gu_out[:, 1], seq_count),
        ],
        axis=1,
    )
    term_gu_out = jnp.stack(
        [
            outer_rows(code_ffn[:, :rank_size], grad_gate_r, seq_count),
            outer_rows(code_ffn[:, rank_size:], grad_up_r, seq_count),
        ],
        axis=1,
    )
    term_ffn_in = outer_rows(ffn_input_b, code_ffn_back, seq_count)
    grad_ffn_part = (
        matmul_t(grad_gate_b, full_gate)
        + matmul_t(grad_up_b, full_up)
        + adapt_in_t(code_ffn_back, pick_ffn_in, seq_count)
    )
    grad_ffn_input = lax.psum(grad_ffn_part.astype(jnp.bfloat16), "tensor").astype(jnp.float32)
    grad_comb = grad_comb + pre_ffn_back(grad_ffn_input)[0]
    grad_inputs, grad_normed, grad_attn, grad_laurel = combine_back(grad_comb)
    grad_laurel_mid = matmul_t(grad_laurel.astype(jnp.bfloat16), full_right).astype(jnp.bfloat16)
    grad_normed = grad_normed + matmul_t(grad_laurel_mid, full_left)
    grad_attn_b = grad_attn.astype(jnp.bfloat16)
    grad_attn_r = grad_attn_b.astype(jnp.float32)
    code_out_back = adapt_out_t(grad_attn_r, pick_out_out, seq_count)
    term_out_out = outer_rows(code_out, grad_attn_r, seq_count)
    term_out_in = outer_rows(attended_b, code_out_back, seq_count)
    grad_attended = (
        matmul_t(grad_attn_b, full_output) + adapt_in_t(code_out_back, pick_out_in, seq_count)
    ).astype(jnp.bfloat16)
    grad_heads = grad_attended.reshape(seq_count, local_len, kv_heads, group_size, head_size)
    recomputed = jnp.exp(masked_scores() - log_total)
    grad_probs = jnp.einsum(
        "slkgd,smkd->skglm", grad_heads, kv_all[1], preferred_element_type=jnp.float32
    )
    grad_scores = (
        recomputed * (grad_probs - jnp.sum(recomputed * grad_probs, axis=-1, keepdims=True))
    ).astype(jnp.bfloat16)
    grad_query = (
        jnp.einsum("skglm,smkd->slkgd", grad_scores, kv_all[0], preferred_element_type=jnp.float32)
        * score_scale
    )
    grad_keys = (
        jnp.einsum("skglm,slkgd->smkd", grad_scores, query_b, preferred_element_type=jnp.float32)
        * score_scale
    )
    grad_values = jnp.einsum(
        "skglm,slkgd->smkd",
        recomputed.astype(jnp.bfloat16),
        grad_heads,
        preferred_element_type=jnp.float32,
    )
    grad_kv = jnp.stack([grad_keys, grad_values])
    grad_kv_later = shifted(grad_kv[:, :, :local_len].astype(jnp.bfloat16), "context", -1).astype(
        jnp.float32
    )
    grad_kv_own = grad_kv[:, :, local_len:] + grad_kv_later
    grad_qlin, grad_klin, grad_vlin = prepare_back(
        (
            grad_query.reshape(token_count, query_heads, head_size),
            grad_kv_own[0].reshape(token_count, kv_heads, head_size),
            grad_kv_own[1].reshape(token_count, kv_heads, head_size),
        )
    )
    grad_qlin_b = grad_qlin.astype(jnp.bfloat16)
    grad_klin_b = grad_klin.astype(jnp.bfloat16)
    grad_vlin_b = grad_vlin.astype(jnp.bfloat16)
    grad_qlin_r = grad_qlin_b.astype(jnp.float32)
    grad_klin_r = grad_klin_b.astype(jnp.float32)
    grad_vlin_r = grad_vlin_b.astype(jnp.float32)
    code_attn_back = jnp.concatenate(
        [
            adapt_out_t(grad_qlin_r, pick_query_out, seq_count),
            adapt_out_t(grad_klin_r, pick_kv_out[:, 0], seq_count),
            adapt_out_t(grad_vlin_r, pick_kv_out[:, 1], seq_count),
        ],
        axis=1,
    )
    term_query_out = outer_rows(code_attn[:, :rank_size], grad_qlin_r, seq_count)
    term_kv_out = jnp.stack(
        [
            outer_rows(code_attn[:, rank_size : 2 * rank_size], grad_klin_r, seq_count),
            outer_rows(code_attn[:, 2 * rank_size :], grad_vlin_r, seq_count),
        ],
        axis=1,
    )
    term_attn_in = outer_rows(normed_b, code_attn_back, seq_count)
    grad_normed_part = (
        matmul_t(grad_qlin_b, full_query)
        + matmul_t(grad_klin_b, full_key)
        + matmul_t(grad_vlin_b, full_value)
        + adapt_in_t(code_attn_back, pick_attn_in, seq_count)
    )
    grad_normed = grad_normed + lax.psum(grad_normed_part.astype(jnp.bfloat16), "tensor").astype(
        jnp.float32
    )
    grad_inputs = grad_inputs + normed_back(grad_normed)[0]

    def to_adapters(term_local):
        return jnp.einsum("sa,s...->a...", onehot, term_local, precision=HIGHEST)

    sum_attn_in = to_adapters(term_attn_in)
    sum_query_out = to_adapters(term_query_out)
    sum_kv_out = to_adapters(term_kv_out)
    sum_out_in = to_adapters(term_out_in)
    sum_out_out = to_adapters(term_out_out)
    sum_ffn_in = to_adapters(term_ffn_in)
    sum_gu_out = to_adapters(term_gu_out)
    sum_down_in = to_adapters(term_down_in)
    sum_down_out = to_adapters(term_down_out)
    grad_sums = lax.psum(
        (
            sum_attn_in,
            place_part(sum_query_out, 2, tensor_slot, tensor_count),
            place_part(sum_kv_out, 3, tensor_slot, tensor_count),
            place_part(sum_out_in, 1, tensor_slot, tensor_count),
            sum_out_out,
            sum_ffn_in,
            place_part(sum_gu_out, 3, tensor_slot, tensor_count),
            place_part(sum_down_in, 1, tensor_slot, tensor_count),
            sum_down_out,
        ),
        ("shard", "context", "tensor"),
    )
    layer_output = output_f.astype(jnp.bfloat16).reshape(tokens.shape)
    input_grad = grad_inputs.astype(jnp.bfloat16).reshape(tokens.shape)
    return (
        layer_output,
        input_grad,
        grad_sums[0],
        grad_sums[1],
        grad_sums[2],
        grad_sums[3],
        grad_sums[4],
        grad_sums[5],
        grad_sums[6],
        grad_sums[7],
        grad_sums[8],
    )


def solution(mesh):
    in_specs = (
        P("shard", "context", None),
        P("shard", "context", None),
        P("shard", None),
        P("shard"),
        P("shard", "context", None),
        P("shard", "tensor"),
        P("shard", "tensor"),
        P("shard", "tensor"),
        P("tensor", "shard"),
        P("shard", "tensor"),
        P("shard", "tensor"),
        P("tensor", "shard"),
        P("shard", None),
        P(None, "shard"),
        P("shard", None),
        P(None, "shard"),
        P(),
        P(),
        P(),
        P(),
        P(),
        P(),
        P(),
        P(),
        P(),
        P(None, None, "tensor"),
        P(None, None, None, "tensor"),
        P(None, "tensor", None),
        P(),
        P(),
        P(None, None, None, "tensor"),
        P(None, "tensor", None),
        P(),
    )
    out_specs = (
        P("shard", "context", None),
        P("shard", "context", None),
        P(),
        P(),
        P(),
        P(),
        P(),
        P(),
        P(),
        P(),
        P(),
    )
    return jax.shard_map(body, mesh=mesh, in_specs=in_specs, out_specs=out_specs, check_vma=False)
```

profile of v0, /device:TPU:0, one launch (start us, length us, event | category | flops | bytes accessed | tf_op | source)
XLA Modules:
  0.0 2002.7 jit_solution(18075510357972300897)
XLA Ops:
  29.1 11.1 all-gather.10.cloned.1.call-done
  45.0 24.3 %all-gather.12.cloned.1.call-done = bf16[2048,256]{1,0:T(8,128)(2,1)} async-done(((bf16[512,256]{1,0:T(8,128)(2,1)}), bf16[2048,256]{1,0:T(8,128)(2,1)}) %all-gather.12.cloned.1.call-update) | async-done | bytes 1048592 | tf_op jit(solution)/shard_map/all_gather | solution.py:182
  83.8 67.4 %all-gather.14.cloned.1.call-done = bf16[2048,1024]{1,0:T(8,128)(2,1)} async-done(((bf16[512,1024]{1,0:T(8,128)(2,1)}), bf16[2048,1024]{1,0:T(8,128)(2,1)}) %all-gather.14.cloned.1.call-update) | async-done | bytes 4194320 | tf_op jit(solution)/shard_map/all_gather | solution.py:180
  151.2 5.2 fusion.259
  156.4 4.0 convolution_add_fusion.3
  176.1 55.8 %all-gather.16.cloned.1.call-done = bf16[1024,2048]{1,0:T(8,128)(2,1)} async-done(((bf16[1024,512]{1,0:T(8,128)(2,1)}), bf16[1024,2048]{1,0:T(8,128)(2,1)}) %all-gather.16.cloned.1.call-update) | async-done | bytes 4194320 | tf_op jit(solution)/shard_map/all_gather | solution.py:183
  231.9 4.6 fusion.260
  236.6 5.0 add_convert_fusion.4
  245.0 11.1 fusion.96
  256.2 13.3 copy.157
  269.5 14.3 all_gather.37
  283.9 13.9 all_gather.38
  297.7 5.2 multiply_reduce_fusion.4
  310.5 5.2 multiply_reduce_fusion.3
  317.8 9.0 fusion.161
  326.8 9.1 fusion.163
  335.8 255.8 %all-gather.18.cloned.1.call-done = bf16[2048,4096]{1,0:T(8,128)(2,1)} async-done(((bf16[512,4096]{1,0:T(8,128)(2,1)}), bf16[2048,4096]{1,0:T(8,128)(2,1)}) %all-gather.18.cloned.1.call-update) | async-done | bytes 16777232 | tf_op jit(solution)/shard_map/all_gather | solution.py:184
  591.6 15.7 convolution_add_fusion.2
  607.3 271.0 %all-gather.20.cloned.1.call-done = bf16[2048,4096]{1,0:T(8,128)(2,1)} async-done(((bf16[512,4096]{1,0:T(8,128)(2,1)}), bf16[2048,4096]{1,0:T(8,128)(2,1)}) %all-gather.20.cloned.1.call-update) | async-done | bytes 16777232 | tf_op jit(solution)/shard_map/all_gather | solution.py:185
  878.3 22.9 %multiply_convert_fusion.1 = (bf16[512,4096]{1,0:T(8,128)(2,1)}, f32[512,4096]{1,0:T(8,128)}) fusion(f32[512,4096]{1,0:T(8,128)} %convolution_add_fusion.2, f32[512,4096]{1,0:T(8,128)} %fusion.163, bf16[512,2048]{1,0:T(8,128)(2,1)S(1)} %multiply_convert_fusion.2, bf16[2048,4096]{1,0:T(8,128)(2,1)} %all-gather.20.cloned.1.call-done), kind=kOutput, calls=%fused_computation.17 | convolution fusion | flops 8613003264 | bytes 48234496 | tf_op jit(solution)/shard_map/dot_general | solution.py:64
  904.5 5.0 fusion.167
  909.5 255.4 %all-gather.22.cloned.1.call-done = bf16[4096,2048]{1,0:T(8,128)(2,1)} async-done(((bf16[4096,512]{1,0:T(8,128)(2,1)}), bf16[4096,2048]{1,0:T(8,128)(2,1)}) %all-gather.22.cloned.1.call-update) | async-done | bytes 16777232 | tf_op jit(solution)/shard_map/all_gather | solution.py:186
  1164.9 15.1 add_convert_fusion.3
  1183.4 58.0 %all-reduce.13.cloned.1.call-done = bf16[512,2048]{1,0:T(8,128)(2,1)} async-done(((bf16[512,2048]{1,0:T(8,128)(2,1)}), bf16[512,2048]{1,0:T(8,128)(2,1)}) %all-reduce.13.cloned.1.call-update) | async-done | bytes 2097168 | tf_op jit(solution)/shard_map/psum | solution.py:308
  1243.4 27.3 %all-gather.24.cloned.1.call-done = bf16[2048,256]{1,0:T(8,128)(2,1)} async-done(((bf16[512,256]{1,0:T(8,128)(2,1)}), bf16[2048,256]{1,0:T(8,128)(2,1)}) %all-gather.24.cloned.1.call-update) | async-done | bytes 1048592 | tf_op jit(solution)/shard_map/all_gather | solution.py:189
  1270.7 4.8 fusion.50
  1275.6 24.2 %all-gather.26.cloned.1.call-done = bf16[256,2048]{1,0:T(8,128)(2,1)} async-done(((bf16[256,512]{1,0:T(8,128)(2,1)}), bf16[256,2048]{1,0:T(8,128)(2,1)}) %all-gather.26.cloned.1.call-update) | async-done | bytes 1048592 | tf_op jit(solution)/shard_map/all_gather | solution.py:190
  1299.8 5.2 fusion.19
  1305.0 8.9 fusion.44
  1318.9 5.7 fusion.178
  1324.6 25.2 %fusion.6 = (bf16[512,4096]{1,0:T(8,128)(2,1)}, bf16[512,4096]{1,0:T(8,128)(2,1)}) fusion(f32[512,4096]{1,0:T(8,128)} %convolution_add_fusion.2, f32[512,4096]{1,0:T(8,128)} %get-tuple-element.61, f32[512,4096]{1,0:T(8,128)} %fusion.178, bf16[512,2048]{1,0:T(8,128)(2,1)S(1)} %fusion.29, bf16[4096,2048]{1,0:T(8,128)(2,1)} %all-gather.22.cloned.1.call-done), kind=kOutput, calls=%fused_computation.8 | convolution fusion | flops 8642363392 | bytes 52428800 | tf_op jit(solution)/shard_map/dot_general | solution.py:68
  1349.8 4.8 convolution_bitcast_fusion.1
  1364.9 3.9 fusion.142
  1370.6 14.2 fusion.261
  1384.8 16.6 add_convert_fusion.1
  1409.7 4.4 broadcast_in_dim.110
  1416.7 47.3 %all-reduce.15.cloned.1.call-done = bf16[512,2048]{1,0:T(8,128)(2,1)} async-done(((bf16[512,2048]{1,0:T(8,128)(2,1)}), bf16[512,2048]{1,0:T(8,128)(2,1)}) %all-reduce.15.cloned.1.call-update) | async-done | bytes 2097168 | tf_op jit(solution)/shard_map/psum | solution.py:365
  1463.9 3.7 multiply_reduce_fusion.1
  1468.7 8.9 multiply_reduce_fusion
  1487.0 5.8 fusion.79
  1492.8 5.3 fusion.7
  1521.8 3.8 add_convert_fusion
  1535.8 57.3 %all-reduce.17.cloned.1.call-done = bf16[512,2048]{1,0:T(8,128)(2,1)} async-done(((bf16[512,2048]{1,0:T(8,128)(2,1)}), bf16[512,2048]{1,0:T(8,128)(2,1)}) %all-reduce.17.cloned.1.call-update) | async-done | bytes 2097168 | tf_op jit(solution)/shard_map/psum | solution.py:441
  1593.1 9.6 fusion.25
  1602.7 5.9 fusion.54
  1608.6 369.8 %all-reduce.19.cloned.1.call-done = (f32[8,2048,48]{1,2,0:T(8,128)}, f32[8,16,2048]{2,1,0:T(8,128)}, f32[8,2,16,512]{3,2,1,0:T(8,128)}, f32[8,2048,16]{1,2,0:T(8...) async-done(((f32[8,2048,48]{1,2,0:T(8,128)}, ...) | async-done | bytes 22544400 | tf_op jit(solution)/shard_map/psum | solution.py:458
  1978.4 4.1 copy.250
  1987.5 4.3 copy.256
  (479 shorter events, 157.5 us)
Async XLA Ops:
  7.2 297.3 %copy-start = (bf16[8,2,16,4096]{3,2,1,0:T(8,128)(2,1)S(1)}, bf16[8,2,16,4096]{3,2,1,0:T(8,128)(2,1)}, u32[]{:S(2)}) copy-start(bf16[8,2,16,4096]{3,2,1,0:T(8,128)(2,1)} %param.63) | copy-start | bytes 6291460
  7.2 33.0 %all-gather.10.cloned.1.call-start = ((), (), s32[]{:S(2)}) async-start(), calls=%async_computation | async-start | bytes 1310720 | tf_op jit(solution)/shard_map/all_gather | solution.py:181
  8.0 61.4 %all-gather.12.cloned.1.call-start = ((), (), s32[]{:S(2)}) async-start(), calls=%async_computation.1 | async-start | bytes 1310720 | tf_op jit(solution)/shard_map/all_gather | solution.py:182
  8.7 142.5 %all-gather.14.cloned.1.call-start = ((), (), s32[]{:S(2)}) async-start(), calls=%async_computation.2 | async-start | bytes 5242880 | tf_op jit(solution)/shard_map/all_gather | solution.py:180
  9.4 222.5 %all-gather.16.cloned.1.call-start = ((), (), s32[]{:S(2)}) async-start(), calls=%async_computation.3 | async-start | bytes 5242880 | tf_op jit(solution)/shard_map/all_gather | solution.py:183
  10.0 297.8 %all-reduce.11.cloned.1.call-start = ((), (), s32[]{:S(2)}) async-start(), calls=%async_computation.4 | async-start | bytes 4194304 | tf_op jit(solution)/shard_map/psum | solution.py:281
  10.1 33.7 %copy-start.143 = (f32[128]{0:T(128)}, f32[128]{0:T(128)S(1)}, u32[]{:S(2)}) copy-start(f32[128]{0:T(128)S(1)} %multiply_exponential_fusion) | copy-start | bytes 1540
  17.4 293.1 %copy-start.102 = (f32[512]{0:T(512)}, f32[512]{0:T(512)S(1)}, u32[]{:S(2)}) copy-start(f32[512]{0:T(512)S(1)} %fusion.214) | copy-start | bytes 6148
  25.3 46.8 %copy-start.100 = (f32[1,512]{1,0:T(1,128)}, f32[1,512]{1,0:T(1,128)S(1)}, u32[]{:S(2)}) copy-start(f32[1,512]{1,0:T(1,128)S(1)} %fusion.204) | copy-start | bytes 6148
  27.2 140.8 %copy-start.38 = (f32[512,128]{1,0:T(8,128)}, f32[512,128]{1,0:T(8,128)S(1)}, u32[]{:S(2)}) copy-start(f32[512,128]{1,0:T(8,128)S(1)} %get-tuple-element.44) | copy-start | bytes 786436
  27.2 140.8 %copy-start.40 = (f32[512,128]{1,0:T(8,128)}, f32[512,128]{1,0:T(8,128)S(1)}, u32[]{:S(2)}) copy-start(f32[512,128]{1,0:T(8,128)S(1)} %get-tuple-element.45) | copy-start | bytes 786436
  42.9 30.9 %copy-start.124 = (f32[512]{0:T(512)}, f32[512]{0:T(512)S(1)}, u32[]{:S(2)}) copy-start(f32[512]{0:T(512)S(1)} %get-tuple-element.54) | copy-start | bytes 6148
  42.9 30.9 %copy-start.112 = (f32[512]{0:T(512)}, f32[512]{0:T(512)S(1)}, u32[]{:S(2)}) copy-start(f32[512]{0:T(512)S(1)} %fusion.215) | copy-start | bytes 6148
  73.8 7.8 collective-permute-start
  77.0 98.2 %copy-start.45 = (bf16[1,1024,16]{2,1,0:T(8,128)(2,1)}, bf16[1,1024,16]{2,1,0:T(8,128)(2,1)S(1)}, u32[]{:S(2)}) copy-start(bf16[1,1024,16]{2,1,0:T(8,128)(2,1)S(1)} %copy.148) | copy-start | bytes 98308
  78.6 158.0 %copy-start.51 = (f32[1,16,2048]{2,0,1:T(1,128)}, f32[1,16,2048]{2,0,1:T(1,128)S(1)}, u32[]{:S(2)}) copy-start(f32[1,16,2048]{2,0,1:T(1,128)S(1)} %fusion.113) | copy-start | bytes 393220
  83.8 72.6 %copy-start.66 = (f32[1,16,1024]{2,0,1:T(1,128)S(1)}, f32[1,16,1024]{2,0,1:T(1,128)}, u32[]{:S(2)}) copy-start(f32[1,16,1024]{2,0,1:T(1,128)} %fusion.148) | copy-start | bytes 196612
  175.2 61.4 %copy-start.18 = (bf16[256,4,512]{2,0,1:T(8,128)(2,1)}, bf16[256,4,512]{2,0,1:T(8,128)(2,1)S(1)}, u32[]{:S(2)}) copy-start(bf16[256,4,512]{2,0,1:T(8,128)(2,1)S(1)} %fusion.76) | copy-start | bytes 3145732
  176.1 60.5 %copy-start.79 = (f32[512,16]{0,1:T(8,128)S(1)}, f32[512,16]{0,1:T(8,128)}, u32[]{:S(2)}) copy-start(f32[512,16]{0,1:T(8,128)} %fusion.164) | copy-start | bytes 98308
  241.7 349.9 %all-gather.18.cloned.1.call-start = ((), (), s32[]{:S(2)}) async-start(), calls=%async_computation.5 | async-start | bytes 20971520 | tf_op jit(solution)/shard_map/all_gather | solution.py:184
  242.3 636.0 %all-gather.20.cloned.1.call-start = ((), (), s32[]{:S(2)}) async-start(), calls=%async_computation.6 | async-start | bytes 20971520 | tf_op jit(solution)/shard_map/all_gather | solution.py:185
  243.0 921.9 %all-gather.22.cloned.1.call-start = ((), (), s32[]{:S(2)}) async-start(), calls=%async_computation.7 | async-start | bytes 20971520 | tf_op jit(solution)/shard_map/all_gather | solution.py:186
  243.8 997.6 %all-reduce.13.cloned.1.call-start = ((), (), s32[]{:S(2)}) async-start(), calls=%async_computation.8 | async-start | bytes 4194304 | tf_op jit(solution)/shard_map/psum | solution.py:308
  304.5 600.0 %copy-start.53 = (f32[1,16,2048]{2,0,1:T(1,128)}, f32[1,16,2048]{2,0,1:T(1,128)S(1)}, u32[]{:S(2)}) copy-start(f32[1,16,2048]{2,0,1:T(1,128)S(1)} %fusion.111) | copy-start | bytes 393220
  316.8 561.5 %copy-start.12 = (bf16[512,2048]{1,0:T(8,128)(2,1)}, bf16[512,2048]{1,0:T(8,128)(2,1)S(1)}, u32[]{:S(2)}) copy-start(bf16[512,2048]{1,0:T(8,128)(2,1)S(1)} %multiply_convert_fusion.2) | copy-start | bytes 6291460
  904.5 275.5 %copy-start.77 = (f32[512,16]{0,1:T(8,128)}, f32[512,16]{0,1:T(8,128)S(1)}, u32[]{:S(2)}) copy-start(f32[512,16]{0,1:T(8,128)S(1)} %fusion.179) | copy-start | bytes 98308
  909.5 273.8 %copy-start.107 = (f32[4,512]{1,0:T(4,128)S(1)}, f32[4,512]{1,0:T(4,128)}, u32[]{:S(2)}) copy-start(f32[4,512]{1,0:T(4,128)} %copy-done.106) | copy-start | bytes 24580
  909.5 273.8 %copy-start.109 = (f32[4,512]{1,0:T(4,128)S(1)}, f32[4,512]{1,0:T(4,128)}, u32[]{:S(2)}) copy-start(f32[4,512]{1,0:T(4,128)} %copy-done.108) | copy-start | bytes 24580
  1180.0 90.7 %copy-start.95 = (f32[2048]{0:T(1024)S(1)}, f32[2048]{0:T(1024)}, u32[]{:S(2)}) copy-start(f32[2048]{0:T(1024)} %param.53) | copy-start | bytes 24580
  1180.1 90.6 %all-gather.24.cloned.1.call-start = ((), (), s32[]{:S(2)}) async-start(), calls=%async_computation.9 | async-start | bytes 1310720 | tf_op jit(solution)/shard_map/all_gather | solution.py:189
  1180.7 119.1 %all-gather.26.cloned.1.call-start = ((), (), s32[]{:S(2)}) async-start(), calls=%async_computation.10 | async-start | bytes 1310720 | tf_op jit(solution)/shard_map/all_gather | solution.py:190
  1181.4 282.5 %all-reduce.15.cloned.1.call-start = ((), (), s32[]{:S(2)}) async-start(), calls=%async_computation.11 | async-start | bytes 4194304 | tf_op jit(solution)/shard_map/psum | solution.py:365
  1243.4 56.4 %copy-start.141 = (f32[2048]{0:T(1024)S(1)}, f32[2048]{0:T(1024)}, u32[]{:S(2)}) copy-start(f32[2048]{0:T(1024)} %param.54) | copy-start | bytes 24580
  1243.4 56.3 %copy-start.147 = (bf16[1,512,256]{2,1,0:T(8,128)(2,1)S(1)}, bf16[1,512,256]{2,1,0:T(8,128)(2,1)}, u32[]{:S(2)}) copy-start(bf16[1,512,256]{2,1,0:T(8,128)(2,1)} %param.34) | copy-start | bytes 786436
  1401.4 191.7 %all-reduce.17.cloned.1.call-start = ((), (), s32[]{:S(2)}) async-start(), calls=%async_computation.12 | async-start | bytes 4194304 | tf_op jit(solution)/shard_map/psum | solution.py:441
  1414.1 49.8 %copy-start.94 = (f32[2048]{0:T(1024)S(1)}, f32[2048]{0:T(1024)}, u32[]{:S(2)}) copy-start(f32[2048]{0:T(1024)} %param.52) | copy-start | bytes 24580
  1414.1 53.6 %copy-start.142 = (f32[2048]{0:T(1024)S(1)}, f32[2048]{0:T(1024)}, u32[]{:S(2)}) copy-start(f32[2048]{0:T(1024)} %param.54) | copy-start | bytes 24580
  1416.6 51.0 %copy-start.121 = (f32[512]{0:T(512)S(1)}, f32[512]{0:T(512)}, u32[]{:S(2)}) copy-start(f32[512]{0:T(512)} %copy-done.120) | copy-start | bytes 6148
  1416.6 51.1 %copy-start.96 = (f32[2048]{0:T(1024)S(1)}, f32[2048]{0:T(1024)}, u32[]{:S(2)}) copy-start(f32[2048]{0:T(1024)} %broadcast_multiply_fusion.4) | copy-start | bytes 24580
  1416.6 51.1 %copy-start.137 = (f32[512]{0:T(512)S(1)}, f32[512]{0:T(512)}, u32[]{:S(2)}) copy-start(f32[512]{0:T(512)} %get-tuple-element.46) | copy-start | bytes 6148
  1416.6 51.1 %copy-start.140 = (f32[512]{0:T(512)S(1)}, f32[512]{0:T(512)}, u32[]{:S(2)}) copy-start(f32[512]{0:T(512)} %copy-done.139) | copy-start | bytes 6148
  1512.4 4.1 collective-permute-start.1
  1525.7 452.7 %all-reduce.19.cloned.1.call-start = ((), (), s32[]{:S(2)}) async-start(), calls=%async_computation.13 | async-start | bytes 45088768 | tf_op jit(solution)/shard_map/psum | solution.py:458
  1535.1 58.0 %copy-start.35 = (bf16[2048,64]{0,1:T(8,128)(2,1)S(1)}, bf16[2048,64]{0,1:T(8,128)(2,1)}, u32[]{:S(2)}) copy-start(bf16[2048,64]{0,1:T(8,128)(2,1)} %copy-done.34) | copy-start | bytes 786436
  1535.1 58.0 %copy-start.37 = (bf16[64,2048]{1,0:T(8,128)(2,1)S(1)}, bf16[64,2048]{1,0:T(8,128)(2,1)}, u32[]{:S(2)}) copy-start(bf16[64,2048]{1,0:T(8,128)(2,1)} %copy-done.36) | copy-start | bytes 786436
  1535.1 58.0 %copy-start.117 = (f32[512]{0:T(512)S(1)}, f32[512]{0:T(512)}, u32[]{:S(2)}) copy-start(f32[512]{0:T(512)} %copy-done.116) | copy-start | bytes 6148
  1535.8 66.9 %copy-start.123 = (f32[512]{0:T(512)S(1)}, f32[512]{0:T(512)}, u32[]{:S(2)}) copy-start(f32[512]{0:T(512)} %copy-done.122) | copy-start | bytes 6148
  1535.8 66.9 %copy-start.103 = (f32[512]{0:T(512)S(1)}, f32[512]{0:T(512)}, u32[]{:S(2)}) copy-start(f32[512]{0:T(512)} %copy-done.102) | copy-start | bytes 6148
  (120 other events, 668.5 us)
Sparse Core Ops, SparseCore 0:
  9.6 30.5 all-gather.9
  41.8 27.4 all-gather.11
  70.9 80.2 all-gather.13
  152.6 79.2 all-gather.15
  241.8 61.4 all-reduce.10
  304.8 286.7 all-gather.17
  593.2 284.9 all-gather.19
  879.9 284.9 all-gather.21
  1180.2 61.0 all-reduce.12
  1242.8 27.9 all-gather.23
  1272.3 27.4 all-gather.25
  1401.5 62.3 all-reduce.14
  1525.8 67.2 all-reduce.16
  1600.6 377.7 all-reduce.18
where the time goes:
time: 2010 us; the launch traced here: 2000 us
  waiting for transfers between devices  1530 us (76%)
  matrix products  290 us (14%)
  other arithmetic  76 us (4%)
  local copies, waits for them, and re-layouts  56.7 us (3%)
  blocking collectives  28.2 us (1%)
    psum x1, waiting for transfers between devices, body(): lax.psum((sum_attn_in, place_part(sum_query_out, 2, tensor_slot, tensor_c...  370 us
    all_gather x1, waiting for transfers between devices, body(): lax.all_gather(w_up, 'shard', axis=0, tiled=True)  271 us
    all_gather x1, waiting for transfers between devices, body(): lax.all_gather(w_gate, 'shard', axis=0, tiled=True)  256 us
    all_gather x1, waiting for transfers between devices, body(): lax.all_gather(w_down, 'shard', axis=1, tiled=True)  255 us
    dot_general x10, matrix products, matmul(): return jnp.dot(left_op, right_op, preferred_element_type=jnp.float32)  84.1 us
    dot_general x9, matrix products, matmul_t(): lax.dot_general(left_op, right_op, (((1,), (1,)), ((), ())), preferred_el...  80.7 us
    all_gather x1, waiting for transfers between devices, body(): lax.all_gather(w_query, 'shard', axis=0, tiled=True)  67.4 us
    psum x1, waiting for transfers between devices, body(): lax.psum(down_part.astype(jnp.bfloat16), 'tensor').astype(jnp.float32)  58 us
  transfers between devices with their start and end apart: 16, of which 13 were waited for; matrix products, arithmetic and copies ran while one was open for 11% of the time, Pallas kernels for 0%

commit v1 on v0

v1 whole, which is shorter than its diff:
```python
import functools
import math

import jax
import jax.numpy as jnp
from jax import lax
from jax.experimental import pallas as pl
from jax.experimental.pallas import tpu as pltpu
from jax.sharding import PartitionSpec as P

WINDOW = 512
EPSILON = 1e-06
ROOT_HALF = 0.7071067811865476

MESH = pl.DeviceIdType.MESH


def gather_kernel(plan, count, shards, depth, *refs):
    sources, fulls, held = refs[:count], refs[count : 2 * count], refs[2 * count : 3 * count]
    load_sem, local_sem, z_recv, y_recv, near_recv, far_recv, z_send, y_send, near_send, far_send = refs[3 * count :]
    z, c = lax.axis_index("shard"), lax.axis_index("context")
    across = lax.rem(c + 2, 4)
    beside = c + 1 - 2 * lax.rem(c, 2)

    barrier = pltpu.get_barrier_semaphore()

    def greet(place):
        pl.semaphore_signal(barrier, inc=1, device_id=place, device_id_type=MESH)

    greet({"context": across})
    greet({"context": beside})

    @pl.when(z > 0)
    def _():
        greet({"shard": z - 1})

    @pl.when(z < shards - 1)
    def _():
        greet({"shard": z + 1})

    pl.semaphore_wait(barrier, 2 + lax.div(z + shards - 1, shards) + lax.div(2 * shards - 2 - z, shards))

    def region(piece, s, q):
        item, axis, row, rows, col, cols = plan[piece]
        rows_here, cols_here = sources[item].shape
        part = rows // 4
        if axis == 0:
            first = s * rows_here + row + q * part
            return fulls[item].at[pl.ds(pl.multiple_of(first, 16), part), pl.ds(col, cols)]
        return fulls[item].at[
            pl.ds(pl.multiple_of(row + q * part, 16), part),
            pl.ds(pl.multiple_of(s * cols_here + col, 128), cols),
        ]

    def own(piece, q):
        item, axis, row, rows, col, cols = plan[piece]
        part = rows // 4
        return sources[item].at[pl.ds(pl.multiple_of(row + q * part, 16), part), pl.ds(col, cols)]

    def copy(source, target, send, recv, place):
        return pltpu.make_async_remote_copy(
            src_ref=source, dst_ref=target, send_sem=send, recv_sem=recv, device_id=place, device_id_type=MESH
        )

    def up(piece, s, source, slot):
        return copy(source, region(piece, s, c), z_send.at[piece, slot], z_recv.at[piece, s], {"shard": z + 1})

    def down(piece, s, source, slot):
        return copy(source, region(piece, s, c), z_send.at[piece, slot], z_recv.at[piece, s], {"shard": z - 1})

    def y_copy(piece, s, q):
        return copy(region(piece, s, q), region(piece, s, q), y_send.at[piece, s], y_recv.at[piece, s], {"context": across})

    def near_copy(piece, s, q):
        return copy(region(piece, s, q), region(piece, s, q), near_send.at[piece, s], near_recv.at[piece, s], {"context": beside})

    def far_copy(piece, s, q):
        return copy(region(piece, s, q), region(piece, s, q), far_send.at[piece, s], far_recv.at[piece, s], {"context": beside})

    loads, stores = [], []
    for item in range(count):
        rows_here, cols_here = sources[item].shape
        axis = next(p[1] for p in plan if p[0] == item)
        if axis == 0:
            target = fulls[item].at[pl.ds(pl.multiple_of(z * rows_here, 16), rows_here), :]
        else:
            target = fulls[item].at[:, pl.ds(pl.multiple_of(z * cols_here, 128), cols_here)]
        loads.append(pltpu.make_async_copy(sources[item], held[item], load_sem.at[item]))
        stores.append(pltpu.make_async_copy(held[item], target, local_sem.at[item]))

    def begin(piece):
        @pl.when(z < shards - 1)
        def _():
            up(piece, z, own(piece, c), z).start()

        @pl.when(z > 0)
        def _():
            down(piece, z, own(piece, c), shards).start()

    def relay(piece):
        def hop(d, carry):
            @pl.when(z >= d)
            def _():
                s = z - d
                up(piece, s, region(piece, s, c), s).wait_recv()

                @pl.when(z < shards - 1)
                def _():
                    up(piece, s, region(piece, s, c), s).start()

                y_copy(piece, s, c).start()
                near_copy(piece, s, c).start()

            @pl.when(z + d <= shards - 1)
            def _():
                s = z + d
                down(piece, s, region(piece, s, c), s).wait_recv()

                @pl.when(z > 0)
                def _():
                    down(piece, s, region(piece, s, c), s).start()

                y_copy(piece, s, c).start()
                near_copy(piece, s, c).start()

            return carry

        lax.fori_loop(1, shards, hop, 0)

    def others(act):
        def one(d, carry):
            act(lax.rem(z + d, shards))
            return carry

        lax.fori_loop(1, shards, one, 0)

    def spread(piece):
        def act(s):
            y_copy(piece, s, across).wait_recv()
            far_copy(piece, s, across).start()

        others(act)

    pieces = len(plan)
    for piece in range(min(depth, pieces)):
        begin(piece)
    for item in range(count):
        loads[item].start()
    for item in range(count):
        loads[item].wait()
        stores[item].start()
    for piece in range(pieces):
        relay(piece)
        if piece + depth < pieces:
            begin(piece + depth)
        if piece >= 1:
            spread(piece - 1)
    spread(pieces - 1)
    for piece in range(pieces):

        @pl.when(z < shards - 1)
        def _():
            up(piece, z, own(piece, c), z).wait_send()

        @pl.when(z > 0)
        def _():
            down(piece, z, own(piece, c), shards).wait_send()

        def act(s, piece=piece):
            near_copy(piece, s, beside).wait_recv()
            far_copy(piece, s, lax.rem(beside + 2, 4)).wait_recv()
            y_copy(piece, s, c).wait_send()
            near_copy(piece, s, c).wait_send()
            far_copy(piece, s, across).wait_send()

            @pl.when((s < z) & (z < shards - 1))
            def _():
                up(piece, s, region(piece, s, c), s).wait_send()

            @pl.when((s > z) & (z > 0))
            def _():
                down(piece, s, region(piece, s, c), s).wait_send()

        others(act)
    for item in range(count):
        stores[item].wait()


def gather(weights, axes, plan, shards, depth, collective_id):
    count = len(weights)
    shapes = []
    for w, axis in zip(weights, axes):
        shape = list(w.shape)
        shape[axis] *= shards
        shapes.append(jax.ShapeDtypeStruct(tuple(shape), w.dtype))
    pieces = len(plan)
    table = pltpu.SemaphoreType.DMA((pieces, shards))
    return pl.pallas_call(
        functools.partial(gather_kernel, plan, count, shards, depth),
        out_shape=shapes,
        in_specs=[pl.BlockSpec(memory_space=pl.ANY)] * count,
        out_specs=[pl.BlockSpec(memory_space=pl.ANY)] * count,
        scratch_shapes=[
            *[pltpu.VMEM(w.shape, w.dtype) for w in weights],
            pltpu.SemaphoreType.DMA((count,)),
            pltpu.SemaphoreType.DMA((count,)),
            table, table, table, table,
            pltpu.SemaphoreType.DMA((pieces, shards + 1)),
            table, table, table,
        ],
        compiler_params=pltpu.CompilerParams(collective_id=collective_id, has_side_effects=True, vmem_limit_bytes=40 * 2**20),
    )(*weights)


def shifted(array, axis, by):
    count = lax.axis_size(axis)
    pairs = [(i, i + by) for i in range(count) if 0 <= i + by < count]
    return lax.ppermute(array, axis, pairs)


def swap(array):
    return lax.ppermute(array, "tensor", [(0, 1), (1, 0)])


def rms_norm(values, scaling):
    return values * lax.rsqrt(jnp.mean(values * values, axis=-1, keepdims=True) + EPSILON) * scaling


def gelu_tanh(values):
    return jax.nn.gelu(values, approximate=True)


def rotate_half(values, cosine, sine_table):
    middle = values.shape[-1] // 2
    former = values[..., :middle]
    latter = values[..., middle:]
    return jnp.concatenate(
        [former * cosine - latter * sine_table, latter * cosine + former * sine_table], axis=-1
    )


def rope_tables(positions, head_size):
    frequency = jnp.exp(
        jnp.arange(head_size // 2, dtype=jnp.float32) * (-2.0 * math.log(10000.0) / head_size)
    )
    angles = positions.astype(jnp.float32)[..., None] * frequency
    return (jnp.cos(angles), jnp.sin(angles))


def low(values):
    return values.astype(jnp.bfloat16)


def wide(values):
    return values.astype(jnp.float32)


def matmul(left_op, right_op):
    return jnp.dot(low(left_op), low(right_op), preferred_element_type=jnp.float32)


def matmul_t(left_op, right_op):
    return lax.dot_general(
        low(left_op), low(right_op), (((1,), (1,)), ((), ())), preferred_element_type=jnp.float32
    )


def outer(left_op, right_op):
    return lax.dot_general(
        low(left_op), low(right_op), (((0,), (0,)), ((), ())), preferred_element_type=jnp.float32
    )


def share(packed):
    part = lax.psum_scatter(packed, "context", scatter_dimension=1, tiled=True)
    whole = lax.all_gather(low(part), ("shard", "context", "tensor"), axis=0, tiled=False)
    shards, contexts, tensors = (lax.axis_size(a) for a in ("shard", "context", "tensor"))
    whole = whole.reshape(shards, contexts, tensors, packed.shape[0], part.shape[1])
    return whole.transpose(2, 0, 3, 1, 4).reshape(tensors, shards, packed.shape[0], packed.shape[1])


def body(
    tokens,
    layer_input,
    segments,
    adapter_ids,
    cotangent,
    w_query,
    w_key,
    w_value,
    w_output,
    w_gate,
    w_up,
    w_down,
    laurel_left,
    laurel_right,
    input_gate,
    input_proj,
    gain_in,
    gain_attn,
    gain_laurel,
    gain_pre,
    gain_post,
    gain_layer,
    gain_query,
    gain_key,
    adapt_attn_in,
    adapt_query_out,
    adapt_kv_out,
    adapt_out_in,
    adapt_out_out,
    adapt_ffn_in,
    adapt_gu_out,
    adapt_down_in,
    adapt_down_out,
):
    seq_count, count, width = tokens.shape
    assert seq_count == 1 and lax.axis_size("tensor") == 2 and lax.axis_size("context") == 4
    half = count // 2
    head_size = gain_query.shape[0]
    rank = adapt_query_out.shape[1]
    heads = adapt_query_out.shape[2] // head_size
    kv_heads = adapt_kv_out.shape[3] // head_size
    group = heads // kv_heads
    side = lax.axis_index("tensor")
    place = lax.axis_index("context")
    shards = lax.axis_size("shard")

    weights = (
        w_query, w_key, w_value, laurel_left, w_output, laurel_right,
        w_gate, w_up, input_gate, input_proj, w_down,
    )
    axes = (0, 0, 0, 0, 1, 1, 0, 0, 0, 1, 1)
    plan = [(i, axes[i], 0, weights[i].shape[0], 0, weights[i].shape[1]) for i in range(6)]
    steps = 4
    hidden_here = w_gate.shape[1]
    cut = hidden_here // steps
    for j in range(steps):
        plan += [(i, 0, 0, weights[i].shape[0], j * cut, cut) for i in (6, 7)]
        if j == steps - 1:
            plan += [(i, axes[i], 0, weights[i].shape[0], 0, weights[i].shape[1]) for i in (8, 9)]
        plan.append((10, 1, j * cut, cut, 0, weights[10].shape[1]))
    (
        full_query, full_key, full_value, full_left, full_output, full_right,
        full_gate, full_up, full_layer_gate, full_layer_proj, full_down,
    ) = gather(weights, axes, tuple(plan), shards, 2, 0)

    chosen = adapter_ids[0]

    def pick(table):
        return lax.dynamic_index_in_dim(table, chosen, 0, keepdims=False)

    pick_attn_in, pick_query_out, pick_kv_out = pick(adapt_attn_in), pick(adapt_query_out), pick(adapt_kv_out)
    pick_out_in, pick_out_out, pick_ffn_in = pick(adapt_out_in), pick(adapt_out_out), pick(adapt_ffn_in)
    pick_gu_out, pick_down_in, pick_down_out = pick(adapt_gu_out), pick(adapt_down_in), pick(adapt_down_out)

    def own_half(array):
        return lax.dynamic_slice_in_dim(array, side * half, half, 0)

    def other_half(array):
        return lax.dynamic_slice_in_dim(array, (1 - side) * half, half, 0)

    def in_order(own, other):
        return jnp.where(
            side == 0, jnp.concatenate([own, other], axis=0), jnp.concatenate([other, own], axis=0)
        )

    start_pos = place * count
    seg_all = segments[0]
    seg_query = lax.dynamic_slice_in_dim(seg_all, start_pos, count, 0)
    before = jnp.sum((seg_all[None, :] < seg_query[:, None]).astype(jnp.int32), axis=1)
    own_pos = start_pos + jnp.arange(count, dtype=jnp.int32) - before
    cosine, sine_table = rope_tables(own_pos, head_size)
    cosine = cosine[:, None, :]
    sine_table = sine_table[:, None, :]
    tokens_f = wide(tokens[0])
    normed_b = low(rms_norm(tokens_f, gain_in))
    tokens_h = wide(own_half(tokens[0]))
    normed_h, normed_back = jax.vjp(lambda v: rms_norm(v, gain_in), tokens_h)
    code_attn = matmul(normed_b, pick_attn_in)
    query_lin = matmul(normed_b, full_query) + matmul(code_attn[:, :rank], pick_query_out)
    key_lin = matmul(normed_b, full_key) + matmul(code_attn[:, rank : 2 * rank], pick_kv_out[0])
    value_lin = matmul(normed_b, full_value) + matmul(code_attn[:, 2 * rank :], pick_kv_out[1])

    def prepare(query_in, key_in, value_in):
        query_rot = rotate_half(
            rms_norm(query_in.reshape(count, heads, head_size), gain_query), cosine, sine_table
        )
        key_rot = rotate_half(
            rms_norm(key_in.reshape(count, kv_heads, head_size), gain_key), cosine, sine_table
        )
        value_nrm = rms_norm(value_in.reshape(count, kv_heads, head_size), 1.0)
        return (query_rot, key_rot, value_nrm)

    (query_rot, key_rot, value_nrm), prepare_back = jax.vjp(prepare, query_lin, key_lin, value_lin)
    query_b = low(query_rot).reshape(count, kv_heads, group, head_size)
    kv_own = low(jnp.stack([key_rot, value_nrm]))
    kv_prior = shifted(kv_own, "context", 1)
    kv_all = jnp.concatenate([kv_prior, kv_own], axis=1)
    query_pos = start_pos + jnp.arange(count, dtype=jnp.int32)
    key_pos = start_pos - count + jnp.arange(2 * count, dtype=jnp.int32)
    seg_prior = lax.dynamic_slice_in_dim(seg_all, jnp.maximum(start_pos - count, 0), count, 0)
    seg_keys = jnp.concatenate([seg_prior, seg_query], axis=0)
    distance = query_pos[:, None] - key_pos[None, :]
    window_ok = (distance >= 0) & (distance < WINDOW) & (key_pos >= 0)[None, :]
    allowed = (seg_query[:, None] == seg_keys[None, :]) & window_ok
    allowed = allowed[None, None]
    score_scale = 1.0 / math.sqrt(head_size)

    def masked_scores():
        raw_scores = (
            jnp.einsum("lkgd,mkd->kglm", query_b, kv_all[0], preferred_element_type=jnp.float32)
            * score_scale
        )
        return jnp.where(allowed, raw_scores, -1e30)

    scores = masked_scores()
    row_max = jnp.max(scores, axis=-1, keepdims=True)
    exponent = jnp.exp(scores - row_max)
    row_total = jnp.sum(exponent, axis=-1, keepdims=True)
    log_total = row_max + jnp.log(row_total)
    attn_probs = low(exponent / row_total)
    attended = jnp.einsum("kglm,mkd->lkgd", attn_probs, kv_all[1], preferred_element_type=jnp.float32)
    attended_b = low(attended.reshape(count, heads * head_size))
    code_out = matmul(attended_b, pick_out_in)
    attn_part = low(matmul(attended_b, full_output) + matmul(code_out, pick_out_out))
    attn_proj = wide(own_half(attn_part)) + wide(swap(other_half(attn_part)))
    laurel_mid = low(matmul(normed_h, full_left))
    laurel_end = matmul(laurel_mid, full_right)

    def combine(inputs_in, normed_in, attn_in, laurel_in):
        return (
            inputs_in + rms_norm(attn_in, gain_attn) + normed_in + rms_norm(laurel_in, gain_laurel)
        ) * ROOT_HALF

    combined, combine_back = jax.vjp(combine, tokens_h, normed_h, attn_proj, laurel_end)
    ffn_input, pre_ffn_back = jax.vjp(lambda v: rms_norm(v, gain_pre), combined)
    ffn_own = low(ffn_input)
    ffn_b = jnp.concatenate([ffn_own, swap(ffn_own)], axis=0)
    code_ffn = matmul(ffn_b, pick_ffn_in)
    gate_lin = matmul(ffn_b, full_gate) + matmul(code_ffn[:, :rank], pick_gu_out[0])
    up_lin = matmul(ffn_b, full_up) + matmul(code_ffn[:, rank:], pick_gu_out[1])

    def activate(gate_in, up_in):
        return gelu_tanh(gate_in) * up_in

    hidden_act, activate_back = jax.vjp(activate, gate_lin, up_lin)
    hidden_b = low(hidden_act)
    code_down = matmul(hidden_b, pick_down_in)
    down_part = low(matmul(hidden_b, full_down) + matmul(code_down, pick_down_out))
    down_proj = wide(down_part[:half]) + wide(swap(down_part[half:]))

    def after_step(combined_in, down_in):
        return combined_in + rms_norm(down_in, gain_post)

    after_ffn, after_back = jax.vjp(after_step, combined, down_proj)
    layer_gate = matmul(after_ffn, full_layer_gate)
    per_layer = wide(own_half(layer_input[0]))

    def mix_layer(gate_in):
        return gelu_tanh(gate_in) * per_layer

    layer_mix, mix_back = jax.vjp(mix_layer, layer_gate)
    layer_proj = matmul(layer_mix, full_layer_proj)

    def finish(after_in, proj_in):
        return after_in + rms_norm(proj_in, gain_layer)

    output_h, finish_back = jax.vjp(finish, after_ffn, layer_proj)
    output_own = low(output_h)
    layer_output = in_order(output_own, swap(output_own))
    grad_after, grad_lproj = finish_back(wide(own_half(cotangent[0])))
    (grad_lgate,) = mix_back(matmul_t(grad_lproj, full_layer_proj))
    grad_after = grad_after + matmul_t(grad_lgate, full_layer_gate)
    grad_comb, grad_down = after_back(grad_after)
    grad_down_own = low(grad_down)
    grad_down_b = jnp.concatenate([grad_down_own, swap(grad_down_own)], axis=0)
    code_down_back = matmul_t(grad_down_b, pick_down_out)
    term_down_out = outer(code_down, grad_down_b)
    term_down_in = outer(code_down_back, hidden_b)
    grad_hidden = matmul_t(grad_down_b, full_down) + matmul_t(code_down_back, pick_down_in)
    grad_gate, grad_up = activate_back(grad_hidden)
    grad_gate_b = low(grad_gate)
    grad_up_b = low(grad_up)
    code_ffn_back = jnp.concatenate(
        [matmul_t(grad_gate_b, pick_gu_out[0]), matmul_t(grad_up_b, pick_gu_out[1])], axis=1
    )
    term_gate_out = outer(code_ffn[:, :rank], grad_gate_b)
    term_up_out = outer(code_ffn[:, rank:], grad_up_b)
    term_ffn_in = outer(code_ffn_back, ffn_b)
    mark = jnp.where(
        (lax.broadcasted_iota(jnp.int32, (rank, 512), 1) == chosen) & (place == 0), 1.0, 0.0
    )
    early = share(
        jnp.concatenate(
            [term_gate_out, term_up_out, term_down_in, term_ffn_in[:rank], term_ffn_in[rank:], term_down_out, mark],
            axis=1,
        )
    )
    grad_ffn_part = low(
        matmul_t(grad_gate_b, full_gate)
        + matmul_t(grad_up_b, full_up)
        + matmul_t(code_ffn_back, pick_ffn_in)
    )
    grad_ffn_input = wide(grad_ffn_part[:half]) + wide(swap(grad_ffn_part[half:]))
    grad_comb = grad_comb + pre_ffn_back(grad_ffn_input)[0]
    grad_inputs, grad_normed, grad_attn, grad_laurel = combine_back(grad_comb)
    grad_laurel_mid = low(matmul_t(grad_laurel, full_right))
    grad_normed = grad_normed + matmul_t(grad_laurel_mid, full_left)
    grad_attn_own = low(grad_attn)
    grad_attn_b = in_order(grad_attn_own, swap(grad_attn_own))
    code_out_back = matmul_t(grad_attn_b, pick_out_out)
    term_out_out = outer(code_out, grad_attn_b)
    term_out_in = outer(code_out_back, attended_b)
    grad_attended = low(matmul_t(grad_attn_b, full_output) + matmul_t(code_out_back, pick_out_in))
    grad_heads = grad_attended.reshape(count, kv_heads, group, head_size)
    recomputed = jnp.exp(masked_scores() - log_total)
    grad_probs = jnp.einsum("lkgd,mkd->kglm", grad_heads, kv_all[1], preferred_element_type=jnp.float32)
    grad_scores = low(
        recomputed * (grad_probs - jnp.sum(recomputed * grad_probs, axis=-1, keepdims=True))
    )
    grad_query = (
        jnp.einsum("kglm,mkd->lkgd", grad_scores, kv_all[0], preferred_element_type=jnp.float32)
        * score_scale
    )
    grad_keys = (
        jnp.einsum("kglm,lkgd->mkd", grad_scores, query_b, preferred_element_type=jnp.float32)
        * score_scale
    )
    grad_values = jnp.einsum(
        "kglm,lkgd->mkd", low(recomputed), grad_heads, preferred_element_type=jnp.float32
    )
    grad_kv = jnp.stack([grad_keys, grad_values])
    grad_kv_later = wide(shifted(low(grad_kv[:, :count]), "context", -1))
    grad_kv_own = grad_kv[:, count:] + grad_kv_later
    grad_qlin, grad_klin, grad_vlin = prepare_back(
        (grad_query.reshape(count, heads, head_size), grad_kv_own[0], grad_kv_own[1])
    )
    grad_qlin_b = low(grad_qlin)
    grad_klin_b = low(grad_klin)
    grad_vlin_b = low(grad_vlin)
    code_attn_back = jnp.concatenate(
        [
            matmul_t(grad_qlin_b, pick_query_out),
            matmul_t(grad_klin_b, pick_kv_out[0]),
            matmul_t(grad_vlin_b, pick_kv_out[1]),
        ],
        axis=1,
    )
    term_query_out = outer(code_attn[:, :rank], grad_qlin_b)
    term_key_out = outer(code_attn[:, rank : 2 * rank], grad_klin_b)
    term_value_out = outer(code_attn[:, 2 * rank :], grad_vlin_b)
    term_attn_in = outer(code_attn_back, normed_b)
    late = share(
        jnp.concatenate(
            [
                term_out_in, term_out_out, term_query_out, term_key_out, term_value_out,
                term_attn_in[:rank], term_attn_in[rank : 2 * rank], term_attn_in[2 * rank :],
            ],
            axis=1,
        )
    )
    grad_normed_part = low(
        matmul_t(grad_qlin_b, full_query)
        + matmul_t(grad_klin_b, full_key)
        + matmul_t(grad_vlin_b, full_value)
        + matmul_t(code_attn_back, pick_attn_in)
    )
    grad_normed = grad_normed + wide(own_half(grad_normed_part)) + wide(swap(other_half(grad_normed_part)))
    grad_own = low(grad_inputs + normed_back(grad_normed)[0])
    input_grad = in_order(grad_own, swap(grad_own))

    at = 0

    def take(packed, columns):
        nonlocal at
        at += columns
        return wide(packed[..., at - columns : at])

    def joined(packed, columns):
        both = take(packed, columns)
        return jnp.concatenate([both[0], both[1]], axis=-1)

    def added(packed, columns):
        both = take(packed, columns)
        return both[0] + both[1]

    gate_out, up_out, down_in = (joined(early, hidden_here) for _ in range(3))
    ffn_in = [added(early, width) for _ in range(2)]
    down_out = added(early, width)
    adapters = adapt_attn_in.shape[0]
    marks = wide(early[0, :, 0, at : at + adapters])
    at = 0
    out_in = joined(late, heads * head_size)
    out_out = added(late, width)
    query_out = joined(late, heads * head_size)
    key_out, value_out = (joined(late, kv_heads * head_size) for _ in range(2))
    attn_in = [added(late, width) for _ in range(3)]

    def tables(terms):
        return sum(
            marks[s].reshape((adapters,) + (1,) * (terms.ndim - 1)) * terms[s][None] for s in range(shards)
        )

    def turned(terms):
        return tables(terms).transpose(0, 2, 1)

    return (
        layer_output[None],
        input_grad[None],
        turned(jnp.concatenate(attn_in, axis=1)),
        tables(query_out),
        tables(jnp.stack([key_out, value_out], axis=1)),
        turned(out_in),
        tables(out_out),
        turned(jnp.concatenate(ffn_in, axis=1)),
        tables(jnp.stack([gate_out, up_out], axis=1)),
        turned(down_in),
        tables(down_out),
    )


def solution(mesh):
    in_specs = (
        P("shard", "context", None),
        P("shard", "context", None),
        P("shard", None),
        P("shard"),
        P("shard", "context", None),
        P("shard", "tensor"),
        P("shard", "tensor"),
        P("shard", "tensor"),
        P("tensor", "shard"),
        P("shard", "tensor"),
        P("shard", "tensor"),
        P("tensor", "shard"),
        P("shard", None),
        P(None, "shard"),
        P("shard", None),
        P(None, "shard"),
        P(),
        P(),
        P(),
        P(),
        P(),
        P(),
        P(),
        P(),
        P(),
        P(None, None, "tensor"),
        P(None, None, None, "tensor"),
        P(None, "tensor", None),
        P(),
        P(),
        P(None, None, None, "tensor"),
        P(None, "tensor", None),
        P(),
    )
    out_specs = (
        P("shard", "context", None),
        P("shard", "context", None),
        P(),
        P(),
        P(),
        P(),
        P(),
        P(),
        P(),
        P(),
        P(),
    )
    return jax.shard_map(body, mesh=mesh, in_specs=in_specs, out_specs=out_specs, check_vma=False)
```

time: 2010 us -> 951 us (0.47)
  waiting for transfers between devices: 1530 us -> 247 us
  Pallas kernels: 0 us -> 288 us
  matrix products: 290 us -> 215 us
  blocking collectives: 28.2 us -> 0 us
    all_gather x9 -> x2, waiting for transfers between devices: 992 us -> 53.6 us  [share(): lax.all_gather(low(part), ('shard', 'context', 'tensor'), axis=0, tiled=F...]
    psum x5 -> x0, waiting for transfers between devices: 532 us -> none  [the longest x1 370 us: body(): lax.psum((sum_attn_in, place_part(sum_query_out, 2, tensor_slot, tensor_c...]
    pallas_call x0 -> x1, Pallas kernels: none -> 288 us  [gather(): pl.pallas_call(functools.partial(gather_kernel, plan, count, shards, dept...]
    ppermute x0 -> x9, waiting for transfers between devices: none -> 162 us  [swap(): return lax.ppermute(array, 'tensor', [(0, 1), (1, 0)])]
    dot_general x67 -> x58, matrix products: 290 us -> 215 us  [the longest x20 98.8 us: matmul_t(): lax.dot_general(low(left_op), low(right_op), (((1,), (1,)), ((), ())), pr...]
    reduce_scatter x0 -> x2, waiting for transfers between devices: none -> 31.9 us  [share(): part = lax.psum_scatter(packed, 'context', scatter_dimension=1, tiled=True)]
    all_gather x2 -> x0, blocking collectives: 28.2 us -> none  [the longest x1 14.3 us: body(): lax.all_gather(laurel_left, 'shard', axis=0, tiled=True)]
    convert_element_type x7 -> x15, other arithmetic: 8.56 us -> 32.4 us  [the longest x9 25 us: low(): return values.astype(jnp.bfloat16)]
  transfers between devices with their start and end apart: 16 -> 15, of which waited for: 13 -> 13; matrix products, arithmetic and copies ran while one was open for 11% -> 9% of each run, Pallas kernels for 0% -> 0%
where the time goes in v1:
time: 951 us; the launch traced here: 940 us
  Pallas kernels  288 us (30%)
  waiting for transfers between devices  247 us (26%)
  matrix products  215 us (23%)
  other arithmetic  92.9 us (10%)
  local copies, waits for them, and re-layouts  61.1 us (6%)
  starting transfers between devices  18.7 us (2%)
  between operations  17 us (2%)
    pallas_call x1, Pallas kernels, gather(): pl.pallas_call(functools.partial(gather_kernel, plan, count, shards, dept...  288 us
    ppermute x9, waiting for transfers between devices, swap(): return lax.ppermute(array, 'tensor', [(0, 1), (1, 0)])  162 us
    dot_general x20, matrix products, matmul_t(): lax.dot_general(low(left_op), low(right_op), (((1,), (1,)), ((), ())), pr...  98.8 us
    dot_general x21, matrix products, matmul(): jnp.dot(low(left_op), low(right_op), preferred_element_type=jnp.float32)  87.2 us
    all_gather x2, waiting for transfers between devices, share(): lax.all_gather(low(part), ('shard', 'context', 'tensor'), axis=0, tiled=F...  53.6 us
    reduce_scatter x2, waiting for transfers between devices, share(): part = lax.psum_scatter(packed, 'context', scatter_dimension=1, tiled=True)  31.9 us
    convert_element_type x9, other arithmetic, low(): return values.astype(jnp.bfloat16)  25 us
    unnamed x327, local copies, waits for them, and re-layouts  22.1 us
  transfers between devices with their start and end apart: 15, of which 13 were waited for; matrix products, arithmetic and copies ran while one was open for 9% of the time, Pallas kernels for 0%

profile of v1, /device:TPU:0, one launch (start us, length us, event | category | flops | bytes accessed | tf_op | source)
XLA Modules:
  0.0 939.7 jit_solution(11915704561294044971)
XLA Ops:
  14.0 287.9 %shard_map.392 = (bf16[2048,1024]{1,0:T(8,128)(2,1)S(1)}, bf16[2048,256]{1,0:T(8,128)(2,1)S(1)}, bf16[2048,256]{1,0:T(8,128)(2,1)S(1)}, bf16[2048,64]{1,0:T(8,12...) custom-call(bf16[512,1024]{1,0:T(8,128)(2,1)S(1)} %copy-done.10, ...), custom_call_target="tpu_custom_call" | custom-call | tf_op jit(solution)/shard_map/pallas_call | solution.py:198
  308.2 2.8 multiply_reduce_fusion.11
  313.3 3.3 collective-permute-start
  316.7 5.2 fusion.297
  324.4 3.2 reshape.762
  327.6 2.9 multiply_reduce_fusion.9
  356.0 4.0 multiply_reduce_fusion.7
  360.0 17.9 %collective-permute-done.1 = bf16[256,2048]{1,0:T(8,128)(2,1)} collective-permute-done((bf16[256,2048]{1,0:T(8,128)(2,1)}, bf16[256,2048]{1,0:T(8,128)(2,1)}, u32[]{:S(2)}, u32[]{:S(2)}) %collective-permute-start.1) | collective-permute-done | bytes 1048608 | tf_op jit(solution)/shard_map/ppermute | solution.py:222
  380.4 3.2 multiply_reduce_fusion.6
  384.3 8.6 multiply_convert_fusion.2
  394.5 22.8 %collective-permute-done.2 = bf16[256,2048]{1,0:T(8,128)(2,1)S(1)} collective-permute-done((bf16[256,2048]{1,0:T(8,128)(2,1)S(1)}, bf16[256,2048]{1,0:T(8,128)(2,1)S(1)}, u32[]{:S(2)}, u32[]{:S(2)}) %collective-permute-start.2) | collective-permute-done | bytes 1048608 | tf_op jit(solution)/shard_map/ppermute | solution.py:222
  420.4 4.6 fusion.199
  425.0 14.5 %convolution_add_fusion.2 = f32[512,4096]{1,0:T(8,128)} fusion(f32[512,4096]{1,0:T(8,128)S(1)} %fusion.194, bf16[2048,4096]{1,0:T(8,128)(2,1)} %get-tuple-element.28, bf16[256,2048]{1,0:T(8,128)(2,1)S(1)} %collective-permute-done.2, bf16[256,2048]{1,0:T(8,128)(2,1)S(1)} %multiply_convert_fusion.2), kind=kOutput, calls=%fused_computation.25 | convolution fusion | flops 8596226048 | bytes 35651584 | tf_op jit(solution)/shard_map/dot_general | solution.py:259
  439.5 19.4 %multiply_convert_fusion.1 = (bf16[512,4096]{1,0:T(8,128)(2,1)}, f32[512,4096]{1,0:T(8,128)}) fusion(f32[512,4096]{1,0:T(8,128)} %convolution_add_fusion.2, f32[512,4096]{1,0:T(8,128)} %fusion.199, bf16[2048,4096]{1,0:T(8,128)(2,1)} %get-tuple-element.29, bf16[256,2048]{1,0:T(8,128)(2,1)} %copy-done.153, bf16[256,2048]{1,0:T(8,128)(2,1)S(1)} %multiply_convert_fusion.2), kind=kOutput, calls=%fused_computation.18 | convolution fusion | flops 8617197568 | bytes 48234496 | tf_op jit(solution)/shard_map/dot_general | solution.py:259
  458.9 3.4 convolution_convert_fusion.11
  464.5 12.8 %add_convert_fusion.2 = bf16[512,2048]{1,0:T(8,128)(2,1)S(1)} fusion(f32[512,2048]{1,0:T(8,128)S(1)} %fusion.208, bf16[512,4096]{1,0:T(8,128)(2,1)S(1)} %copy-done.34, bf16[4096,2048]{1,0:T(8,128)(2,1)} %get-tuple-element.30), kind=kOutput, calls=%fused_computation.59 | convolution fusion | flops 8592031744 | bytes 27262976 | tf_op jit(solution)/shard_map/dot_general | solution.py:259
  479.0 21.9 %collective-permute-done.3 = bf16[256,2048]{1,0:T(8,128)(2,1)S(1)} collective-permute-done((bf16[256,2048]{1,0:T(8,128)(2,1)S(1)}, bf16[256,2048]{1,0:T(8,128)(2,1)S(1)}, u32[]{:S(2)}, u32[]{:S(2)}) %collective-permute-start.3) | collective-permute-done | bytes 1048608 | tf_op jit(solution)/shard_map/ppermute | solution.py:222
  505.4 6.0 multiply_reduce_fusion.3
  511.4 5.7 fusion.31
  518.5 21.0 %collective-permute-done.5 = bf16[256,2048]{1,0:T(8,128)(2,1)S(1)} collective-permute-done((bf16[256,2048]{1,0:T(8,128)(2,1)S(1)}, bf16[256,2048]{1,0:T(8,128)(2,1)S(1)}, u32[]{:S(2)}, u32[]{:S(2)}) %collective-permute-start.5) | collective-permute-done | bytes 1048608 | tf_op jit(solution)/shard_map/ppermute | solution.py:222
  542.0 5.4 fusion.176
  547.4 23.8 %fusion.6 = (bf16[512,4096]{1,0:T(8,128)(2,1)}, bf16[512,4096]{1,0:T(8,128)(2,1)}) fusion(f32[512,4096]{1,0:T(8,128)} %convolution_add_fusion.2, f32[512,4096]{1,0:T(8,128)} %get-tuple-element.140, f32[512,4096]{1,0:T(8,128)} %fusion.176, bf16[4096,2048]{1,0:T(8,128)(2,1)} %get-tuple-element.30, bf16[256,2048]{1,0:T(8,128)(2,1)} %copy-done.154, ...), kind=kOutput, calls=%fused_computation.8 | convolution fusion | flops 8646557696 | bytes 52428800 | tf_op jit(solution)/shard_map/dot_general | solution.py:263
  571.3 3.5 convolution_convert_fusion.10
  574.8 14.0 %fusion.311 = f32[512,2048]{1,0:T(8,128)} fusion(bf16[512,4096]{1,0:T(8,128)(2,1)S(1)} %copy-done.38, bf16[2048,4096]{1,0:T(8,128)(2,1)} %get-tuple-element.28), kind=kOutput, calls=%fused_computation.550 | convolution fusion | flops 8589934592 | bytes 25165824 | tf_op jit(solution)/shard_map/dot_general | solution.py:263
  590.0 3.7 fusion.179
  593.7 15.7 %add_convert_fusion.1 = bf16[512,2048]{1,0:T(8,128)(2,1)S(1)} fusion(f32[512,2048]{1,0:T(8,128)} %fusion.179, f32[512,2048]{1,0:T(8,128)} %fusion.311, bf16[512,4096]{1,0:T(8,128)(2,1)} %get-tuple-element.41, bf16[2048,4096]{1,0:T(8,128)(2,1)} %get-tuple-element.29), kind=kOutput, calls=%fused_computation.58 | convolution fusion | flops 8593080320 | bytes 31457280 | tf_op jit(solution)/shard_map/dot_general | solution.py:263
  613.9 19.7 %collective-permute-done.6 = bf16[256,2048]{1,0:T(8,128)(2,1)S(1)} collective-permute-done((bf16[256,2048]{1,0:T(8,128)(2,1)}, bf16[256,2048]{1,0:T(8,128)(2,1)S(1)}, u32[]{:S(2)}, u32[]{:S(2)}) %collective-permute-start.6) | collective-permute-done | bytes 1048608 | tf_op jit(solution)/shard_map/ppermute | solution.py:222
  635.4 4.2 multiply_reduce_fusion.1
  648.9 14.2 %collective-permute-done.7 = bf16[256,2048]{1,0:T(8,128)(2,1)S(1)} collective-permute-done((bf16[256,2048]{1,0:T(8,128)(2,1)S(1)}, bf16[256,2048]{1,0:T(8,128)(2,1)S(1)}, u32[]{:S(2)}, u32[]{:S(2)}) %collective-permute-start.7) | collective-permute-done | bytes 1048608 | tf_op jit(solution)/shard_map/ppermute | solution.py:222
  666.0 3.4 add_convert_fusion.4
  671.1 4.8 fusion.57
  676.0 5.6 fusion.7
  714.9 16.8 %reduce-scatter.5.cloned.1.call-done = f32[16,2688]{1,0:T(8,128)} async-done(((f32[16,10752]{1,0:T(8,128)}), f32[16,2688]{1,0:T(8,128)}) %reduce-scatter.5.cloned.1.call-update) | async-done | bytes 172048 | tf_op jit(solution)/shard_map/reduce_scatter | solution.py:275
  733.3 4.7 fusion.312
  745.6 15.1 %reduce-scatter.3.cloned.1.call-done = f32[16,4736]{1,0:T(8,128)} async-done(((f32[16,18944]{1,0:T(8,128)}), f32[16,4736]{1,0:T(8,128)}) %reduce-scatter.3.cloned.1.call-update) | async-done | bytes 303120 | tf_op jit(solution)/shard_map/reduce_scatter | solution.py:275
  764.0 6.5 collective-permute-done.9
  770.4 6.8 fusion.43
  777.3 3.1 fusion.37
  781.9 12.8 %collective-permute-done.4 = bf16[256,2048]{1,0:T(8,128)(2,1)S(1)} collective-permute-done((bf16[256,2048]{1,0:T(8,128)(2,1)S(1)}, bf16[256,2048]{1,0:T(8,128)(2,1)S(1)}, u32[]{:S(2)}, u32[]{:S(2)}) %collective-permute-start.4) | collective-permute-done | bytes 1048608 | tf_op jit(solution)/shard_map/ppermute | solution.py:222
  797.1 25.0 %collective-permute-done.10 = bf16[256,2048]{1,0:T(8,128)(2,1)S(1)} collective-permute-done((bf16[256,2048]{1,0:T(8,128)(2,1)S(1)}, bf16[256,2048]{1,0:T(8,128)(2,1)S(1)}, u32[]{:S(2)}, u32[]{:S(2)}) %collective-permute-start.10) | collective-permute-done | bytes 1048608 | tf_op jit(solution)/shard_map/ppermute | solution.py:222
  824.5 4.0 all-gather.7.cloned.1.call-done
  828.5 4.7 copy.171
  833.2 4.8 reshape.772
  845.3 49.6 %all-gather.5.cloned.1.call-done = bf16[512,4736]{1,0:T(8,128)(2,1)} async-done(((bf16[16,4736]{1,0:T(8,128)(2,1)}), bf16[512,4736]{1,0:T(8,128)(2,1)}) %all-gather.5.cloned.1.call-update) | async-done | bytes 4849680 | tf_op jit(solution)/shard_map/all_gather | solution.py:276
  894.9 7.1 copy.153
  902.0 7.9 reshape.770
  916.5 3.0 multiply_add_fusion.1
  919.6 4.4 multiply_add_fusion
  (496 shorter events, 157.0 us)
Async XLA Ops:
  7.2 411.9 %copy-start = (bf16[8,2,16,4096]{3,2,1,0:T(8,128)(2,1)S(1)}, bf16[8,2,16,4096]{3,2,1,0:T(8,128)(2,1)}, u32[]{:S(2)}) copy-start(bf16[8,2,16,4096]{3,2,1,0:T(8,128)(2,1)} %param.63) | copy-start | bytes 6291460
  7.2 724.4 %reduce-scatter.5.cloned.1.call-start = ((), (), s32[]{:S(2)}) async-start(), calls=%async_computation.3 | async-start | bytes 860160 | tf_op jit(solution)/shard_map/reduce_scatter | solution.py:275
  7.3 327.4 %copy-start.146 = (f32[128]{0:T(128)}, f32[128]{0:T(128)S(1)}, u32[]{:S(2)}) copy-start(f32[128]{0:T(128)S(1)} %multiply_exponential_fusion) | copy-start | bytes 1540
  10.2 306.5 %copy-start.150 = (f32[512]{0:T(512)}, f32[512]{0:T(512)S(1)}, u32[]{:S(2)}) copy-start(f32[512]{0:T(512)S(1)} %add_rsqrt_fusion) | copy-start | bytes 6148
  13.0 308.9 %copy-start.91 = (bf16[512,48]{0,1:T(8,128)(2,1)}, bf16[512,48]{0,1:T(8,128)(2,1)S(1)}, u32[]{:S(2)}) copy-start(bf16[512,48]{0,1:T(8,128)(2,1)S(1)} %fusion.62) | copy-start | bytes 147460
  14.0 290.0 %copy-start.30 = (bf16[1,512,2048]{2,1,0:T(8,128)(2,1)S(1)}, bf16[1,512,2048]{2,1,0:T(8,128)(2,1)}, u32[]{:S(2)}) copy-start(bf16[1,512,2048]{2,1,0:T(8,128)(2,1)} %param.33) | copy-start | bytes 6291460
  304.0 51.9 %copy-start.2 = (bf16[2048,64]{1,0:T(8,128)(2,1)}, bf16[2048,64]{1,0:T(8,128)(2,1)S(1)}, u32[]{:S(2)}) copy-start(bf16[2048,64]{1,0:T(8,128)(2,1)S(1)} %get-tuple-element.26) | copy-start | bytes 786436
  304.0 51.9 %copy-start.8 = (bf16[64,2048]{1,0:T(8,128)(2,1)}, bf16[64,2048]{1,0:T(8,128)(2,1)S(1)}, u32[]{:S(2)}) copy-start(bf16[64,2048]{1,0:T(8,128)(2,1)S(1)} %get-tuple-element.27) | copy-start | bytes 786436
  307.2 27.5 %copy-start.106 = (f32[512]{0:T(512)}, f32[512]{0:T(512)S(1)}, u32[]{:S(2)}) copy-start(f32[512]{0:T(512)S(1)} %subtract_convert_fusion.1) | copy-start | bytes 6148
  313.3 22.7 %collective-permute-start = (bf16[2,512,1,256]{1,3,2,0:T(8,128)(2,1)}, bf16[2,512,1,256]{1,3,2,0:T(8,128)(2,1)}, u32[]{:S(2)}, u32[]{:S(2)}) collective-permute-start(bf16[2,512,1,256]{1,3,2,0:T(8,128)(2,1)} %pad_maximum_fusion.12), channel_id=1, source_target_pairs={{0,2},{2,4},{4,6},{1,3},{3,5},{5,7},{8,10},{10,12},{12,14},{9,11},... | collective-permute-start | bytes 1572872 | tf_op jit(solution)/shard_map/ppermute | solution.py:218
  352.4 25.5 %collective-permute-start.1 = (bf16[256,2048]{1,0:T(8,128)(2,1)}, bf16[256,2048]{1,0:T(8,128)(2,1)}, u32[]{:S(2)}, u32[]{:S(2)}) collective-permute-start(bf16[256,2048]{1,0:T(8,128)(2,1)} %constant_dynamic-slice_fusion.1), channel_id=1, source_target_pairs={{0,1},{1,0},{2,3},{3,2},{4,5},{5,4},{6,7},{7,6},{8,9},{9,8},{10,11... | collective-permute-start | bytes 3145736 | tf_op jit(solution)/shard_map/ppermute | solution.py:222
  355.4 25.0 %copy-start.121 = (f32[256]{0:T(256)}, f32[256]{0:T(256)S(1)}, u32[]{:S(2)}) copy-start(f32[256]{0:T(256)S(1)} %fusion.272) | copy-start | bytes 3076
  355.9 24.5 %copy-start.112 = (f32[2048]{0:T(1024)S(1)}, f32[2048]{0:T(1024)}, u32[]{:S(2)}) copy-start(f32[2048]{0:T(1024)} %param.51) | copy-start | bytes 24580
  355.9 24.5 %copy-start.114 = (f32[2048]{0:T(1024)S(1)}, f32[2048]{0:T(1024)}, u32[]{:S(2)}) copy-start(f32[2048]{0:T(1024)} %param.50) | copy-start | bytes 24580
  360.0 20.4 %copy-start.28 = (f32[256,2048]{1,0:T(8,128)S(1)}, f32[256,2048]{1,0:T(8,128)}, u32[]{:S(2)}) copy-start(f32[256,2048]{1,0:T(8,128)} %get-tuple-element.132) | copy-start | bytes 6291460
  360.0 23.6 %copy-start.123 = (f32[256]{0:T(256)}, f32[256]{0:T(256)S(1)}, u32[]{:S(2)}) copy-start(f32[256]{0:T(256)S(1)} %fusion.273) | copy-start | bytes 3076
  383.6 35.4 %copy-start.24 = (f32[256,2048]{1,0:T(8,128)}, f32[256,2048]{1,0:T(8,128)S(1)}, u32[]{:S(2)}) copy-start(f32[256,2048]{1,0:T(8,128)S(1)} %get-tuple-element.39) | copy-start | bytes 6291460
  392.9 46.6 %copy-start.70 = (bf16[256,2048]{1,0:T(8,128)(2,1)}, bf16[256,2048]{1,0:T(8,128)(2,1)S(1)}, u32[]{:S(2)}) copy-start(bf16[256,2048]{1,0:T(8,128)(2,1)S(1)} %multiply_convert_fusion.2) | copy-start | bytes 3145732
  392.9 24.4 %collective-permute-start.2 = (bf16[256,2048]{1,0:T(8,128)(2,1)S(1)}, bf16[256,2048]{1,0:T(8,128)(2,1)S(1)}, u32[]{:S(2)}, u32[]{:S(2)}) collective-permute-start(bf16[256,2048]{1,0:T(8,128)(2,1)S(1)} %multiply_convert_fusion.2), channel_id=1, source_target_pairs={{0,1},{1,0},{2,3},{3,2},{4,5},{5,4},{6,7},{7,6},{8,9},{9,8},{10,11... | collective-permute-start | bytes 3145736 | tf_op jit(solution)/shard_map/ppermute | solution.py:222
  477.3 24.0 %copy-start.48 = (bf16[512,2048]{1,0:T(8,128)(2,1)}, bf16[512,2048]{1,0:T(8,128)(2,1)S(1)}, u32[]{:S(2)}) copy-start(bf16[512,2048]{1,0:T(8,128)(2,1)S(1)} %add_convert_fusion.2) | copy-start | bytes 6291460
  477.3 24.0 %copy-start.19 = (bf16[2048,256]{1,0:T(8,128)(2,1)S(1)}, bf16[2048,256]{1,0:T(8,128)(2,1)}, u32[]{:S(2)}) copy-start(bf16[2048,256]{1,0:T(8,128)(2,1)} %copy-done.18) | copy-start | bytes 3145732
  477.3 24.0 %copy-start.25 = (f32[256,2048]{1,0:T(8,128)S(1)}, f32[256,2048]{1,0:T(8,128)}, u32[]{:S(2)}) copy-start(f32[256,2048]{1,0:T(8,128)} %copy-done.24) | copy-start | bytes 6291460
  477.3 24.0 %copy-start.139 = (f32[2048]{0:T(1024)S(1)}, f32[2048]{0:T(1024)}, u32[]{:S(2)}) copy-start(f32[2048]{0:T(1024)} %param.53) | copy-start | bytes 24580
  477.4 23.5 %collective-permute-start.3 = (bf16[256,2048]{1,0:T(8,128)(2,1)S(1)}, bf16[256,2048]{1,0:T(8,128)(2,1)S(1)}, u32[]{:S(2)}, u32[]{:S(2)}) collective-permute-start(bf16[256,2048]{1,0:T(8,128)(2,1)S(1)} %slice.522), channel_id=1, source_target_pairs={{0,1},{1,0},{2,3},{3,2},{4,5},{5,4},{6,7},{7,6},{8,9},{9,8},{10,11... | collective-permute-start | bytes 3145736 | tf_op jit(solution)/shard_map/ppermute | solution.py:222
  517.1 30.4 %copy-start.68 = (bf16[256,2048]{1,0:T(8,128)(2,1)}, bf16[256,2048]{1,0:T(8,128)(2,1)S(1)}, u32[]{:S(2)}) copy-start(bf16[256,2048]{1,0:T(8,128)(2,1)S(1)} %get-tuple-element.52) | copy-start | bytes 3145732
  517.1 22.5 %collective-permute-start.5 = (bf16[256,2048]{1,0:T(8,128)(2,1)S(1)}, bf16[256,2048]{1,0:T(8,128)(2,1)S(1)}, u32[]{:S(2)}, u32[]{:S(2)}) collective-permute-start(bf16[256,2048]{1,0:T(8,128)(2,1)S(1)} %get-tuple-element.52), channel_id=1, source_target_pairs={{0,1},{1,0},{2,3},{3,2},{4,5},{5,4},{6,7},{7,6},{8,9},{9,8},{10,11... | collective-permute-start | bytes 3145736 | tf_op jit(solution)/shard_map/ppermute | solution.py:222
  593.7 20.1 %copy-start.113 = (f32[2048]{0:T(1024)S(1)}, f32[2048]{0:T(1024)}, u32[]{:S(2)}) copy-start(f32[2048]{0:T(1024)} %param.51) | copy-start | bytes 24580
  593.7 20.1 %copy-start.115 = (f32[2048]{0:T(1024)S(1)}, f32[2048]{0:T(1024)}, u32[]{:S(2)}) copy-start(f32[2048]{0:T(1024)} %param.50) | copy-start | bytes 24580
  610.7 22.8 %copy-start.26 = (f32[256,2048]{1,0:T(8,128)S(1)}, f32[256,2048]{1,0:T(8,128)}, u32[]{:S(2)}) copy-start(f32[256,2048]{1,0:T(8,128)} %copy-done.24) | copy-start | bytes 6291460
  610.7 22.8 %copy-start.98 = (f32[2048]{0:T(1024)S(1)}, f32[2048]{0:T(1024)}, u32[]{:S(2)}) copy-start(f32[2048]{0:T(1024)} %param.52) | copy-start | bytes 24580
  611.8 21.8 %collective-permute-start.6 = (bf16[256,2048]{1,0:T(8,128)(2,1)}, bf16[256,2048]{1,0:T(8,128)(2,1)S(1)}, u32[]{:S(2)}, u32[]{:S(2)}) collective-permute-start(bf16[256,2048]{1,0:T(8,128)(2,1)} %slice.524), channel_id=1, source_target_pairs={{0,1},{1,0},{2,3},{3,2},{4,5},{5,4},{6,7},{7,6},{8,9},{9,8},{10,11... | collective-permute-start | bytes 3145736 | tf_op jit(solution)/shard_map/ppermute | solution.py:222
  613.8 21.5 %copy-start.128 = (f32[256]{0:T(256)S(1)}, f32[256]{0:T(256)}, u32[]{:S(2)}) copy-start(f32[256]{0:T(256)} %copy-done.127) | copy-start | bytes 3076
  613.8 21.6 %copy-start.29 = (f32[256,2048]{1,0:T(8,128)S(1)}, f32[256,2048]{1,0:T(8,128)}, u32[]{:S(2)}) copy-start(f32[256,2048]{1,0:T(8,128)} %get-tuple-element.132) | copy-start | bytes 6291460
  613.8 21.5 %copy-start.33 = (bf16[512,2048]{1,0:T(8,128)(2,1)S(1)}, bf16[512,2048]{1,0:T(8,128)(2,1)}, u32[]{:S(2)}) copy-start(bf16[512,2048]{1,0:T(8,128)(2,1)} %copy-done.32) | copy-start | bytes 6291460
  613.8 21.5 %copy-start.149 = (f32[256]{0:T(256)S(1)}, f32[256]{0:T(256)}, u32[]{:S(2)}) copy-start(f32[256]{0:T(256)} %get-tuple-element.127) | copy-start | bytes 3076
  642.4 20.7 %collective-permute-start.7 = (bf16[256,2048]{1,0:T(8,128)(2,1)S(1)}, bf16[256,2048]{1,0:T(8,128)(2,1)S(1)}, u32[]{:S(2)}, u32[]{:S(2)}) collective-permute-start(bf16[256,2048]{1,0:T(8,128)(2,1)S(1)} %fusion.34), channel_id=1, source_target_pairs={{0,1},{1,0},{2,3},{3,2},{4,5},{5,4},{6,7},{7,6},{8,9},{9,8},{10,11... | collective-permute-start | bytes 3145736 | tf_op jit(solution)/shard_map/ppermute | solution.py:222
  689.1 9.4 %collective-permute-start.8 = (bf16[2,512,1,256]{1,3,2,0:T(8,128)(2,1)}, bf16[2,512,1,256]{1,3,2,0:T(8,128)(2,1)}, u32[]{:S(2)}, u32[]{:S(2)}) collective-permute-start(bf16[2,512,1,256]{1,3,2,0:T(8,128)(2,1)} %fusion.78), channel_id=1, source_target_pairs={{2,0},{4,2},{6,4},{3,1},{5,3},{7,5},{10,8},{12,10},{14,12},{11,9},... | collective-permute-start | bytes 1572872 | tf_op jit(solution)/shard_map/ppermute | solution.py:218
  708.1 52.6 %reduce-scatter.3.cloned.1.call-start = ((), (), s32[]{:S(2)}) async-start(), calls=%async_computation.2 | async-start | bytes 1515520 | tf_op jit(solution)/shard_map/reduce_scatter | solution.py:275
  714.8 113.7 %all-gather.7.cloned.1.call-start = ((), (), s32[]{:S(2)}) async-start(), calls=%async_computation.5 | async-start | bytes 2838528 | tf_op jit(solution)/shard_map/all_gather | solution.py:276
  733.2 161.7 %all-gather.5.cloned.1.call-start = ((), (), s32[]{:S(2)}) async-start(), calls=%async_computation.4 | async-start | bytes 5001216 | tf_op jit(solution)/shard_map/all_gather | solution.py:276
  743.0 20.9 %copy-start.138 = (f32[256]{0:T(256)S(1)}, f32[256]{0:T(256)}, u32[]{:S(2)}) copy-start(f32[256]{0:T(256)} %copy-done.137) | copy-start | bytes 3076
  743.0 20.9 %copy-start.148 = (f32[256]{0:T(256)S(1)}, f32[256]{0:T(256)}, u32[]{:S(2)}) copy-start(f32[256]{0:T(256)} %get-tuple-element.33) | copy-start | bytes 3076
  743.0 27.4 %copy-start.3 = (bf16[2048,64]{1,0:T(8,128)(2,1)S(1)}, bf16[2048,64]{1,0:T(8,128)(2,1)}, u32[]{:S(2)}) copy-start(bf16[2048,64]{1,0:T(8,128)(2,1)} %copy-done.2) | copy-start | bytes 786436
  743.0 27.4 %copy-start.9 = (bf16[64,2048]{1,0:T(8,128)(2,1)S(1)}, bf16[64,2048]{1,0:T(8,128)(2,1)}, u32[]{:S(2)}) copy-start(bf16[64,2048]{1,0:T(8,128)(2,1)} %copy-done.8) | copy-start | bytes 786436
  743.0 27.4 %copy-start.124 = (f32[256]{0:T(256)S(1)}, f32[256]{0:T(256)}, u32[]{:S(2)}) copy-start(f32[256]{0:T(256)} %copy-done.123) | copy-start | bytes 3076
  744.1 26.4 %collective-permute-start.9 = (bf16[256,2048]{1,0:T(8,128)(2,1)}, bf16[256,2048]{1,0:T(8,128)(2,1)}, u32[]{:S(2)}, u32[]{:S(2)}) collective-permute-start(bf16[256,2048]{1,0:T(8,128)(2,1)} %constant_dynamic-slice_fusion), channel_id=1, source_target_pairs={{0,1},{1,0},{2,3},{3,2},{4,5},{5,4},{6,7},{7,6},{8,9},{9,8},{10,11... | collective-permute-start | bytes 3145736 | tf_op jit(solution)/shard_map/ppermute | solution.py:222
  762.4 32.4 %collective-permute-start.4 = (bf16[256,2048]{1,0:T(8,128)(2,1)S(1)}, bf16[256,2048]{1,0:T(8,128)(2,1)S(1)}, u32[]{:S(2)}, u32[]{:S(2)}) collective-permute-start(bf16[256,2048]{1,0:T(8,128)(2,1)S(1)} %copy-done.54), channel_id=1, source_target_pairs={{0,1},{1,0},{2,3},{3,2},{4,5},{5,4},{6,7},{7,6},{8,9},{9,8},{10,11... | collective-permute-start | bytes 3145736 | tf_op jit(solution)/shard_map/ppermute | solution.py:222
  780.4 41.7 %collective-permute-start.10 = (bf16[256,2048]{1,0:T(8,128)(2,1)S(1)}, bf16[256,2048]{1,0:T(8,128)(2,1)S(1)}, u32[]{:S(2)}, u32[]{:S(2)}) collective-permute-start(bf16[256,2048]{1,0:T(8,128)(2,1)S(1)} %fusion.37), channel_id=1, source_target_pairs={{0,1},{1,0},{2,3},{3,2},{4,5},{5,4},{6,7},{7,6},{8,9},{9,8},{10,11... | collective-permute-start | bytes 3145736 | tf_op jit(solution)/shard_map/ppermute | solution.py:222
  (128 other events, 432.4 us)
Sparse Core Ops, SparseCore 0:
  708.2 23.3 reduce-scatter.4
  734.8 25.8 reduce-scatter.2
  764.6 63.8 all-gather.6
  832.1 62.7 all-gather.4

commit v2 on v1

v2 whole, which is shorter than its diff:
```python
import functools
import math

import jax
import jax.numpy as jnp
from jax import lax
from jax.experimental import pallas as pl
from jax.experimental.pallas import tpu as pltpu
from jax.sharding import PartitionSpec as P

WINDOW = 512
EPSILON = 1e-06
ROOT_HALF = 0.7071067811865476
GELU_SCALE = math.sqrt(2.0 / math.pi)
GELU_CUBE = 0.044715

MESH = pl.DeviceIdType.MESH


def shifted(array, axis, by):
    count = lax.axis_size(axis)
    pairs = [(i, i + by) for i in range(count) if 0 <= i + by < count]
    return lax.ppermute(array, axis, pairs)


def swap(array):
    return lax.ppermute(array, "tensor", [(0, 1), (1, 0)])


def rms_norm(values, scaling):
    return values * lax.rsqrt(jnp.mean(values * values, axis=-1, keepdims=True) + EPSILON) * scaling


def gelu_tanh(values):
    return jax.nn.gelu(values, approximate=True)


def rotate_half(values, cosine, sine_table):
    middle = values.shape[-1] // 2
    former = values[..., :middle]
    latter = values[..., middle:]
    return jnp.concatenate(
        [former * cosine - latter * sine_table, latter * cosine + former * sine_table], axis=-1
    )


def rope_tables(positions, head_size):
    frequency = jnp.exp(
        jnp.arange(head_size // 2, dtype=jnp.float32) * (-2.0 * math.log(10000.0) / head_size)
    )
    angles = positions.astype(jnp.float32)[..., None] * frequency
    return (jnp.cos(angles), jnp.sin(angles))


def low(values):
    return values.astype(jnp.bfloat16)


def wide(values):
    return values.astype(jnp.float32)


def matmul(left_op, right_op):
    return jnp.dot(low(left_op), low(right_op), preferred_element_type=jnp.float32)


def matmul_t(left_op, right_op):
    return lax.dot_general(
        low(left_op), low(right_op), (((1,), (1,)), ((), ())), preferred_element_type=jnp.float32
    )


def outer(left_op, right_op):
    return lax.dot_general(
        low(left_op), low(right_op), (((0,), (0,)), ((), ())), preferred_element_type=jnp.float32
    )


def dot(left, right):
    return lax.dot_general(left, right, (((1,), (0,)), ((), ())), preferred_element_type=jnp.float32)


def dot_t(left, right):
    return lax.dot_general(left, right, (((1,), (1,)), ((), ())), preferred_element_type=jnp.float32)


def dot_o(left, right):
    return lax.dot_general(left, right, (((0,), (0,)), ((), ())), preferred_element_type=jnp.float32)


def row_mean(values):
    return jnp.mean(values, axis=-1, keepdims=True)


def inverse_rms(values):
    return lax.rsqrt(row_mean(values * values) + EPSILON)


def rms_back(values, inverse, scaled):
    return inverse * scaled - values * (inverse * inverse * inverse * row_mean(values * scaled))


def gelu_parts(values):
    squared = values * values
    bend = jnp.tanh(GELU_SCALE * values * (1.0 + GELU_CUBE * squared))
    rise = 0.5 * (1.0 + bend)
    slope = rise + 0.5 * values * (1.0 - bend * bend) * (GELU_SCALE * (1.0 + 3.0 * GELU_CUBE * squared))
    return values * rise, slope


def ffn_back_kernel(
    grad, gate, up, codes, code_down, ffn, w_down, w_gate, w_up, down_in, down_out, gu_out, ffn_in,
    part, term_gate, term_up, term_down, term_ffn, term_out, total, back_codes, ffn_codes,
):
    step = pl.program_id(0)
    rank = down_in.shape[0]

    @pl.when(step == 0)
    def _():
        back_codes[...] = low(dot_t(grad[...], down_out[...]))
        total[...] = jnp.zeros_like(total)
        ffn_codes[...] = jnp.zeros_like(ffn_codes)
        term_out[...] = dot_o(code_down[...], grad[...])

    hidden_grad = dot_t(grad[...], w_down[...]) + dot(back_codes[...], down_in[...])
    up_now = wide(up[...])
    act, slope = gelu_parts(wide(gate[...]))
    grad_gate = low(hidden_grad * up_now * slope)
    grad_up = low(hidden_grad * act)
    hidden = low(act * up_now)
    total[...] += dot_t(grad_gate, w_gate[...]) + dot_t(grad_up, w_up[...])
    ffn_codes[0] += dot_t(grad_gate, gu_out[0])
    ffn_codes[1] += dot_t(grad_up, gu_out[1])
    term_gate[...] = dot_o(codes[:, :rank], grad_gate)
    term_up[...] = dot_o(codes[:, rank:], grad_up)
    term_down[...] = dot_o(back_codes[...], hidden)

    @pl.when(step == pl.num_programs(0) - 1)
    def _():
        first, second = low(ffn_codes[0]), low(ffn_codes[1])
        part[...] = low(total[...] + dot(first, ffn_in[:rank]) + dot(second, ffn_in[rank:]))
        term_ffn[:rank] = dot_o(first, ffn[...])
        term_ffn[rank:] = dot_o(second, ffn[...])


def ffn_back(group, grad, gate, up, codes, code_down, ffn, w_down, w_gate, w_up, down_in, down_out, gu_out, ffn_in):
    rows, width = grad.shape
    hidden = gate.shape[1]
    rank = down_in.shape[0]
    block = min(512, hidden)
    whole = lambda *shape: pl.BlockSpec(shape, lambda j: (0,) * len(shape))
    picked = lambda columns: pl.BlockSpec((rows, columns), lambda j: (group, 0))
    f32 = jnp.float32
    return pl.pallas_call(
        ffn_back_kernel,
        grid=(hidden // block,),
        in_specs=[
            whole(rows, width),
            pl.BlockSpec((rows, block), lambda j: (group, j)),
            pl.BlockSpec((rows, block), lambda j: (group, j)),
            picked(2 * rank),
            picked(rank),
            picked(width),
            pl.BlockSpec((block, width), lambda j: (j, 0)),
            pl.BlockSpec((width, block), lambda j: (0, j)),
            pl.BlockSpec((width, block), lambda j: (0, j)),
            pl.BlockSpec((rank, block), lambda j: (0, j)),
            whole(rank, width),
            pl.BlockSpec((2, rank, block), lambda j: (0, 0, j)),
            whole(2 * rank, width),
        ],
        out_specs=[
            whole(rows, width),
            pl.BlockSpec((rank, block), lambda j: (0, j)),
            pl.BlockSpec((rank, block), lambda j: (0, j)),
            pl.BlockSpec((rank, block), lambda j: (0, j)),
            whole(2 * rank, width),
            whole(rank, width),
        ],
        out_shape=[
            jax.ShapeDtypeStruct((rows, width), jnp.bfloat16),
            jax.ShapeDtypeStruct((rank, hidden), f32),
            jax.ShapeDtypeStruct((rank, hidden), f32),
            jax.ShapeDtypeStruct((rank, hidden), f32),
            jax.ShapeDtypeStruct((2 * rank, width), f32),
            jax.ShapeDtypeStruct((rank, width), f32),
        ],
        scratch_shapes=[
            pltpu.VMEM((rows, width), f32),
            pltpu.VMEM((rows, rank), jnp.bfloat16),
            pltpu.VMEM((2, rows, rank), f32),
        ],
        compiler_params=pltpu.CompilerParams(vmem_limit_bytes=48 * 2**20),
        cost_estimate=pl.CostEstimate(
            flops=6 * rows * width * hidden, bytes_accessed=6 * width * hidden, transcendentals=rows * hidden
        ),
    )(grad, gate, up, codes, code_down, ffn, w_down, w_gate, w_up, down_in, down_out, gu_out, ffn_in)


def crown_kernel(
    mine, theirs, combined, per_layer, cotangent, input_gate, input_proj, gain_post, gain_layer,
    output, grad_down, grad_after,
):
    down = wide(mine[...]) + wide(theirs[...])
    down_inverse = inverse_rms(down)
    after = combined[...] + down * down_inverse * gain_post[...]
    mixing = wide(per_layer[...])
    act, slope = gelu_parts(dot(low(after), input_gate[...]))
    proj = dot(low(act * mixing), input_proj[...])
    proj_inverse = inverse_rms(proj)
    output[...] = low(after + proj * proj_inverse * gain_layer[...])
    grad = wide(cotangent[...])
    grad_proj = rms_back(proj, proj_inverse, grad * gain_layer[...])
    grad_gate = dot_t(low(grad_proj), input_proj[...]) * mixing * slope
    grad = grad + dot_t(low(grad_gate), input_gate[...])
    grad_after[...] = grad
    grad_down[...] = low(rms_back(down, down_inverse, grad * gain_post[...]))


def comb_back_kernel(
    mine, theirs, grad_after, combined, attn_proj, laurel_mid, left, right, gain_pre, gain_attn, gain_laurel,
    grad_attn, grad_comb, grad_normed,
):
    grad = (wide(mine[...]) + wide(theirs[...])) * gain_pre[...]
    comb = combined[...]
    grad = (grad_after[...] + rms_back(comb, inverse_rms(comb), grad)) * ROOT_HALF
    grad_comb[...] = grad
    proj = attn_proj[...]
    grad_attn[...] = low(rms_back(proj, inverse_rms(proj), grad * gain_attn[...]))
    end = dot(laurel_mid[...], right[...])
    grad_end = low(rms_back(end, inverse_rms(end), grad * gain_laurel[...]))
    grad_normed[...] = grad + dot(low(dot_t(grad_end, right[...])), left[...])


def rowwise(kernel, group, rows, arrays, constants, outs):
    width = max(a.shape[1] for a, _ in arrays)

    def spec(columns, at):
        return pl.BlockSpec((rows, columns), lambda i: (at, 0))

    return pl.pallas_call(
        kernel,
        grid=(1,),
        in_specs=[spec(a.shape[1], group if own is None else own) for a, own in arrays]
        + [pl.BlockSpec(c.shape, lambda i: (0, 0)) for c in constants],
        out_specs=[spec(columns, 0) for columns, _ in outs],
        out_shape=[jax.ShapeDtypeStruct((rows, columns), kind) for columns, kind in outs],
        compiler_params=pltpu.CompilerParams(vmem_limit_bytes=48 * 2**20),
        cost_estimate=pl.CostEstimate(
            flops=40 * rows * width + 2 * rows * width * 1024, bytes_accessed=24 * rows * width, transcendentals=rows
        ),
    )(*[a for a, _ in arrays], *constants)


def mover(sources, fulls, semaphores, shards):
    z_recv, y_recv, near_recv, far_recv, z_send, y_send, near_send, far_send = semaphores
    z, c = lax.axis_index("shard"), lax.axis_index("context")
    across = lax.rem(c + 2, 4)
    beside = c + 1 - 2 * lax.rem(c, 2)

    def greet(also=()):
        barrier = pltpu.get_barrier_semaphore()

        def signal(place):
            pl.semaphore_signal(barrier, inc=1, device_id=place, device_id_type=MESH)

        signal({"context": across})
        signal({"context": beside})
        for place in also:
            signal(place)

        @pl.when(z > 0)
        def _():
            signal({"shard": z - 1})

        @pl.when(z < shards - 1)
        def _():
            signal({"shard": z + 1})

        peers = 2 + len(also) + lax.div(z + shards - 1, shards) + lax.div(2 * shards - 2 - z, shards)
        pl.semaphore_wait(barrier, peers)

    def region(piece, s, q):
        _, item, axis, row, rows, col, cols = piece
        rows_here, cols_here = sources[item].shape
        part = rows // 4
        if axis == 0:
            return fulls[item].at[
                pl.ds(pl.multiple_of(s * rows_here + row + q * part, 16), part),
                pl.ds(pl.multiple_of(col, 128), cols),
            ]
        return fulls[item].at[
            pl.ds(pl.multiple_of(row + q * part, 16), part),
            pl.ds(pl.multiple_of(s * cols_here + col, 128), cols),
        ]

    def own(piece):
        _, item, axis, row, rows, col, cols = piece
        part = rows // 4
        return sources[item].at[
            pl.ds(pl.multiple_of(row + c * part, 16), part), pl.ds(pl.multiple_of(col, 128), cols)
        ]

    def copy(source, target, send, recv, place):
        return pltpu.make_async_remote_copy(
            src_ref=source, dst_ref=target, send_sem=send, recv_sem=recv, device_id=place, device_id_type=MESH
        )

    def along(piece, s, source, sender, by):
        slot = piece[0]
        return copy(source, region(piece, s, c), z_send.at[slot, sender], z_recv.at[slot, s], {"shard": z + by})

    def passed(piece, s, by):
        return along(piece, s, region(piece, s, c), s, by)

    def y_copy(piece, s, q):
        at = region(piece, s, q)
        return copy(at, at, y_send.at[piece[0], s], y_recv.at[piece[0], s], {"context": across})

    def near_copy(piece, s, q):
        at = region(piece, s, q)
        return copy(at, at, near_send.at[piece[0], s], near_recv.at[piece[0], s], {"context": beside})

    def far_copy(piece, s, q):
        at = region(piece, s, q)
        return copy(at, at, far_send.at[piece[0], s], far_recv.at[piece[0], s], {"context": beside})

    def begin(pieces):
        @pl.when(z < shards - 1)
        def _():
            for piece in pieces:
                along(piece, z, own(piece), z, 1).start()

        @pl.when(z > 0)
        def _():
            for piece in pieces:
                along(piece, z, own(piece), shards, -1).start()

    def relay(pieces, first=1, last=None):
        def hop(d, carry):
            @pl.when(z >= d)
            def _():
                s = z - d
                for piece in pieces:
                    passed(piece, s, 1).wait_recv()

                    @pl.when(z < shards - 1)
                    def _(piece=piece):
                        passed(piece, s, 1).start()

                    y_copy(piece, s, c).start()
                    near_copy(piece, s, c).start()

            @pl.when(z + d <= shards - 1)
            def _():
                s = z + d
                for piece in pieces:
                    passed(piece, s, -1).wait_recv()

                    @pl.when(z > 0)
                    def _(piece=piece):
                        passed(piece, s, -1).start()

                    y_copy(piece, s, c).start()
                    near_copy(piece, s, c).start()

            return carry

        last = shards - 1 if last is None else last
        if first == last:
            hop(first, 0)
        else:
            lax.fori_loop(first, last + 1, hop, 0)

    def others(pieces, act):
        def one(d, carry):
            for piece in pieces:
                act(piece, lax.rem(z + d, shards))
            return carry

        lax.fori_loop(1, shards, one, 0)

    def spread(pieces):
        def act(piece, s):
            y_copy(piece, s, across).wait_recv()
            far_copy(piece, s, across).start()

        others(pieces, act)

    def finish(pieces):
        def act(piece, s):
            near_copy(piece, s, beside).wait_recv()
            far_copy(piece, s, lax.rem(beside + 2, 4)).wait_recv()

        others(pieces, act)

    def flush(pieces):
        @pl.when(z < shards - 1)
        def _():
            for piece in pieces:
                along(piece, z, own(piece), z, 1).wait_send()

        @pl.when(z > 0)
        def _():
            for piece in pieces:
                along(piece, z, own(piece), shards, -1).wait_send()

        def act(piece, s):
            y_copy(piece, s, c).wait_send()
            near_copy(piece, s, c).wait_send()
            far_copy(piece, s, across).wait_send()

            @pl.when((s < z) & (z < shards - 1))
            def _():
                passed(piece, s, 1).wait_send()

            @pl.when((s > z) & (z > 0))
            def _():
                passed(piece, s, -1).wait_send()

        others(pieces, act)

    def own_place(item, axis):
        rows_here, cols_here = sources[item].shape
        if axis == 0:
            return fulls[item].at[pl.ds(pl.multiple_of(z * rows_here, 16), rows_here), :]
        return fulls[item].at[:, pl.ds(pl.multiple_of(z * cols_here, 128), cols_here)]

    return greet, begin, relay, spread, finish, flush, own_place


def mover_semaphores(slots, shards):
    table = pltpu.SemaphoreType.DMA((slots, shards))
    return [table, table, table, table, pltpu.SemaphoreType.DMA((slots, shards + 1)), table, table, table]


def full_shapes(weights, axes, shards):
    shapes = []
    for w, axis in zip(weights, axes):
        shape = list(w.shape)
        shape[axis] *= shards
        shapes.append(jax.ShapeDtypeStruct(tuple(shape), w.dtype))
    return shapes


def gather_kernel(axes, shards, *refs):
    count = len(axes)
    sources, fulls, held = refs[:count], refs[count : 2 * count], refs[2 * count : 3 * count]
    load_sem, store_sem = refs[3 * count : 3 * count + 2]
    greet, begin, relay, spread, finish, flush, own_place = mover(
        sources, fulls, refs[3 * count + 2 :], shards
    )
    pieces = [
        [(i, i, axes[i], 0, sources[i].shape[0], 0, sources[i].shape[1])] for i in range(count)
    ]
    greet()
    for piece in pieces:
        begin(piece)
    loads = [pltpu.make_async_copy(sources[i], held[i], load_sem.at[i]) for i in range(count)]
    stores = [pltpu.make_async_copy(held[i], own_place(i, axes[i]), store_sem.at[i]) for i in range(count)]
    for load in loads:
        load.start()
    for load, store in zip(loads, stores):
        load.wait()
        store.start()
    for piece in pieces:
        relay(piece)
    for piece in pieces:
        spread(piece)
    for piece in pieces:
        finish(piece)
    for piece in pieces:
        flush(piece)
    for store in stores:
        store.wait()


def gather(weights, axes, shards):
    count = len(weights)
    return pl.pallas_call(
        functools.partial(gather_kernel, axes, shards),
        out_shape=full_shapes(weights, axes, shards),
        in_specs=[pl.BlockSpec(memory_space=pl.ANY)] * count,
        out_specs=[pl.BlockSpec(memory_space=pl.ANY)] * count,
        scratch_shapes=[pltpu.VMEM(w.shape, w.dtype) for w in weights]
        + [pltpu.SemaphoreType.DMA((count,)), pltpu.SemaphoreType.DMA((count,))]
        + mover_semaphores(count, shards),
        compiler_params=pltpu.CompilerParams(
            collective_id=0, has_side_effects=True, vmem_limit_bytes=32 * 2**20
        ),
    )(*weights)


FORE_AXES = (1, 1, 0, 1, 0, 0, 1)


def fore_kernel(
    shards, block,
    w_output, w_right, w_lgate, w_lproj, w_gate, w_up, w_down,
    attended, tokens, laurel_mid, out_in, out_out, ffn_in, gu_out, down_in, down_out,
    gain_in, gain_attn, gain_laurel, gain_pre,
    full_output, full_right, full_lgate, full_lproj, full_gate, full_up, full_down, gate_out, up_out, ffn_out,
    attn_proj, combined, code_out, code_ffn, code_down, part,
    stage_a, stage_b, stage_c, stage_d, stage_e, stage_f, stage_g, out_w, right_w, gate_w, up_w, down_w, sent, got, ffn, total, codes, hidden,
    gate_keep, up_keep,
    load_sem, store_sem, weight_sem, keep_sem, ffn_sem, swap_send, swap_recv, *semaphores,
):
    sources = (w_output, w_right, w_lgate, w_lproj, w_gate, w_up, w_down)
    fulls = (full_output, full_right, full_lgate, full_lproj, full_gate, full_up, full_down)
    side = lax.axis_index("tensor")
    partner = {"tensor": 1 - side}
    greet, begin, relay, spread, finish, flush, own_place = mover(sources, fulls, semaphores, shards)
    rank = out_in.shape[0]
    count, width = ffn.shape
    half = count // 2
    quarter = half // 2
    groups = w_gate.shape[1] // block

    def whole(i):
        return (i, i, FORE_AXES[i], 0, sources[i].shape[0], 0, sources[i].shape[1])

    first = [whole(0), whole(1)]
    small = [whole(2), whole(3)]

    def group(g):
        base = 4 + 3 * g
        return [
            (base, 4, 0, 0, sources[4].shape[0], g * block, block),
            (base + 1, 5, 0, 0, sources[5].shape[0], g * block, block),
            (base + 2, 6, 1, g * block, block, 0, sources[6].shape[1]),
        ]

    greet([partner])
    begin(first)
    begin(group(0))
    begin(small)
    begin(group(1))
    stages = (stage_a, stage_b, stage_c, stage_d, stage_e, stage_f, stage_g)
    loads = [pltpu.make_async_copy(sources[i], stages[i], load_sem.at[i]) for i in range(7)]
    stores = [pltpu.make_async_copy(stages[i], own_place(i, FORE_AXES[i]), store_sem.at[i]) for i in range(7)]
    for load in loads:
        load.start()
    for load, store in zip(loads, stores):
        load.wait()
        store.start()
    for store in stores:
        store.wait()

    relay(first)
    spread(first)
    finish(first)
    load_out = pltpu.make_async_copy(full_output, out_w, weight_sem.at[0])
    load_right = pltpu.make_async_copy(full_right, right_w, weight_sem.at[1])
    load_out.start()
    load_right.start()
    code = low(dot_t(attended[...], out_in[...]))
    code_out[...] = code
    load_out.wait()
    load_right.wait()
    mine = pl.ds(pl.multiple_of(side * half, half), half)
    theirs = pl.ds(pl.multiple_of((1 - side) * half, half), half)
    sent[...] = low(dot(attended[theirs, :], out_w[...]) + dot(code_out[theirs, :], out_out[...]))
    swap_attn = pltpu.make_async_remote_copy(
        src_ref=sent, dst_ref=got, send_sem=swap_send.at[0], recv_sem=swap_recv.at[0],
        device_id=partner, device_id_type=MESH,
    )
    swap_attn.start()
    attn_proj[...] = dot(attended[mine, :], out_w[...]) + dot(code_out[mine, :], out_out[...])

    relay(group(0))
    swap_attn.wait()
    rows = 64

    def combine(i, carry):
        at = pl.ds(pl.multiple_of(i * rows, rows), rows)
        proj = attn_proj[at, :] + wide(got[at, :])
        attn_proj[at, :] = proj
        token = wide(tokens[at, :])
        normed = token * inverse_rms(token) * gain_in[...]
        end = dot(laurel_mid[at, :], right_w[...])
        comb = (
            token + proj * inverse_rms(proj) * gain_attn[...] + normed + end * inverse_rms(end) * gain_laurel[...]
        ) * ROOT_HALF
        combined[at, :] = comb
        to = pl.multiple_of(i * rows + lax.div(i * rows, quarter) * quarter, rows)
        ffn[pl.ds(to, rows), :] = low(comb * inverse_rms(comb) * gain_pre[...])
        return carry

    lax.fori_loop(0, half // rows, combine, 0)
    swaps = []
    for k in range(2):
        swaps.append(
            pltpu.make_async_remote_copy(
                src_ref=ffn.at[pl.ds(k * half, quarter), :], dst_ref=ffn.at[pl.ds(k * half + quarter, quarter), :],
                send_sem=swap_send.at[1 + k], recv_sem=swap_recv.at[1 + k],
                device_id=partner, device_id_type=MESH,
            )
        )
        swaps[k].start()
    relay(small)
    spread(small)
    total[...] = jnp.zeros_like(total)
    codes[...] = jnp.zeros_like(codes)

    def keeps(g, slot):
        at = pl.ds(pl.multiple_of(g * block, block), block)
        return (
            pltpu.make_async_copy(gate_keep.at[slot], gate_out.at[:, at], keep_sem.at[0, slot]),
            pltpu.make_async_copy(up_keep.at[slot], up_out.at[:, at], keep_sem.at[1, slot]),
        )

    def weights(g):
        at = pl.ds(pl.multiple_of(g * block, block), block)
        return (
            pltpu.make_async_copy(full_gate.at[:, at], gate_w, weight_sem.at[2]),
            pltpu.make_async_copy(full_up.at[:, at], up_w, weight_sem.at[3]),
            pltpu.make_async_copy(full_down.at[at, :], down_w, weight_sem.at[4]),
        )

    def climb(g):
        at = pl.ds(pl.multiple_of(g * block, block), block)
        slot = lax.rem(g, 2)

        @pl.when(g >= 2)
        def _():
            for keep in keeps(g - 2, slot):
                keep.wait()

        ready = weights(g)
        ready[0].wait()
        gate = dot(ffn[...], gate_w[...]) + dot(code_ffn[:, :rank], gu_out[0, :, at])
        gate_keep[slot] = low(gate)
        act = gelu_parts(gate)[0]
        ready[1].wait()
        up = dot(ffn[...], up_w[...]) + dot(code_ffn[:, rank:], gu_out[1, :, at])
        up_keep[slot] = low(up)
        hidden[...] = low(act * up)
        for keep in keeps(g, slot):
            keep.start()

    def descend(g):
        at = pl.ds(pl.multiple_of(g * block, block), block)
        weights(g)[2].wait()
        codes[...] += dot_t(hidden[...], down_in[:, at])
        total[...] += dot(hidden[...], down_w[...])

    def round_(g, carry):
        more = g + 1 < groups

        @pl.when(more)
        def _():
            relay(group(g + 1), 1, 1)

        @pl.when(g + 2 < groups)
        def _():
            begin(group(g + 2))

        spread(group(g))

        @pl.when(g >= 1)
        def _():
            descend(g - 1)

        @pl.when(more)
        def _():
            relay(group(g + 1), 2, 2)

        finish(group(g))
        for load in weights(g):
            load.start()

        @pl.when(more)
        def _():
            relay(group(g + 1), 3)

        @pl.when(g == 0)
        def _():
            for swap_ffn in swaps:
                swap_ffn.wait()
            pltpu.make_async_copy(ffn, ffn_out, ffn_sem).start()
            code_ffn[...] = low(dot_t(ffn[...], ffn_in[...]))

        climb(g)
        return carry

    lax.fori_loop(0, groups, round_, 0)
    descend(groups - 1)
    code_down[...] = low(codes[...])
    part[...] = low(total[...] + dot(code_down[...], down_out[...]))
    finish(small)
    for g in (groups - 2, groups - 1):
        for keep in keeps(g, g % 2):
            keep.wait()
    pltpu.make_async_copy(ffn, ffn_out, ffn_sem).wait()
    flush(first)
    flush(small)

    def flush_group(g, carry):
        flush(group(g))
        return carry

    lax.fori_loop(0, groups, flush_group, 0)


def fore(
    weights, attended, tokens, laurel_mid, out_in, out_out, ffn_in, gu_out, down_in, down_out, gains, shards
):
    count = attended.shape[0]
    width = tokens.shape[1]
    hidden = weights[4].shape[1]
    half = count // 2
    rank = out_in.shape[0]
    block = min(512, hidden)
    groups = hidden // block
    bf16, f32 = jnp.bfloat16, jnp.float32
    anywhere, vmem = pl.BlockSpec(memory_space=pl.ANY), pl.BlockSpec(memory_space=pltpu.VMEM)
    shape = jax.ShapeDtypeStruct
    return pl.pallas_call(
        functools.partial(fore_kernel, shards, block),
        out_shape=full_shapes(weights, FORE_AXES, shards)
        + [
            shape((count, hidden), bf16),
            shape((count, hidden), bf16),
            shape((count, width), bf16),
            shape((half, width), f32),
            shape((half, width), f32),
            shape((count, rank), bf16),
            shape((count, 2 * rank), bf16),
            shape((count, rank), bf16),
            shape((count, width), bf16),
        ],
        in_specs=[anywhere] * 7 + [vmem] * 13,
        out_specs=[anywhere] * 10 + [vmem] * 6,
        scratch_shapes=[
            *[pltpu.VMEM(w.shape, bf16) for w in weights],
            pltpu.VMEM((weights[0].shape[0], width), bf16),
            pltpu.VMEM((weights[1].shape[0], width), bf16),
            pltpu.VMEM((width, block), bf16),
            pltpu.VMEM((width, block), bf16),
            pltpu.VMEM((block, width), bf16),
            pltpu.VMEM((half, width), bf16),
            pltpu.VMEM((half, width), bf16),
            pltpu.VMEM((count, width), bf16),
            pltpu.VMEM((count, width), f32),
            pltpu.VMEM((count, rank), f32),
            pltpu.VMEM((count, block), bf16),
            pltpu.VMEM((2, count, block), bf16),
            pltpu.VMEM((2, count, block), bf16),
            pltpu.SemaphoreType.DMA((7,)),
            pltpu.SemaphoreType.DMA((7,)),
            pltpu.SemaphoreType.DMA((5,)),
            pltpu.SemaphoreType.DMA((2, 2)),
            pltpu.SemaphoreType.DMA,
            pltpu.SemaphoreType.DMA((3,)),
            pltpu.SemaphoreType.DMA((3,)),
        ]
        + mover_semaphores(4 + 3 * groups, shards),
        compiler_params=pltpu.CompilerParams(
            collective_id=1, has_side_effects=True, vmem_limit_bytes=60 * 2**20
        ),
    )(*weights, attended, tokens, laurel_mid, out_in, out_out, ffn_in, gu_out, down_in, down_out, *gains)


def share(packed):
    part = lax.psum_scatter(packed, "context", scatter_dimension=1, tiled=True)
    whole = lax.all_gather(low(part), ("shard", "context", "tensor"), axis=0, tiled=False)
    shards, contexts, tensors = (lax.axis_size(a) for a in ("shard", "context", "tensor"))
    whole = whole.reshape(shards, contexts, tensors, packed.shape[0], part.shape[1])
    return whole.transpose(2, 0, 3, 1, 4).reshape(tensors, shards, packed.shape[0], packed.shape[1])


def body(
    tokens,
    layer_input,
    segments,
    adapter_ids,
    cotangent,
    w_query,
    w_key,
    w_value,
    w_output,
    w_gate,
    w_up,
    w_down,
    laurel_left,
    laurel_right,
    input_gate,
    input_proj,
    gain_in,
    gain_attn,
    gain_laurel,
    gain_pre,
    gain_post,
    gain_layer,
    gain_query,
    gain_key,
    adapt_attn_in,
    adapt_query_out,
    adapt_kv_out,
    adapt_out_in,
    adapt_out_out,
    adapt_ffn_in,
    adapt_gu_out,
    adapt_down_in,
    adapt_down_out,
):
    seq_count, count, width = tokens.shape
    assert seq_count == 1 and lax.axis_size("tensor") == 2 and lax.axis_size("context") == 4
    half = count // 2
    head_size = gain_query.shape[0]
    rank = adapt_query_out.shape[1]
    heads = adapt_query_out.shape[2] // head_size
    kv_heads = adapt_kv_out.shape[3] // head_size
    group = heads // kv_heads
    side = lax.axis_index("tensor")
    place = lax.axis_index("context")
    shards = lax.axis_size("shard")

    full_query, full_key, full_value, full_left = gather(
        (w_query, w_key, w_value, laurel_left.T), (0, 0, 0, 1), shards
    )
    hidden_here = w_gate.shape[1]
    chosen = adapter_ids[0]

    def pick(table):
        return lax.dynamic_index_in_dim(table, chosen, 0, keepdims=False)

    pick_attn_in, pick_query_out, pick_kv_out = pick(adapt_attn_in), pick(adapt_query_out), pick(adapt_kv_out)
    pick_out_in, pick_out_out, pick_ffn_in = pick(adapt_out_in), pick(adapt_out_out), pick(adapt_ffn_in)
    pick_gu_out, pick_down_in, pick_down_out = pick(adapt_gu_out), pick(adapt_down_in), pick(adapt_down_out)

    def own_half(array):
        return lax.dynamic_slice_in_dim(array, side * half, half, 0)

    def other_half(array):
        return lax.dynamic_slice_in_dim(array, (1 - side) * half, half, 0)

    def in_order(own, other):
        return jnp.where(
            side == 0, jnp.concatenate([own, other], axis=0), jnp.concatenate([other, own], axis=0)
        )

    start_pos = place * count
    seg_all = segments[0]
    seg_query = lax.dynamic_slice_in_dim(seg_all, start_pos, count, 0)
    before = jnp.sum((seg_all[None, :] < seg_query[:, None]).astype(jnp.int32), axis=1)
    own_pos = start_pos + jnp.arange(count, dtype=jnp.int32) - before
    cosine, sine_table = rope_tables(own_pos, head_size)
    cosine = cosine[:, None, :]
    sine_table = sine_table[:, None, :]
    tokens_f = wide(tokens[0])
    normed_b = low(rms_norm(tokens_f, gain_in))
    tokens_h = wide(own_half(tokens[0]))
    normed_h, normed_back = jax.vjp(lambda v: rms_norm(v, gain_in), tokens_h)
    code_attn = matmul(normed_b, pick_attn_in)
    query_lin = matmul(normed_b, full_query) + matmul(code_attn[:, :rank], pick_query_out)
    key_lin = matmul(normed_b, full_key) + matmul(code_attn[:, rank : 2 * rank], pick_kv_out[0])
    value_lin = matmul(normed_b, full_value) + matmul(code_attn[:, 2 * rank :], pick_kv_out[1])

    def prepare(query_in, key_in, value_in):
        query_rot = rotate_half(
            rms_norm(query_in.reshape(count, heads, head_size), gain_query), cosine, sine_table
        )
        key_rot = rotate_half(
            rms_norm(key_in.reshape(count, kv_heads, head_size), gain_key), cosine, sine_table
        )
        value_nrm = rms_norm(value_in.reshape(count, kv_heads, head_size), 1.0)
        return (query_rot, key_rot, value_nrm)

    (query_rot, key_rot, value_nrm), prepare_back = jax.vjp(prepare, query_lin, key_lin, value_lin)
    query_b = low(query_rot).reshape(count, kv_heads, group, head_size)
    kv_own = low(jnp.stack([key_rot, value_nrm]))
    kv_prior = shifted(kv_own, "context", 1)
    kv_all = jnp.concatenate([kv_prior, kv_own], axis=1)
    query_pos = start_pos + jnp.arange(count, dtype=jnp.int32)
    key_pos = start_pos - count + jnp.arange(2 * count, dtype=jnp.int32)
    seg_prior = lax.dynamic_slice_in_dim(seg_all, jnp.maximum(start_pos - count, 0), count, 0)
    seg_keys = jnp.concatenate([seg_prior, seg_query], axis=0)
    distance = query_pos[:, None] - key_pos[None, :]
    window_ok = (distance >= 0) & (distance < WINDOW) & (key_pos >= 0)[None, :]
    allowed = (seg_query[:, None] == seg_keys[None, :]) & window_ok
    allowed = allowed[None, None]
    score_scale = 1.0 / math.sqrt(head_size)

    def masked_scores():
        raw_scores = (
            jnp.einsum("lkgd,mkd->kglm", query_b, kv_all[0], preferred_element_type=jnp.float32)
            * score_scale
        )
        return jnp.where(allowed, raw_scores, -1e30)

    scores = masked_scores()
    row_max = jnp.max(scores, axis=-1, keepdims=True)
    exponent = jnp.exp(scores - row_max)
    row_total = jnp.sum(exponent, axis=-1, keepdims=True)
    log_total = row_max + jnp.log(row_total)
    attn_probs = low(exponent / row_total)
    attended = jnp.einsum("kglm,mkd->lkgd", attn_probs, kv_all[1], preferred_element_type=jnp.float32)
    attended_b = low(attended.reshape(count, heads * head_size))
    laurel_mid = low(matmul_t(normed_h, full_left))
    (
        full_output, full_right, full_layer_gate, full_layer_proj, full_gate, full_up, full_down,
        gate_b, up_b, ffn_b, attn_proj, combined, code_out, code_ffn, code_down, down_part,
    ) = fore(
        (w_output, laurel_right, input_gate, input_proj, w_gate, w_up, w_down),
        attended_b, own_half(tokens[0]), laurel_mid,
        pick_out_in.T, pick_out_out, pick_ffn_in.T, pick_gu_out, pick_down_in.T, pick_down_out,
        (gain_in[None], gain_attn[None], gain_laurel[None], gain_pre[None]), shards,
    )
    quarter = half // 2
    bf16, f32 = jnp.bfloat16, jnp.float32
    per_layer_h, cotangent_h = own_half(layer_input[0]), own_half(cotangent[0])
    crowned = []
    for g in range(2):
        theirs = swap(down_part[g * half + quarter : (g + 1) * half])
        output_g, grad_down_g, grad_after_g = rowwise(
            crown_kernel, g, quarter,
            [(down_part, 2 * g), (theirs, 0), (combined, None), (per_layer_h, None), (cotangent_h, None)],
            [full_layer_gate, full_layer_proj, gain_post[None], gain_layer[None]],
            [(width, bf16), (width, bf16), (width, f32)],
        )
        crowned.append((output_g, grad_down_g, grad_after_g, swap(grad_down_g)))
    parted = []
    for g in range(2):
        grad_down_b = jnp.concatenate([crowned[g][1], crowned[g][3]], axis=0)
        parted.append(
            ffn_back(
                g, grad_down_b, gate_b, up_b, code_ffn, code_down, ffn_b, full_down, full_gate, full_up,
                pick_down_in.T, pick_down_out, pick_gu_out, pick_ffn_in.T,
            )
        )
    term_gate_out, term_up_out, term_down_in, term_ffn_in, term_down_out = (
        parted[0][i] + parted[1][i] for i in range(1, 6)
    )
    mark = jnp.where(
        (lax.broadcasted_iota(jnp.int32, (rank, 512), 1) == chosen) & (place == 0), 1.0, 0.0
    )
    early = share(
        jnp.concatenate(
            [term_gate_out, term_up_out, term_down_in, term_ffn_in[:rank], term_ffn_in[rank:], term_down_out, mark],
            axis=1,
        )
    )
    turned_back = []
    for g in range(2):
        part = parted[g][0]
        turned_back.append(
            rowwise(
                comb_back_kernel, g, quarter,
                [
                    (part, 0), (swap(part[quarter:]), 0), (crowned[g][2], 0), (combined, None),
                    (attn_proj, None), (laurel_mid, None),
                ],
                [full_left, full_right, gain_pre[None], gain_attn[None], gain_laurel[None]],
                [(width, bf16), (width, f32), (width, f32)],
            )
        )
    grad_inputs = jnp.concatenate([turned_back[0][1], turned_back[1][1]], axis=0)
    grad_normed = jnp.concatenate([turned_back[0][2], turned_back[1][2]], axis=0)
    grad_attn_b = in_order(
        jnp.concatenate([turned_back[0][0], turned_back[1][0]], axis=0),
        jnp.concatenate([swap(turned_back[0][0]), swap(turned_back[1][0])], axis=0),
    )
    output_own = jnp.concatenate([crowned[0][0], crowned[1][0]], axis=0)
    layer_output = in_order(output_own, swap(output_own))
    code_out_back = matmul_t(grad_attn_b, pick_out_out)
    term_out_out = outer(code_out, grad_attn_b)
    term_out_in = outer(code_out_back, attended_b)
    grad_attended = low(matmul_t(grad_attn_b, full_output) + matmul_t(code_out_back, pick_out_in))
    grad_heads = grad_attended.reshape(count, kv_heads, group, head_size)
    recomputed = jnp.exp(masked_scores() - log_total)
    grad_probs = jnp.einsum("lkgd,mkd->kglm", grad_heads, kv_all[1], preferred_element_type=jnp.float32)
    grad_scores = low(
        recomputed * (grad_probs - jnp.sum(recomputed * grad_probs, axis=-1, keepdims=True))
    )
    grad_query = (
        jnp.einsum("kglm,mkd->lkgd", grad_scores, kv_all[0], preferred_element_type=jnp.float32)
        * score_scale
    )
    grad_keys = (
        jnp.einsum("kglm,lkgd->mkd", grad_scores, query_b, preferred_element_type=jnp.float32)
        * score_scale
    )
    grad_values = jnp.einsum(
        "kglm,lkgd->mkd", low(recomputed), grad_heads, preferred_element_type=jnp.float32
    )
    grad_kv = jnp.stack([grad_keys, grad_values])
    grad_kv_later = wide(shifted(low(grad_kv[:, :count]), "context", -1))
    grad_kv_own = grad_kv[:, count:] + grad_kv_later
    grad_qlin, grad_klin, grad_vlin = prepare_back(
        (grad_query.reshape(count, heads, head_size), grad_kv_own[0], grad_kv_own[1])
    )
    grad_qlin_b = low(grad_qlin)
    early, grad_qlin_b = lax.optimization_barrier((early, grad_qlin_b))
    grad_klin_b = low(grad_klin)
    grad_vlin_b = low(grad_vlin)
    code_attn_back = jnp.concatenate(
        [
            matmul_t(grad_qlin_b, pick_query_out),
            matmul_t(grad_klin_b, pick_kv_out[0]),
            matmul_t(grad_vlin_b, pick_kv_out[1]),
        ],
        axis=1,
    )
    term_query_out = outer(code_attn[:, :rank], grad_qlin_b)
    term_key_out = outer(code_attn[:, rank : 2 * rank], grad_klin_b)
    term_value_out = outer(code_attn[:, 2 * rank :], grad_vlin_b)
    term_attn_in = outer(code_attn_back, normed_b)
    late = share(
        jnp.concatenate(
            [
                term_out_in, term_out_out, term_query_out, term_key_out, term_value_out,
                term_attn_in[:rank], term_attn_in[rank : 2 * rank], term_attn_in[2 * rank :],
            ],
            axis=1,
        )
    )
    grad_normed_part = low(
        matmul_t(grad_qlin_b, full_query)
        + matmul_t(grad_klin_b, full_key)
        + matmul_t(grad_vlin_b, full_value)
        + matmul_t(code_attn_back, pick_attn_in)
    )
    grad_normed = grad_normed + wide(own_half(grad_normed_part)) + wide(swap(other_half(grad_normed_part)))
    grad_own = low(grad_inputs + normed_back(grad_normed)[0])
    input_grad = in_order(grad_own, swap(grad_own))

    at = 0

    def take(packed, columns):
        nonlocal at
        at += columns
        return wide(packed[..., at - columns : at])

    def joined(packed, columns):
        both = take(packed, columns)
        return jnp.concatenate([both[0], both[1]], axis=-1)

    def added(packed, columns):
        both = take(packed, columns)
        return both[0] + both[1]

    gate_out, up_out, down_in = (joined(early, hidden_here) for _ in range(3))
    ffn_in = [added(early, width) for _ in range(2)]
    down_out = added(early, width)
    adapters = adapt_attn_in.shape[0]
    marks = wide(early[0, :, 0, at : at + adapters])
    at = 0
    out_in = joined(late, heads * head_size)
    out_out = added(late, width)
    query_out = joined(late, heads * head_size)
    key_out, value_out = (joined(late, kv_heads * head_size) for _ in range(2))
    attn_in = [added(late, width) for _ in range(3)]

    def tables(terms):
        return sum(
            marks[s].reshape((adapters,) + (1,) * (terms.ndim - 1)) * terms[s][None] for s in range(shards)
        )

    def turned(terms):
        return tables(terms).transpose(0, 2, 1)

    return (
        layer_output[None],
        input_grad[None],
        turned(jnp.concatenate(attn_in, axis=1)),
        tables(query_out),
        tables(jnp.stack([key_out, value_out], axis=1)),
        turned(out_in),
        tables(out_out),
        turned(jnp.concatenate(ffn_in, axis=1)),
        tables(jnp.stack([gate_out, up_out], axis=1)),
        turned(down_in),
        tables(down_out),
    )


def solution(mesh):
    in_specs = (
        P("shard", "context", None),
        P("shard", "context", None),
        P("shard", None),
        P("shard"),
        P("shard", "context", None),
        P("shard", "tensor"),
        P("shard", "tensor"),
        P("shard", "tensor"),
        P("tensor", "shard"),
        P("shard", "tensor"),
        P("shard", "tensor"),
        P("tensor", "shard"),
        P("shard", None),
        P(None, "shard"),
        P("shard", None),
        P(None, "shard"),
        P(),
        P(),
        P(),
        P(),
        P(),
        P(),
        P(),
        P(),
        P(),
        P(None, None, "tensor"),
        P(None, None, None, "tensor"),
        P(None, "tensor", None),
        P(),
        P(),
        P(None, None, None, "tensor"),
        P(None, "tensor", None),
        P(),
    )
    out_specs = (
        P("shard", "context", None),
        P("shard", "context", None),
        P(),
        P(),
        P(),
        P(),
        P(),
        P(),
        P(),
        P(),
        P(),
    )
    return jax.shard_map(body, mesh=mesh, in_specs=in_specs, out_specs=out_specs, check_vma=False)
```

time: 951 us -> 773 us (0.81)
  matrix products: 215 us -> 66.9 us
  waiting for transfers between devices: 247 us -> 120 us
  Pallas kernels: 288 us -> 404 us
  other arithmetic: 92.9 us -> 70.6 us
    pallas_call x1 -> x8, Pallas kernels: 288 us -> 404 us  [the longest x1 290 us: fore(): pl.pallas_call(functools.partial(fore_kernel, shards, block), out_shape=f...]
    ppermute x9 -> x11, waiting for transfers between devices: 162 us -> 86.6 us  [swap(): return lax.ppermute(array, 'tensor', [(0, 1), (1, 0)])]
    dot_general x21 -> x7, matrix products: 87.2 us -> 13.7 us  [matmul(): jnp.dot(low(left_op), low(right_op), preferred_element_type=jnp.float32)]
    dot_general x20 -> x11, matrix products: 98.8 us -> 28.1 us  [matmul_t(): lax.dot_general(low(left_op), low(right_op), (((1,), (1,)), ((), ())), pr...]
    reduce_scatter x2, waiting for transfers between devices: 31.9 us -> 4.35 us  [share(): part = lax.psum_scatter(packed, 'context', scatter_dimension=1, tiled=True)]
    all_gather x2, waiting for transfers between devices: 53.6 us -> 28.6 us  [share(): lax.all_gather(low(part), ('shard', 'context', 'tensor'), axis=0, tiled=F...]
    convert_element_type x9 -> x6, other arithmetic: 25 us -> 7.35 us  [low(): return values.astype(jnp.bfloat16)]
    unnamed x327 -> x258, local copies, waits for them, and re-layouts: 22.1 us -> 22.8 us
  transfers between devices with their start and end apart: 15 -> 17, of which waited for: 13 -> 12; matrix products, arithmetic and copies ran while one was open for 9% -> 15% of each run, Pallas kernels for 0% -> 6%
where the time goes in v2:
time: 773 us; the launch traced here: 767 us
  Pallas kernels  404 us (52%)
  waiting for transfers between devices  120 us (16%)
  other arithmetic  70.6 us (9%)
  local copies, waits for them, and re-layouts  68.9 us (9%)
  matrix products  66.9 us (9%)
  starting transfers between devices  19.9 us (3%)
  between operations  16.8 us (2%)
    pallas_call x1, Pallas kernels, fore(): pl.pallas_call(functools.partial(fore_kernel, shards, block), out_shape=f...  290 us
    ppermute x11, waiting for transfers between devices, swap(): return lax.ppermute(array, 'tensor', [(0, 1), (1, 0)])  86.6 us
    pallas_call x2, Pallas kernels, ffn_back(): pl.pallas_call(ffn_back_kernel, grid=(hidden // block,), in_specs=[whole(...  52.7 us
    pallas_call x1, Pallas kernels, gather(): pl.pallas_call(functools.partial(gather_kernel, axes, shards), out_shape=...  44.3 us
    all_gather x2, waiting for transfers between devices, share(): lax.all_gather(low(part), ('shard', 'context', 'tensor'), axis=0, tiled=F...  28.6 us
    dot_general x11, matrix products, matmul_t(): lax.dot_general(low(left_op), low(right_op), (((1,), (1,)), ((), ())), pr...  28.1 us
    unnamed x258, local copies, waits for them, and re-layouts  22.8 us
    add x7, other arithmetic, tables(): sum((marks[s].reshape((adapters,) + (1,) * (terms.ndim - 1)) * terms[s][N...  18.1 us
  transfers between devices with their start and end apart: 17, of which 12 were waited for; matrix products, arithmetic and copies ran while one was open for 15% of the time, Pallas kernels for 6%

profile of v2, /device:TPU:0, one launch (start us, length us, event | category | flops | bytes accessed | tf_op | source)
XLA Modules:
  0.0 767.1 jit_solution(9323132481121158114)
XLA Ops:
  10.9 2.5 fusion.46
  15.6 44.3 %shard_map.392 = (bf16[2048,1024]{1,0:T(8,128)(2,1)S(1)}, bf16[2048,256]{1,0:T(8,128)(2,1)S(1)}, bf16[2048,256]{1,0:T(8,128)(2,1)S(1)}, bf16[64,2048]{1,0:T(8,128)(2,1)S(1)}) custom-call(bf16[512,1024]{1,0:T(8,128)(2,1)S(1)} %copy-done.18, bf16[512,256]{1,0:T(8,128)(2,1)S(1)} %copy-done.36, bf16[512,256]{1,0:T(8,128)(2,1)S(1)} %copy-done.37, ...), custom_call_target="tpu_custom_call" | custom-call | tf_op jit(solution)/shard_map/pallas_call | solution.py:480
  65.1 3.7 collective-permute-start
  75.7 4.7 fusion.162
  80.5 2.5 convolution_add_fusion
  83.0 3.2 reshape.690
  86.2 2.9 multiply_reduce_fusion
  106.3 290.2 %shard_map.393 = (bf16[1024,2048]{1,0:T(8,128)(2,1)}, bf16[64,2048]{1,0:T(8,128)(2,1)}, bf16[2048,256]{1,0:T(8,128)(2,1)}, bf16[256,2048]{1,0:T(8,128)(2,1)}, bf...) custom-call(bf16[1024,512]{1,0:T(8,128)(2,1)} %w_output.1, ...), custom_call_target="tpu_custom_call" | custom-call | tf_op jit(solution)/shard_map/pallas_call | solution.py:718
  396.6 2.3 fusion.166
  401.0 12.5 %collective-permute-done.1.theirs = bf16[128,2048]{1,0:T(8,128)(2,1)S(1)} collective-permute-done((bf16[128,2048]{1,0:T(8,128)(2,1)S(1)}, bf16[128,2048]{1,0:T(8,128)(2,1)S(1)}, u32[]{:S(2)}, u32[]{:S(2)}) %collective-permute-start.1) | collective-permute-done | bytes 524320 | tf_op jit(solution)/shard_map/ppermute | solution.py:27
  413.6 5.0 shard_map.394
  421.8 3.1 collective-permute-done.2.theirs
  425.0 4.3 shard_map.395
  432.5 3.7 collective-permute-done.4
  437.5 26.2 %shard_map.396 = (bf16[256,2048]{1,0:T(8,128)(2,1)S(1)}, f32[16,4096]{1,0:T(8,128)S(1)}, f32[16,4096]{1,0:T(8,128)S(1)}, f32[16,4096]{1,0:T(8,128)S(1)}, f32[32,2048]{1,0:T(8,128)S(1)}, /*index=5*/f32[16,2048]{1,0:T(8,128)S(1)}) custom-call(bf16[256,2048]{1,0:T(8,128)(2,1)S(1)} %pad_maximum_fusion.5.grad, bf16[512,4096]{1,0:T(8,128)(2,1)} %get-tuple-element.68.gate, ...), custom_call_target="tpu_custom_call" | custom-call | flops 12884901888 | bytes 50331648 | tf_op jit(solution)/shard_map/pallas_call | solution.py:154
  463.8 26.6 %shard_map.398 = (bf16[256,2048]{1,0:T(8,128)(2,1)S(1)}, f32[16,4096]{1,0:T(8,128)S(1)}, f32[16,4096]{1,0:T(8,128)S(1)}, f32[16,4096]{1,0:T(8,128)S(1)}, f32[32,2048]{1,0:T(8,128)S(1)}, /*index=5*/f32[16,2048]{1,0:T(8,128)S(1)}) custom-call(bf16[256,2048]{1,0:T(8,128)(2,1)S(1)} %pad_maximum_fusion.6.grad, bf16[512,4096]{1,0:T(8,128)(2,1)} %get-tuple-element.68.gate, ...), custom_call_target="tpu_custom_call" | custom-call | flops 12884901888 | bytes 50331648 | tf_op jit(solution)/shard_map/pallas_call | solution.py:154
  500.9 33.1 %collective-permute-done.7.theirs = bf16[128,2048]{1,0:T(8,128)(2,1)S(1)} collective-permute-done((bf16[128,2048]{1,0:T(8,128)(2,1)S(1)}, bf16[128,2048]{1,0:T(8,128)(2,1)S(1)}, u32[]{:S(2)}, u32[]{:S(2)}) %collective-permute-start.7) | collective-permute-done | bytes 524320 | tf_op jit(solution)/shard_map/ppermute | solution.py:27
  538.0 3.6 shard_map.399
  545.0 3.8 shard_map.397
  551.2 3.2 maximum_select_fusion
  557.7 7.7 %collective-permute-done.8 = bf16[128,2048]{1,0:T(8,128)(2,1)S(1)} collective-permute-done((bf16[128,2048]{1,0:T(8,128)(2,1)}, bf16[128,2048]{1,0:T(8,128)(2,1)S(1)}, u32[]{:S(2)}, u32[]{:S(2)}) %collective-permute-start.8) | collective-permute-done | bytes 524320 | tf_op jit(solution)/shard_map/ppermute | solution.py:27
  565.4 2.5 maximum_select_fusion.1
  568.7 2.3 fusion.126
  571.0 3.4 add_convert_fusion.1
  575.9 5.7 fusion
  582.4 2.4 fusion.15
  592.3 3.9 fusion.45
  596.2 4.9 fusion.41
  609.3 2.9 fusion.169
  612.1 2.8 fusion.170
  614.9 8.2 %all-gather.5.cloned.1.call-done = bf16[512,4736]{1,0:T(8,128)(2,1)} async-done(((bf16[16,4736]{1,0:T(8,128)(2,1)}), bf16[512,4736]{1,0:T(8,128)(2,1)}) %all-gather.5.cloned.1.call-update) | async-done | bytes 4849680 | tf_op jit(solution)/shard_map/all_gather | solution.py:766
  623.1 7.1 copy.148
  630.2 8.0 %reshape.693 = bf16[2,4,16,18944]{3,2,1,0:T(8,128)(2,1)} reshape(bf16[2,4,16,4,4736]{4,3,2,1,0:T(4,128)(2,1)} %copy.148) | data formatting | bytes 9699328 | tf_op jit(solution)/shard_map/reshape | solution.py:769
  638.1 6.7 fusion.168
  646.0 2.9 slice_convert_fusion
  654.3 5.5 add_convert_fusion
  666.6 4.7 multiply_add_fusion
  671.3 3.0 slice_convert_fusion.7
  675.7 4.4 reduce-scatter.5.cloned.1.call-done
  681.6 4.6 multiply_add_fusion.1
  690.6 2.4 fusion.21
  696.5 24.0 %collective-permute-done.12 = bf16[256,2048]{1,0:T(8,128)(2,1)S(1)} collective-permute-done((bf16[256,2048]{1,0:T(8,128)(2,1)S(1)}, bf16[256,2048]{1,0:T(8,128)(2,1)S(1)}, u32[]{:S(2)}, u32[]{:S(2)}) %collective-permute-start.12) | collective-permute-done | bytes 1048608 | tf_op jit(solution)/shard_map/ppermute | solution.py:27
  720.5 2.3 maximum_select_fusion.2
  722.8 20.5 %all-gather.7.cloned.1.call-done = bf16[512,2688]{1,0:T(8,128)(2,1)} async-done(((bf16[16,2688]{1,0:T(8,128)(2,1)}), bf16[512,2688]{1,0:T(8,128)(2,1)}) %all-gather.7.cloned.1.call-update) | async-done | bytes 2752528 | tf_op jit(solution)/shard_map/all_gather | solution.py:766
  743.3 4.7 copy.179
  748.0 3.4 reshape.700
  755.3 2.5 multiply_add_fusion.2
  757.8 2.1 multiply_add_fusion.4
  (410 shorter events, 113.7 us)
Async XLA Ops:
  7.2 393.1 %copy-start = (bf16[1,512,2048]{2,1,0:T(8,128)(2,1)S(1)}, bf16[1,512,2048]{2,1,0:T(8,128)(2,1)}, u32[]{:S(2)}) copy-start(bf16[1,512,2048]{2,1,0:T(8,128)(2,1)} %param.37) | copy-start | bytes 6291460
  7.2 547.2 %reduce-scatter.3.cloned.1.call-start = ((), (), s32[]{:S(2)}) async-start(), calls=%async_computation.2 | async-start | bytes 1515520 | tf_op jit(solution)/shard_map/reduce_scatter | solution.py:765
  7.3 61.6 %copy-start.118 = (f32[128]{0:T(128)}, f32[128]{0:T(128)S(1)}, u32[]{:S(2)}) copy-start(f32[128]{0:T(128)S(1)} %multiply_exponential_fusion) | copy-start | bytes 1540
  10.2 65.4 %copy-start.122 = (f32[512]{0:T(512)}, f32[512]{0:T(512)S(1)}, u32[]{:S(2)}) copy-start(f32[512]{0:T(512)S(1)} %add_rsqrt_fusion) | copy-start | bytes 6148
  10.9 58.0 %copy-start.97 = (f32[512]{0:T(512)}, f32[512]{0:T(512)S(1)}, u32[]{:S(2)}) copy-start(f32[512]{0:T(512)S(1)} %subtract_convert_fusion.1) | copy-start | bytes 6148
  13.5 67.0 %copy-start.87 = (bf16[512,48]{0,1:T(8,128)(2,1)}, bf16[512,48]{0,1:T(8,128)(2,1)S(1)}, u32[]{:S(2)}) copy-start(bf16[512,48]{0,1:T(8,128)(2,1)S(1)} %fusion.46) | copy-start | bytes 147460
  13.5 46.5 %copy-start.60 = (bf16[1,512,2048]{2,1,0:T(8,128)(2,1)S(1)}, bf16[1,512,2048]{2,1,0:T(8,128)(2,1)}, u32[]{:S(2)}) copy-start(bf16[1,512,2048]{2,1,0:T(8,128)(2,1)} %param.33) | copy-start | bytes 6291460
  62.7 9.6 %copy-start.78 = (bf16[1,512,1,256]{1,3,2,0:T(8,128)(2,1)}, bf16[1,512,1,256]{1,3,2,0:T(8,128)(2,1)S(1)}, u32[]{:S(2)}) copy-start(bf16[1,512,1,256]{1,3,2,0:T(8,128)(2,1)S(1)} %fusion.92) | copy-start | bytes 786436
  64.2 9.6 %copy-start.80 = (bf16[1,512,1,256]{1,3,2,0:T(8,128)(2,1)}, bf16[1,512,1,256]{1,3,2,0:T(8,128)(2,1)S(1)}, u32[]{:S(2)}) copy-start(bf16[1,512,1,256]{1,3,2,0:T(8,128)(2,1)S(1)} %maximum_bitcast_fusion.2) | copy-start | bytes 786436
  65.1 33.5 %collective-permute-start = (bf16[2,512,1,256]{1,3,2,0:T(8,128)(2,1)}, bf16[2,512,1,256]{1,3,2,0:T(8,128)(2,1)}, u32[]{:S(2)}, u32[]{:S(2)}) collective-permute-start(bf16[2,512,1,256]{1,3,2,0:T(8,128)(2,1)} %pad_maximum_fusion.10), channel_id=1, source_target_pairs={{0,2},{2,4},{4,6},{1,3},{3,5},{5,7},{8,10},{10,12},{12,14},{9,11},... | collective-permute-start | bytes 1572872 | tf_op jit(solution)/shard_map/ppermute | solution.py:23
  75.5 16.4 %copy-start.51 = (bf16[256,2048]{1,0:T(8,128)(2,1)}, bf16[256,2048]{1,0:T(8,128)(2,1)S(1)}, u32[]{:S(2)}) copy-start(bf16[256,2048]{1,0:T(8,128)(2,1)S(1)} %get-tuple-element.104.tokens) | copy-start | bytes 3145732
  75.5 16.4 %copy-start.120 = (f32[256]{0:T(256)}, f32[256]{0:T(256)S(1)}, u32[]{:S(2)}) copy-start(f32[256]{0:T(256)S(1)} %fusion.156) | copy-start | bytes 3076
  94.4 7.2 copy-start.85
  94.4 7.2 copy-start.86
  105.0 291.5 %copy-start.67 = (bf16[256,4,512]{2,0,1:T(8,128)(2,1)}, bf16[256,4,512]{2,0,1:T(8,128)(2,1)S(1)}, u32[]{:S(2)}) copy-start(bf16[256,4,512]{2,0,1:T(8,128)(2,1)S(1)} %fusion.38) | copy-start | bytes 3145732
  396.5 17.1 %copy-start.4 = (bf16[2048,256]{1,0:T(8,128)(2,1)S(1)}, bf16[2048,256]{1,0:T(8,128)(2,1)}, u32[]{:S(2)}) copy-start(bf16[2048,256]{1,0:T(8,128)(2,1)} %get-tuple-element.63.input_gate) | copy-start | bytes 3145732
  396.5 17.0 %copy-start.6 = (bf16[256,2048]{1,0:T(8,128)(2,1)S(1)}, bf16[256,2048]{1,0:T(8,128)(2,1)}, u32[]{:S(2)}) copy-start(bf16[256,2048]{1,0:T(8,128)(2,1)} %get-tuple-element.64.input_proj) | copy-start | bytes 3145732
  396.5 17.0 %copy-start.42 = (f32[2048]{0:T(1024)S(1)}, f32[2048]{0:T(1024)}, u32[]{:S(2)}) copy-start(f32[2048]{0:T(1024)} %param.53) | copy-start | bytes 24580
  396.5 17.0 %copy-start.43 = (f32[2048]{0:T(1024)S(1)}, f32[2048]{0:T(1024)}, u32[]{:S(2)}) copy-start(f32[2048]{0:T(1024)} %param.54) | copy-start | bytes 24580
  398.8 14.8 %collective-permute-start.1 = (bf16[128,2048]{1,0:T(8,128)(2,1)S(1)}, bf16[128,2048]{1,0:T(8,128)(2,1)S(1)}, u32[]{:S(2)}, u32[]{:S(2)}) collective-permute-start(bf16[128,2048]{1,0:T(8,128)(2,1)S(1)} %get-tuple-element.137), channel_id=1, source_target_pairs={{0,1},{1,0},{2,3},{3,2},{4,5},{5,4},{6,7},{7,6},{8,9},{9,8},{10,11... | collective-permute-start | bytes 1572872 | tf_op jit(solution)/shard_map/ppermute | solution.py:27
  400.4 24.5 %collective-permute-start.2 = (bf16[128,2048]{1,0:T(8,128)(2,1)}, bf16[128,2048]{1,0:T(8,128)(2,1)}, u32[]{:S(2)}, u32[]{:S(2)}) collective-permute-start(bf16[128,2048]{1,0:T(8,128)(2,1)} %get-tuple-element.138), channel_id=1, source_target_pairs={{0,1},{1,0},{2,3},{3,2},{4,5},{5,4},{6,7},{7,6},{8,9},{9,8},{10,11... | collective-permute-start | bytes 1572872 | tf_op jit(solution)/shard_map/ppermute | solution.py:27
  413.6 11.3 %copy-start.5 = (bf16[2048,256]{1,0:T(8,128)(2,1)S(1)}, bf16[2048,256]{1,0:T(8,128)(2,1)}, u32[]{:S(2)}) copy-start(bf16[2048,256]{1,0:T(8,128)(2,1)} %get-tuple-element.63.input_gate) | copy-start | bytes 3145732
  413.6 11.3 %copy-start.7 = (bf16[256,2048]{1,0:T(8,128)(2,1)S(1)}, bf16[256,2048]{1,0:T(8,128)(2,1)}, u32[]{:S(2)}) copy-start(bf16[256,2048]{1,0:T(8,128)(2,1)} %get-tuple-element.64.input_proj) | copy-start | bytes 3145732
  420.3 15.8 %collective-permute-start.4 = (bf16[128,2048]{1,0:T(8,128)(2,1)}, bf16[128,2048]{1,0:T(8,128)(2,1)}, u32[]{:S(2)}, u32[]{:S(2)}) collective-permute-start(bf16[128,2048]{1,0:T(8,128)(2,1)} %get-tuple-element.67), channel_id=1, source_target_pairs={{0,1},{1,0},{2,3},{3,2},{4,5},{5,4},{6,7},{7,6},{8,9},{9,8},{10,11... | collective-permute-start | bytes 1572872 | tf_op jit(solution)/shard_map/ppermute | solution.py:27
  424.9 12.5 %copy-start.3 = (bf16[2,16,4096]{2,1,0:T(8,128)(2,1)S(1)}, bf16[2,16,4096]{2,1,0:T(8,128)(2,1)}, u32[]{:S(2)}) copy-start(bf16[2,16,4096]{2,1,0:T(8,128)(2,1)} %dynamic-slice_bitcast_fusion.2.gu_out) | copy-start | bytes 786436
  424.9 12.5 %copy-start.8 = (bf16[32,2048]{1,0:T(8,128)(2,1)S(1)}, bf16[32,2048]{1,0:T(8,128)(2,1)}, u32[]{:S(2)}) copy-start(bf16[32,2048]{1,0:T(8,128)(2,1)} %dynamic-slice_bitcast_fusion.5.ffn_in) | copy-start | bytes 393220
  424.9 12.6 %copy-start.9 = (bf16[16,4096]{1,0:T(8,128)(2,1)S(1)}, bf16[16,4096]{1,0:T(8,128)(2,1)}, u32[]{:S(2)}) copy-start(bf16[16,4096]{1,0:T(8,128)(2,1)} %dynamic-slice_bitcast_fusion.4.down_in) | copy-start | bytes 393220
  424.9 12.6 %copy-start.16 = (bf16[16,2048]{1,0:T(8,128)(2,1)S(1)}, bf16[16,2048]{1,0:T(8,128)(2,1)}, u32[]{:S(2)}) copy-start(bf16[16,2048]{1,0:T(8,128)(2,1)} %get-tuple-element.198.down_out) | copy-start | bytes 196612
  424.9 12.6 %copy-start.32 = (bf16[512,32]{1,0:T(8,128)(2,1)S(1)}, bf16[512,32]{1,0:T(8,128)(2,1)}, u32[]{:S(2)}) copy-start(bf16[512,32]{1,0:T(8,128)(2,1)} %get-tuple-element.70.codes) | copy-start | bytes 98308
  424.9 12.6 %copy-start.33 = (bf16[512,16]{1,0:T(8,128)(2,1)S(1)}, bf16[512,16]{1,0:T(8,128)(2,1)}, u32[]{:S(2)}) copy-start(bf16[512,16]{1,0:T(8,128)(2,1)} %get-tuple-element.71.code_down) | copy-start | bytes 49156
  431.0 32.7 %collective-permute-start.6 = (bf16[128,2048]{1,0:T(8,128)(2,1)S(1)}, bf16[128,2048]{1,0:T(8,128)(2,1)S(1)}, u32[]{:S(2)}, u32[]{:S(2)}) collective-permute-start(bf16[128,2048]{1,0:T(8,128)(2,1)S(1)} %get-tuple-element.81), channel_id=1, source_target_pairs={{0,1},{1,0},{2,3},{3,2},{4,5},{5,4},{6,7},{7,6},{8,9},{9,8},{10,11... | collective-permute-start | bytes 1572872 | tf_op jit(solution)/shard_map/ppermute | solution.py:27
  495.3 127.8 %all-gather.5.cloned.1.call-start = ((), (), s32[]{:S(2)}) async-start(), calls=%async_computation.4 | async-start | bytes 5001216 | tf_op jit(solution)/shard_map/all_gather | solution.py:766
  495.3 39.4 %copy-start.31 = (bf16[256,64]{1,0:T(8,128)(2,1)S(1)}, bf16[256,64]{1,0:T(8,128)(2,1)}, u32[]{:S(2)}) copy-start(bf16[256,64]{1,0:T(8,128)(2,1)} %convolution_convert_fusion.laurel_mid) | copy-start | bytes 98308
  495.3 39.4 %copy-start.38 = (f32[2048]{0:T(1024)S(1)}, f32[2048]{0:T(1024)}, u32[]{:S(2)}) copy-start(f32[2048]{0:T(1024)} %param.50) | copy-start | bytes 24580
  495.4 39.4 %copy-start.39 = (f32[2048]{0:T(1024)S(1)}, f32[2048]{0:T(1024)}, u32[]{:S(2)}) copy-start(f32[2048]{0:T(1024)} %param.51) | copy-start | bytes 24580
  495.4 39.4 %copy-start.40 = (f32[2048]{0:T(1024)S(1)}, f32[2048]{0:T(1024)}, u32[]{:S(2)}) copy-start(f32[2048]{0:T(1024)} %param.52) | copy-start | bytes 24580
  496.4 54.8 %collective-permute-start.3 = (bf16[256,2048]{1,0:T(8,128)(2,1)}, bf16[256,2048]{1,0:T(8,128)(2,1)}, u32[]{:S(2)}, u32[]{:S(2)}) collective-permute-start(bf16[256,2048]{1,0:T(8,128)(2,1)} %pad_maximum_fusion.4), channel_id=1, source_target_pairs={{0,1},{1,0},{2,3},{3,2},{4,5},{5,4},{6,7},{7,6},{8,9},{9,8},{10,11... | collective-permute-start | bytes 3145736 | tf_op jit(solution)/shard_map/ppermute | solution.py:27
  497.9 36.0 %collective-permute-start.7 = (bf16[128,2048]{1,0:T(8,128)(2,1)S(1)}, bf16[128,2048]{1,0:T(8,128)(2,1)S(1)}, u32[]{:S(2)}, u32[]{:S(2)}) collective-permute-start(bf16[128,2048]{1,0:T(8,128)(2,1)S(1)} %slice.393), channel_id=1, source_target_pairs={{0,1},{1,0},{2,3},{3,2},{4,5},{5,4},{6,7},{7,6},{8,9},{9,8},{10,11... | collective-permute-start | bytes 1572872 | tf_op jit(solution)/shard_map/ppermute | solution.py:27
  499.4 45.6 %collective-permute-start.5 = (bf16[128,2048]{1,0:T(8,128)(2,1)}, bf16[128,2048]{1,0:T(8,128)(2,1)}, u32[]{:S(2)}, u32[]{:S(2)}) collective-permute-start(bf16[128,2048]{1,0:T(8,128)(2,1)} %slice.392), channel_id=1, source_target_pairs={{0,1},{1,0},{2,3},{3,2},{4,5},{5,4},{6,7},{7,6},{8,9},{9,8},{10,11... | collective-permute-start | bytes 1572872 | tf_op jit(solution)/shard_map/ppermute | solution.py:27
  542.6 15.2 %collective-permute-start.9 = (bf16[128,2048]{1,0:T(8,128)(2,1)}, bf16[128,2048]{1,0:T(8,128)(2,1)}, u32[]{:S(2)}, u32[]{:S(2)}) collective-permute-start(bf16[128,2048]{1,0:T(8,128)(2,1)} %get-tuple-element.98), channel_id=1, source_target_pairs={{0,1},{1,0},{2,3},{3,2},{4,5},{5,4},{6,7},{7,6},{8,9},{9,8},{10,11... | collective-permute-start | bytes 1572872 | tf_op jit(solution)/shard_map/ppermute | solution.py:27
  549.7 15.7 %collective-permute-start.8 = (bf16[128,2048]{1,0:T(8,128)(2,1)}, bf16[128,2048]{1,0:T(8,128)(2,1)S(1)}, u32[]{:S(2)}, u32[]{:S(2)}) collective-permute-start(bf16[128,2048]{1,0:T(8,128)(2,1)} %get-tuple-element.97), channel_id=1, source_target_pairs={{0,1},{1,0},{2,3},{3,2},{4,5},{5,4},{6,7},{7,6},{8,9},{9,8},{10,11... | collective-permute-start | bytes 1572872 | tf_op jit(solution)/shard_map/ppermute | solution.py:27
  556.0 11.9 %copy-start.84 = (bf16[16,2048]{1,0:T(8,128)(2,1)S(1)}, bf16[16,2048]{1,0:T(8,128)(2,1)}, u32[]{:S(2)}) copy-start(bf16[16,2048]{1,0:T(8,128)(2,1)} %get-tuple-element.199.out_out) | copy-start | bytes 196612
  556.1 124.0 %reduce-scatter.5.cloned.1.call-start = ((), (), s32[]{:S(2)}) async-start(), calls=%async_computation.3 | async-start | bytes 860160 | tf_op jit(solution)/shard_map/reduce_scatter | solution.py:765
  601.2 4.0 collective-permute-start.10
  638.1 7.7 %copy-start.48 = (bf16[2,4,16,18944]{3,2,1,0:T(8,128)(2,1)S(1)}, bf16[2,4,16,18944]{3,2,1,0:T(8,128)(2,1)}, u32[]{:S(2)}) copy-start(bf16[2,4,16,18944]{3,2,1,0:T(8,128)(2,1)} %reshape.693) | copy-start | bytes 14548996
  654.2 89.1 %all-gather.7.cloned.1.call-start = ((), (), s32[]{:S(2)}) async-start(), calls=%async_computation.5 | async-start | bytes 2838528 | tf_op jit(solution)/shard_map/all_gather | solution.py:766
  660.8 26.8 %collective-permute-start.11 = (bf16[256,2048]{1,0:T(8,128)(2,1)}, bf16[256,2048]{1,0:T(8,128)(2,1)}, u32[]{:S(2)}, u32[]{:S(2)}) collective-permute-start(bf16[256,2048]{1,0:T(8,128)(2,1)} %constant_dynamic-slice_fusion), channel_id=1, source_target_pairs={{0,1},{1,0},{2,3},{3,2},{4,5},{5,4},{6,7},{7,6},{8,9},{9,8},{10,11... | collective-permute-start | bytes 3145736 | tf_op jit(solution)/shard_map/ppermute | solution.py:27
  693.0 27.5 %collective-permute-start.12 = (bf16[256,2048]{1,0:T(8,128)(2,1)S(1)}, bf16[256,2048]{1,0:T(8,128)(2,1)S(1)}, u32[]{:S(2)}, u32[]{:S(2)}) collective-permute-start(bf16[256,2048]{1,0:T(8,128)(2,1)S(1)} %fusion.21), channel_id=1, source_target_pairs={{0,1},{1,0},{2,3},{3,2},{4,5},{5,4},{6,7},{7,6},{8,9},{9,8},{10,11... | collective-permute-start | bytes 3145736 | tf_op jit(solution)/shard_map/ppermute | solution.py:27
  (96 other events, 278.9 us)
Sparse Core Ops, SparseCore 0:
  495.4 26.5 reduce-scatter.2
  556.2 66.8 all-gather.4
  654.4 25.6 reduce-scatter.4
  683.2 60.0 all-gather.6

commit v3 on v2

--- a/solution.py
+++ b/solution.py
@@ -108,148 +108,596 @@
     return values * rise, slope
 
 
-def ffn_back_kernel(
-    grad, gate, up, codes, code_down, ffn, w_down, w_gate, w_up, down_in, down_out, gu_out, ffn_in,
-    part, term_gate, term_up, term_down, term_ffn, term_out, total, back_codes, ffn_codes,
+def greet_all(shards, places, ends):
+    z = lax.axis_index("shard")
+    barrier = pltpu.get_barrier_semaphore()
+
+    def signal(place):
+        pl.semaphore_signal(barrier, inc=1, device_id=place, device_id_type=MESH)
+
+    for place in places:
+        signal(place)
+    peers = len(places)
+    if ends:
+
+        @pl.when(z > 0)
+        def _():
+            signal({"shard": z - 1})
+
+        @pl.when(z < shards - 1)
+        def _():
+            signal({"shard": z + 1})
+
+        peers = peers + lax.div(z + shards - 1, shards) + lax.div(2 * shards - 2 - z, shards)
+    pl.semaphore_wait(barrier, peers)
+
+
+def context_partners():
+    c = lax.axis_index("context")
+    return lax.rem(c + 2, 4), c + 1 - 2 * lax.rem(c, 2)
+
+
+def sharer(pack, whole, inbox, turn_in, turn_out, piece, semaphores, shards):
+    (
+        pre_send, pre_recv, z_send, z_recv, x_send, x_recv, y_send, y_recv, near_send, near_recv,
+        far_send, far_recv, keep_sem,
+    ) = semaphores
+    z, c, side = (lax.axis_index(a) for a in ("shard", "context", "tensor"))
+    across, beside = context_partners()
+    opposite = lax.rem(beside + 2, 4)
+    columns = piece.shape[1]
+
+    def cols(q):
+        return pl.ds(pl.multiple_of(q * columns, 128), columns)
+
+    def region(t, s, q):
+        return whole.at[t, s, :, cols(q)]
+
+    def copy(source, target, send, recv, place):
+        return pltpu.make_async_remote_copy(
+            src_ref=source, dst_ref=target, send_sem=send, recv_sem=recv, device_id=place, device_id_type=MESH
+        )
+
+    def halves(k):
+        q = beside if k == 0 else opposite
+        return copy(pack.at[:, cols(q)], inbox.at[k], pre_send.at[k], pre_recv.at[k], {"context": beside})
+
+    def turned():
+        return copy(turn_out, turn_in, pre_send.at[2], pre_recv.at[2], {"context": across})
+
+    def z_copy(s, source, sender, by):
+        return copy(source, region(side, s, c), z_send.at[sender], z_recv.at[s], {"shard": z + by})
+
+    def passed(s, by):
+        return z_copy(s, region(side, s, c), s, by)
+
+    def x_copy(s, source, t):
+        return copy(source, region(t, s, c), x_send.at[s], x_recv.at[s], {"tensor": 1 - side})
+
+    def y_copy(t, s, source, q):
+        return copy(source, region(t, s, q), y_send.at[t, s], y_recv.at[t, s], {"context": across})
+
+    def near_copy(t, s, source, q):
+        return copy(source, region(t, s, q), near_send.at[t, s], near_recv.at[t, s], {"context": beside})
+
+    def far_copy(t, s, q):
+        at = region(t, s, q)
+        return copy(at, at, far_send.at[t, s], far_recv.at[t, s], {"context": beside})
+
+    def keep():
+        return pltpu.make_async_copy(piece, region(side, z, c), keep_sem)
+
+    def start():
+        for k in range(2):
+            halves(k).start()
+
+    def turn():
+        for k in range(2):
+            halves(k).wait_recv()
+        turn_out[...] = low(pack[:, cols(across)] + inbox[1])
+        turned().start()
+
+    def settle():
+        turned().wait_recv()
+        piece[...] = low(pack[:, cols(c)] + inbox[0] + wide(turn_in[...]))
+        keep().start()
+
+        @pl.when(z < shards - 1)
+        def _():
+            z_copy(z, piece, z, 1).start()
+
+        @pl.when(z > 0)
+        def _():
+            z_copy(z, piece, shards, -1).start()
+
+        x_copy(z, piece, side).start()
+        y_copy(side, z, piece, c).start()
+        near_copy(side, z, piece, c).start()
+
+    def hand_on(s):
+        at = region(side, s, c)
+        x_copy(s, at, side).start()
+        y_copy(side, s, at, c).start()
+        near_copy(side, s, at, c).start()
+
+    def hop(d):
+        @pl.when(z >= d)
+        def _():
+            s = z - d
+            passed(s, 1).wait_recv()
+
+            @pl.when(z < shards - 1)
+            def _():
+                passed(s, 1).start()
+
+            hand_on(s)
+
+        @pl.when(z + d <= shards - 1)
+        def _():
+            s = z + d
+            passed(s, -1).wait_recv()
+
+            @pl.when(z > 0)
+            def _():
+                passed(s, -1).start()
+
+            hand_on(s)
+
+    def hops(first):
+        lax.fori_loop(first, shards, lambda d, carry: (hop(d), carry)[1], 0)
+
+    def cross_over():
+        def one(s, carry):
+            at = region(1 - side, s, c)
+            x_copy(s, at, 1 - side).wait_recv()
+            y_copy(1 - side, s, at, c).start()
+            near_copy(1 - side, s, at, c).start()
+            return carry
+
+        lax.fori_loop(0, shards, one, 0)
+
+    def every(act):
+        def one(s, carry):
+            for t in range(2):
+                act(t, s)
+            return carry
+
+        lax.fori_loop(0, shards, one, 0)
+
+    def spread():
+        def act(t, s):
+            y_copy(t, s, region(t, s, across), across).wait_recv()
+            far_copy(t, s, across).start()
+
+        every(act)
+
+    def finish():
+        def act(t, s):
+            near_copy(t, s, region(t, s, beside), beside).wait_recv()
+            far_copy(t, s, opposite).wait_recv()
+            y_copy(t, s, region(t, s, c), c).wait_send()
+            near_copy(t, s, region(t, s, c), c).wait_send()
+            far_copy(t, s, across).wait_send()
+
+        every(act)
+
+        def one(s, carry):
+            x_copy(s, region(side, s, c), side).wait_send()
+
+            @pl.when((s < z) & (z < shards - 1))
+            def _():
+                passed(s, 1).wait_send()
+
+            @pl.when((s > z) & (z > 0))
+            def _():
+                passed(s, -1).wait_send()
+
+            return carry
+
+        lax.fori_loop(0, shards, one, 0)
+
+        @pl.when(z < shards - 1)
+        def _():
+            z_copy(z, piece, z, 1).wait_send()
+
+        @pl.when(z > 0)
+        def _():
+            z_copy(z, piece, shards, -1).wait_send()
+
+        for k in range(2):
+            halves(k).wait_send()
+        turned().wait_send()
+        keep().wait()
+
+    return start, turn, settle, hop, hops, cross_over, spread, finish
+
+
+def sharer_scratch(rows, columns, shards):
+    part = columns // 4
+    dma = pltpu.SemaphoreType.DMA
+    return [
+        pltpu.VMEM((2, rows, part), jnp.float32),
+        pltpu.VMEM((rows, part), jnp.bfloat16),
+        pltpu.VMEM((rows, part), jnp.bfloat16),
+        pltpu.VMEM((rows, part), jnp.bfloat16),
+        dma((3,)), dma((3,)), dma((shards + 1,)), dma((shards,)), dma((shards,)), dma((shards,)),
+        dma((2, shards)), dma((2, shards)), dma((2, shards)), dma((2, shards)), dma((2, shards)), dma((2, shards)),
+        dma,
+    ]
+
+
+def tail_kernel(
+    shards,
+    grad_query, grad_key, grad_value, w_query, w_key, w_value, code_attn, normed, query_out, kv_out, attn_in,
+    out_in_term, out_out_term, tokens, gain_in, grad_comb, grad_normed,
+    input_grad_out, whole,
+    pack, mine, sent, got, result, send_sem, recv_sem, keep_sem, *shared,
 ):
-    step = pl.program_id(0)
+    side = lax.axis_index("tensor")
+    partner = {"tensor": 1 - side}
+    across, beside = context_partners()
+    count, width = normed.shape
+    half = count // 2
+    quarter = half // 2
+    rank = query_out.shape[0]
+    start, turn, settle, hop, hops, cross_over, spread, finish = sharer(
+        pack, whole, shared[0], shared[1], shared[2], shared[3], shared[4:], shards
+    )
+    greet_all(shards, [partner, {"context": across}, {"context": beside}], True)
+    parts = ((grad_query, w_query, query_out[...]), (grad_key, w_key, kv_out[0]), (grad_value, w_value, kv_out[1]))
+    at = 0
+
+    def put(term):
+        nonlocal at
+        pack[:, at : at + term.shape[1]] = term
+        at += term.shape[1]
+
+    put(out_in_term[...])
+    put(out_out_term[...])
+    backs = []
+    for i, (grad, _, table) in enumerate(parts):
+        put(dot_o(code_attn[:, i * rank : (i + 1) * rank], grad[...]))
+        backs.append(low(dot_t(grad[...], table)))
+    for back in backs:
+        put(dot_o(back, normed[...]))
+    start()
+
+    def product(here):
+        total = dot_t(grad_query[here, :], w_query[...])
+        total += dot_t(grad_key[here, :], w_key[...]) + dot_t(grad_value[here, :], w_value[...])
+        for i, (grad, _, table) in enumerate(parts):
+            back = low(dot_t(grad[here, :], table))
+            total += dot(back, attn_in[i * rank : (i + 1) * rank, :])
+        return total
+
+    def send(source, target, k):
+        return pltpu.make_async_remote_copy(
+            src_ref=source, dst_ref=target, send_sem=send_sem.at[k], recv_sem=recv_sem.at[k],
+            device_id=partner, device_id_type=MESH,
+        )
+
+    def rows(k):
+        return pl.ds(k * quarter, quarter)
+
+    def rows_of(owner, k):
+        return pl.ds(pl.multiple_of(owner * half + k * quarter, quarter), quarter)
+
+    swaps = []
+    for k in range(2):
+        sent[rows(k), :] = low(product(rows_of(1 - side, k)))
+        swaps.append(send(sent.at[rows(k), :], got.at[rows(k), :], k))
+        swaps[k].start()
+    turn()
+    for k in range(2):
+        mine[rows(k), :] = product(rows_of(side, k))
+        if k == 0:
+            settle()
+    ends = []
+    for k in range(2):
+        swaps[k].wait_recv()
+        here = rows(k)
+        grad = (grad_normed[here, :] + mine[here, :] + wide(got[here, :])) * gain_in[...]
+        token = wide(tokens[here, :])
+        there = rows_of(side, k)
+        result[there, :] = low(grad_comb[here, :] + rms_back(token, inverse_rms(token), grad))
+        ends.append(send(result.at[there, :], result.at[there, :], 2 + k))
+        ends[k].start()
+        if k == 0:
+            hop(1)
+    hops(2)
+    cross_over()
+    spread()
+    for end in ends:
+        end.wait()
+    keep = pltpu.make_async_copy(result, input_grad_out, keep_sem)
+    keep.start()
+    for swap_part in swaps:
+        swap_part.wait_send()
+    finish()
+    keep.wait()
+
+
+def tail(arrays, shards):
+    count, width = arrays[7].shape
+    rank = arrays[8].shape[0]
+    half = count // 2
+    columns = sum(a.shape[1] for a in arrays[:3]) + arrays[11].shape[1] + arrays[12].shape[1] + 3 * width
+    bf16, f32 = jnp.bfloat16, jnp.float32
+    anywhere, vmem = pl.BlockSpec(memory_space=pl.ANY), pl.BlockSpec(memory_space=pltpu.VMEM)
+    return pl.pallas_call(
+        functools.partial(tail_kernel, shards),
+        out_shape=[
+            jax.ShapeDtypeStruct((count, width), bf16),
+            jax.ShapeDtypeStruct((2, shards, rank, columns), bf16),
+        ],
+        in_specs=[vmem] * len(arrays),
+        out_specs=[anywhere] * 2,
+        scratch_shapes=[
+            pltpu.VMEM((rank, columns), f32),
+            pltpu.VMEM((half, width), f32),
+            pltpu.VMEM((half, width), bf16),
+            pltpu.VMEM((half, width), bf16),
+            pltpu.VMEM((count, width), bf16),
+            pltpu.SemaphoreType.DMA((4,)),
+            pltpu.SemaphoreType.DMA((4,)),
+            pltpu.SemaphoreType.DMA,
+        ]
+        + sharer_scratch(rank, columns, shards),
+        compiler_params=pltpu.CompilerParams(
+            collective_id=3, has_side_effects=True, vmem_limit_bytes=56 * 2**20
+        ),
+    )(*arrays)
+
+
+def aft_kernel(
+    shards, block, strip,
+    full_gate, full_up, full_down, gate_in, up_in,
+    part, combined, per_layer, cotangent, lgate, lproj, code_ffn, code_down, ffn, down_in, down_out, gu_out, ffn_in,
+    attn_proj, laurel_mid, left, right, mark, gain_post, gain_layer, gain_pre, gain_attn, gain_laurel,
+    grad_attn_out, whole, output, grad_comb, grad_normed, pack,
+    got, grad, grad_gate, grad_up, down_w, gate_v, up_v, gate_w, up_w, mine, sent, came, attn, back_codes, ffn_codes,
+    fetch_sem, strip_sem, keep_sem, send_sem, recv_sem, *shared,
+):
+    side = lax.axis_index("tensor")
+    partner = {"tensor": 1 - side}
+    across, beside = context_partners()
+    greet_all(shards, [partner, {"context": across}, {"context": beside}], True)
+    start, turn, settle, hop, hops, cross_over, spread, finish = sharer(
+        pack, whole, shared[0], shared[1], shared[2], shared[3], shared[4:], shards
+    )
+    count, width = grad.shape
+    half = count // 2
+    quarter = half // 2
     rank = down_in.shape[0]
-
-    @pl.when(step == 0)
-    def _():
-        back_codes[...] = low(dot_t(grad[...], down_out[...]))
-        total[...] = jnp.zeros_like(total)
-        ffn_codes[...] = jnp.zeros_like(ffn_codes)
-        term_out[...] = dot_o(code_down[...], grad[...])
-
-    hidden_grad = dot_t(grad[...], w_down[...]) + dot(back_codes[...], down_in[...])
-    up_now = wide(up[...])
-    act, slope = gelu_parts(wide(gate[...]))
-    grad_gate = low(hidden_grad * up_now * slope)
-    grad_up = low(hidden_grad * act)
-    hidden = low(act * up_now)
-    total[...] += dot_t(grad_gate, w_gate[...]) + dot_t(grad_up, w_up[...])
-    ffn_codes[0] += dot_t(grad_gate, gu_out[0])
-    ffn_codes[1] += dot_t(grad_up, gu_out[1])
-    term_gate[...] = dot_o(codes[:, :rank], grad_gate)
-    term_up[...] = dot_o(codes[:, rank:], grad_up)
-    term_down[...] = dot_o(back_codes[...], hidden)
-
-    @pl.when(step == pl.num_programs(0) - 1)
-    def _():
-        first, second = low(ffn_codes[0]), low(ffn_codes[1])
-        part[...] = low(total[...] + dot(first, ffn_in[:rank]) + dot(second, ffn_in[rank:]))
-        term_ffn[:rank] = dot_o(first, ffn[...])
-        term_ffn[rank:] = dot_o(second, ffn[...])
-
-
-def ffn_back(group, grad, gate, up, codes, code_down, ffn, w_down, w_gate, w_up, down_in, down_out, gu_out, ffn_in):
-    rows, width = grad.shape
-    hidden = gate.shape[1]
-    rank = down_in.shape[0]
-    block = min(512, hidden)
-    whole = lambda *shape: pl.BlockSpec(shape, lambda j: (0,) * len(shape))
-    picked = lambda columns: pl.BlockSpec((rows, columns), lambda j: (group, 0))
-    f32 = jnp.float32
+    hidden = grad_gate.shape[1]
+    steps = hidden // block
+    strips = width // strip
+
+    def send(source, target, k):
+        return pltpu.make_async_remote_copy(
+            src_ref=source, dst_ref=target, send_sem=send_sem.at[k], recv_sem=recv_sem.at[k],
+            device_id=partner, device_id_type=MESH,
+        )
+
+    def rows(k):
+        return pl.ds(k * quarter, quarter)
+
+    down_swaps = [send(part.at[rows(2 + k), :], got.at[rows(k), :], k) for k in range(2)]
+    grad_swaps = [send(grad.at[rows(k), :], grad.at[rows(2 + k), :], 2 + k) for k in range(2)]
+    for swap_down in down_swaps:
+        swap_down.start()
+
+    def fetches(t):
+        slot, j = lax.rem(t, 2), lax.rem(t, steps)
+        at = pl.ds(pl.multiple_of(j * block, block), block)
+        here = pl.ds(pl.multiple_of(lax.div(t, steps) * half, half), half)
+        return (
+            pltpu.make_async_copy(full_down.at[at, :], down_w.at[slot], fetch_sem.at[0, slot]),
+            pltpu.make_async_copy(gate_in.at[here, at], gate_v.at[slot], fetch_sem.at[1, slot]),
+            pltpu.make_async_copy(up_in.at[here, at], up_v.at[slot], fetch_sem.at[2, slot]),
+        )
+
+    def strip_fetches(k):
+        slot = lax.rem(k, 2)
+        at = pl.ds(pl.multiple_of(k * strip, strip), strip)
+        return (
+            pltpu.make_async_copy(full_gate.at[at, :], gate_w.at[slot], strip_sem.at[0, slot]),
+            pltpu.make_async_copy(full_up.at[at, :], up_w.at[slot], strip_sem.at[1, slot]),
+        )
+
+    for fetch in fetches(0) + strip_fetches(0):
+        fetch.start()
+    pack[...] = jnp.zeros_like(pack)
+    ffn_codes[...] = jnp.zeros_like(ffn_codes)
+
+    for k in range(2):
+        down_swaps[k].wait_recv()
+        at = rows(k)
+        down = wide(part[at, :]) + wide(got[at, :])
+        down_inverse = inverse_rms(down)
+        after = combined[at, :] + down * down_inverse * gain_post[...]
+        mixing = wide(per_layer[at, :])
+        act, slope = gelu_parts(dot(low(after), lgate[...]))
+        proj = dot(low(act * mixing), lproj[...])
+        proj_inverse = inverse_rms(proj)
+        output[at, :] = low(after + proj * proj_inverse * gain_layer[...])
+        top = wide(cotangent[at, :])
+        grad_proj = rms_back(proj, proj_inverse, top * gain_layer[...])
+        grad_mix = dot_t(low(grad_proj), lproj[...]) * mixing * slope
+        top = top + dot_t(low(grad_mix), lgate[...])
+        grad_comb[at, :] = top
+        grad[at, :] = low(rms_back(down, down_inverse, top * gain_post[...]))
+        grad_swaps[k].start()
+        back_codes[at, :] = low(dot_t(grad[at, :], down_out[...]))
+
+    def level(t, carry):
+        @pl.when(t + 1 < 2 * steps)
+        def _():
+            for fetch in fetches(t + 1):
+                fetch.start()
+
+        @pl.when(t == steps)
+        def _():
+            for k in range(2):
+                grad_swaps[k].wait_recv()
+            back_codes[half:, :] = low(dot_t(grad[half:, :], down_out[...]))
+
+        slot, j = lax.rem(t, 2), lax.rem(t, steps)
+        at = pl.ds(pl.multiple_of(j * block, block), block)
+        here = pl.ds(pl.multiple_of(lax.div(t, steps) * half, half), half)
+        for fetch in fetches(t):
+            fetch.wait()
+        back = back_codes[here, :]
+        hidden_grad = dot_t(grad[here, :], down_w[slot]) + dot(back, down_in[:, at])
+        up_now = wide(up_v[slot])
+        act, slope = gelu_parts(wide(gate_v[slot]))
+        grad_g = low(hidden_grad * up_now * slope)
+        grad_u = low(hidden_grad * act)
+        grad_gate[here, at] = grad_g
+        grad_up[here, at] = grad_u
+        ffn_codes[0, here, :] += dot_t(grad_g, gu_out[0, :, at])
+        ffn_codes[1, here, :] += dot_t(grad_u, gu_out[1, :, at])
+        codes = code_ffn[here, :]
+
+        def put(i, term):
+            pack[:, pl.ds(pl.multiple_of(i * hidden + j * block, block), block)] += term
+
+        put(0, dot_o(codes[:, :rank], grad_g))
+        put(1, dot_o(codes[:, rank:], grad_u))
+        put(2, dot_o(back, low(act * up_now)))
+        return carry
+
+    lax.fori_loop(0, 2 * steps, level, 0)
+    base = 3 * hidden
+    pack[:, base : base + width] = dot_o(low(ffn_codes[0]), ffn[...])
+    pack[:, base + width : base + 2 * width] = dot_o(low(ffn_codes[1]), ffn[...])
+    pack[:, base + 2 * width : base + 3 * width] = dot_o(code_down[...], grad[...])
+    pack[:, base + 3 * width :] = mark[...]
+    start()
+
+    def strip_send(k):
+        return send(sent.at[k], came.at[k], 4 + k)
+
+    def cross(k, carry):
+        @pl.when(k + 1 < strips)
+        def _():
+            for fetch in strip_fetches(k + 1):
+                fetch.start()
+
+        slot = lax.rem(k, 2)
+        at = pl.ds(pl.multiple_of(k * strip, strip), strip)
+        for fetch in strip_fetches(k):
+            fetch.wait()
+        result = (
+            dot_t(grad_gate[...], gate_w[slot])
+            + dot_t(grad_up[...], up_w[slot])
+            + dot(low(ffn_codes[0]), ffn_in[:rank, at])
+            + dot(low(ffn_codes[1]), ffn_in[rank:, at])
+        )
+        sent[k] = low(result[half:])
+        strip_send(k).start()
+        mine[:, at] = result[:half]
+        for when, act in ((1, turn), (2, settle), (3, lambda: hop(1)), (4, lambda: hop(2)), (5, lambda: hops(3))):
+            pl.when(k == when)(act)
+        return carry
+
+    lax.fori_loop(0, strips, cross, 0)
+    cross_over()
+
+    def add(k, carry):
+        at = pl.ds(pl.multiple_of(k * strip, strip), strip)
+        strip_send(k).wait_recv()
+        mine[:, at] += wide(came[k])
+        return carry
+
+    lax.fori_loop(0, strips, add, 0)
+    attn_swaps = []
+    for k in range(2):
+        at = rows(k)
+        comb = combined[at, :]
+        top = (grad_comb[at, :] + rms_back(comb, inverse_rms(comb), mine[at, :] * gain_pre[...])) * ROOT_HALF
+        grad_comb[at, :] = top
+        proj = attn_proj[at, :]
+        there = pl.ds(pl.multiple_of(side * half + k * quarter, quarter), quarter)
+        attn[there, :] = low(rms_back(proj, inverse_rms(proj), top * gain_attn[...]))
+        attn_swaps.append(send(attn.at[there, :], attn.at[there, :], 4 + strips + k))
+        attn_swaps[k].start()
+        end = dot(laurel_mid[at, :], right[...])
+        grad_end = low(rms_back(end, inverse_rms(end), top * gain_laurel[...]))
+        grad_normed[at, :] = top + dot(low(dot_t(grad_end, right[...])), left[...])
+    spread()
+    for swap_attn in attn_swaps:
+        swap_attn.wait()
+    keep = pltpu.make_async_copy(attn, grad_attn_out, keep_sem)
+    keep.start()
+    for k in range(2):
+        down_swaps[k].wait_send()
+        grad_swaps[k].wait_send()
+
+    def flush(k, carry):
+        strip_send(k).wait_send()
+        return carry
+
+    lax.fori_loop(0, strips, flush, 0)
+    finish()
+    keep.wait()
+
+
+def aft(weights, kept, arrays, shards):
+    full_gate = weights[0]
+    part, combined, per_layer = arrays[:3]
+    count, width = part.shape
+    hidden = full_gate.shape[1]
+    half = count // 2
+    rank = arrays[9].shape[0]
+    block, strip = min(512, hidden), 256
+    strips = width // strip
+    columns = 3 * hidden + 3 * width + arrays[17].shape[1]
+    bf16, f32 = jnp.bfloat16, jnp.float32
+    shape = jax.ShapeDtypeStruct
+    anywhere, vmem = pl.BlockSpec(memory_space=pl.ANY), pl.BlockSpec(memory_space=pltpu.VMEM)
     return pl.pallas_call(
-        ffn_back_kernel,
-        grid=(hidden // block,),
-        in_specs=[
-            whole(rows, width),
-            pl.BlockSpec((rows, block), lambda j: (group, j)),
-            pl.BlockSpec((rows, block), lambda j: (group, j)),
-            picked(2 * rank),
-            picked(rank),
-            picked(width),
-            pl.BlockSpec((block, width), lambda j: (j, 0)),
-            pl.BlockSpec((width, block), lambda j: (0, j)),
-            pl.BlockSpec((width, block), lambda j: (0, j)),
-            pl.BlockSpec((rank, block), lambda j: (0, j)),
-            whole(rank, width),
-            pl.BlockSpec((2, rank, block), lambda j: (0, 0, j)),
-            whole(2 * rank, width),
+        functools.partial(aft_kernel, shards, block, strip),
+        out_shape=[
+            shape((count, width), bf16),
+            shape((2, shards, rank, columns), bf16),
+            shape((half, width), bf16),
+            shape((half, width), f32),
+            shape((half, width), f32),
         ],
-        out_specs=[
-            whole(rows, width),
-            pl.BlockSpec((rank, block), lambda j: (0, j)),
-            pl.BlockSpec((rank, block), lambda j: (0, j)),
-            pl.BlockSpec((rank, block), lambda j: (0, j)),
-            whole(2 * rank, width),
-            whole(rank, width),
-        ],
-        out_shape=[
-            jax.ShapeDtypeStruct((rows, width), jnp.bfloat16),
-            jax.ShapeDtypeStruct((rank, hidden), f32),
-            jax.ShapeDtypeStruct((rank, hidden), f32),
-            jax.ShapeDtypeStruct((rank, hidden), f32),
-            jax.ShapeDtypeStruct((2 * rank, width), f32),
-            jax.ShapeDtypeStruct((rank, width), f32),
-        ],
+        in_specs=[anywhere] * 5 + [vmem] * len(arrays),
+        out_specs=[anywhere] * 2 + [vmem] * 3,
         scratch_shapes=[
-            pltpu.VMEM((rows, width), f32),
-            pltpu.VMEM((rows, rank), jnp.bfloat16),
-            pltpu.VMEM((2, rows, rank), f32),
-        ],
-        compiler_params=pltpu.CompilerParams(vmem_limit_bytes=48 * 2**20),
+            pltpu.VMEM((rank, columns), f32),
+            pltpu.VMEM((half, width), bf16),
+            pltpu.VMEM((count, width), bf16),
+            pltpu.VMEM((count, hidden), bf16),
+            pltpu.VMEM((count, hidden), bf16),
+            pltpu.VMEM((2, block, width), bf16),
+            pltpu.VMEM((2, half, block), bf16),
+            pltpu.VMEM((2, half, block), bf16),
+            pltpu.VMEM((2, strip, hidden), bf16),
+            pltpu.VMEM((2, strip, hidden), bf16),
+            pltpu.VMEM((half, width), f32),
+            pltpu.VMEM((strips, half, strip), bf16),
+            pltpu.VMEM((strips, half, strip), bf16),
+            pltpu.VMEM((count, width), bf16),
+            pltpu.VMEM((count, rank), bf16),
+            pltpu.VMEM((2, count, rank), f32),
+            pltpu.SemaphoreType.DMA((3, 2)),
+            pltpu.SemaphoreType.DMA((2, 2)),
+            pltpu.SemaphoreType.DMA,
+            pltpu.SemaphoreType.DMA((6 + strips,)),
+            pltpu.SemaphoreType.DMA((6 + strips,)),
+        ]
+        + sharer_scratch(rank, columns, shards),
+        compiler_params=pltpu.CompilerParams(
+            collective_id=2, has_side_effects=True, vmem_limit_bytes=60 * 2**20
+        ),
         cost_estimate=pl.CostEstimate(
-            flops=6 * rows * width * hidden, bytes_accessed=6 * width * hidden, transcendentals=rows * hidden
+            flops=6 * count * width * hidden, bytes_accessed=8 * width * hidden, transcendentals=count * hidden
         ),
-    )(grad, gate, up, codes, code_down, ffn, w_down, w_gate, w_up, down_in, down_out, gu_out, ffn_in)
-
-
-def crown_kernel(
-    mine, theirs, combined, per_layer, cotangent, input_gate, input_proj, gain_post, gain_layer,
-    output, grad_down, grad_after,
-):
-    down = wide(mine[...]) + wide(theirs[...])
-    down_inverse = inverse_rms(down)
-    after = combined[...] + down * down_inverse * gain_post[...]
-    mixing = wide(per_layer[...])
-    act, slope = gelu_parts(dot(low(after), input_gate[...]))
-    proj = dot(low(act * mixing), input_proj[...])
-    proj_inverse = inverse_rms(proj)
-    output[...] = low(after + proj * proj_inverse * gain_layer[...])
-    grad = wide(cotangent[...])
-    grad_proj = rms_back(proj, proj_inverse, grad * gain_layer[...])
-    grad_gate = dot_t(low(grad_proj), input_proj[...]) * mixing * slope
-    grad = grad + dot_t(low(grad_gate), input_gate[...])
-    grad_after[...] = grad
-    grad_down[...] = low(rms_back(down, down_inverse, grad * gain_post[...]))
-
-
-def comb_back_kernel(
-    mine, theirs, grad_after, combined, attn_proj, laurel_mid, left, right, gain_pre, gain_attn, gain_laurel,
-    grad_attn, grad_comb, grad_normed,
-):
-    grad = (wide(mine[...]) + wide(theirs[...])) * gain_pre[...]
-    comb = combined[...]
-    grad = (grad_after[...] + rms_back(comb, inverse_rms(comb), grad)) * ROOT_HALF
-    grad_comb[...] = grad
-    proj = attn_proj[...]
-    grad_attn[...] = low(rms_back(proj, inverse_rms(proj), grad * gain_attn[...]))
-    end = dot(laurel_mid[...], right[...])
-    grad_end = low(rms_back(end, inverse_rms(end), grad * gain_laurel[...]))
-    grad_normed[...] = grad + dot(low(dot_t(grad_end, right[...])), left[...])
-
-
-def rowwise(kernel, group, rows, arrays, constants, outs):
-    width = max(a.shape[1] for a, _ in arrays)
-
-    def spec(columns, at):
-        return pl.BlockSpec((rows, columns), lambda i: (at, 0))
-
-    return pl.pallas_call(
-        kernel,
-        grid=(1,),
-        in_specs=[spec(a.shape[1], group if own is None else own) for a, own in arrays]
-        + [pl.BlockSpec(c.shape, lambda i: (0, 0)) for c in constants],
-        out_specs=[spec(columns, 0) for columns, _ in outs],
-        out_shape=[jax.ShapeDtypeStruct((rows, columns), kind) for columns, kind in outs],
-        compiler_params=pltpu.CompilerParams(vmem_limit_bytes=48 * 2**20),
-        cost_estimate=pl.CostEstimate(
-            flops=40 * rows * width + 2 * rows * width * 1024, bytes_accessed=24 * rows * width, transcendentals=rows
-        ),
-    )(*[a for a, _ in arrays], *constants)
+    )(*weights, *kept, *arrays)
 
 
 def mover(sources, fulls, semaphores, shards):
@@ -582,8 +1030,7 @@
             token + proj * inverse_rms(proj) * gain_attn[...] + normed + end * inverse_rms(end) * gain_laurel[...]
         ) * ROOT_HALF
         combined[at, :] = comb
-        to = pl.multiple_of(i * rows + lax.div(i * rows, quarter) * quarter, rows)
-        ffn[pl.ds(to, rows), :] = low(comb * inverse_rms(comb) * gain_pre[...])
+        ffn[at, :] = low(comb * inverse_rms(comb) * gain_pre[...])
         return carry
 
     lax.fori_loop(0, half // rows, combine, 0)
@@ -591,7 +1038,7 @@
     for k in range(2):
         swaps.append(
             pltpu.make_async_remote_copy(
-                src_ref=ffn.at[pl.ds(k * half, quarter), :], dst_ref=ffn.at[pl.ds(k * half + quarter, quarter), :],
+                src_ref=ffn.at[pl.ds(k * quarter, quarter), :], dst_ref=ffn.at[pl.ds(half + k * quarter, quarter), :],
                 send_sem=swap_send.at[1 + k], recv_sem=swap_recv.at[1 + k],
                 device_id=partner, device_id_type=MESH,
             )
@@ -761,14 +1208,6 @@
     )(*weights, attended, tokens, laurel_mid, out_in, out_out, ffn_in, gu_out, down_in, down_out, *gains)
 
 
-def share(packed):
-    part = lax.psum_scatter(packed, "context", scatter_dimension=1, tiled=True)
-    whole = lax.all_gather(low(part), ("shard", "context", "tensor"), axis=0, tiled=False)
-    shards, contexts, tensors = (lax.axis_size(a) for a in ("shard", "context", "tensor"))
-    whole = whole.reshape(shards, contexts, tensors, packed.shape[0], part.shape[1])
-    return whole.transpose(2, 0, 3, 1, 4).reshape(tensors, shards, packed.shape[0], packed.shape[1])
-
-
 def body(
     tokens,
     layer_input,
@@ -851,7 +1290,7 @@
     tokens_f = wide(tokens[0])
     normed_b = low(rms_norm(tokens_f, gain_in))
     tokens_h = wide(own_half(tokens[0]))
-    normed_h, normed_back = jax.vjp(lambda v: rms_norm(v, gain_in), tokens_h)
+    normed_h = rms_norm(tokens_h, gain_in)
     code_attn = matmul(normed_b, pick_attn_in)
     query_lin = matmul(normed_b, full_query) + matmul(code_attn[:, :rank], pick_query_out)
     key_lin = matmul(normed_b, full_key) + matmul(code_attn[:, rank : 2 * rank], pick_kv_out[0])
@@ -907,61 +1346,19 @@
         pick_out_in.T, pick_out_out, pick_ffn_in.T, pick_gu_out, pick_down_in.T, pick_down_out,
         (gain_in[None], gain_attn[None], gain_laurel[None], gain_pre[None]), shards,
     )
-    quarter = half // 2
-    bf16, f32 = jnp.bfloat16, jnp.float32
-    per_layer_h, cotangent_h = own_half(layer_input[0]), own_half(cotangent[0])
-    crowned = []
-    for g in range(2):
-        theirs = swap(down_part[g * half + quarter : (g + 1) * half])
-        output_g, grad_down_g, grad_after_g = rowwise(
-            crown_kernel, g, quarter,
-            [(down_part, 2 * g), (theirs, 0), (combined, None), (per_layer_h, None), (cotangent_h, None)],
-            [full_layer_gate, full_layer_proj, gain_post[None], gain_layer[None]],
-            [(width, bf16), (width, bf16), (width, f32)],
-        )
-        crowned.append((output_g, grad_down_g, grad_after_g, swap(grad_down_g)))
-    parted = []
-    for g in range(2):
-        grad_down_b = jnp.concatenate([crowned[g][1], crowned[g][3]], axis=0)
-        parted.append(
-            ffn_back(
-                g, grad_down_b, gate_b, up_b, code_ffn, code_down, ffn_b, full_down, full_gate, full_up,
-                pick_down_in.T, pick_down_out, pick_gu_out, pick_ffn_in.T,
-            )
-        )
-    term_gate_out, term_up_out, term_down_in, term_ffn_in, term_down_out = (
-        parted[0][i] + parted[1][i] for i in range(1, 6)
-    )
     mark = jnp.where(
         (lax.broadcasted_iota(jnp.int32, (rank, 512), 1) == chosen) & (place == 0), 1.0, 0.0
     )
-    early = share(
-        jnp.concatenate(
-            [term_gate_out, term_up_out, term_down_in, term_ffn_in[:rank], term_ffn_in[rank:], term_down_out, mark],
-            axis=1,
-        )
-    )
-    turned_back = []
-    for g in range(2):
-        part = parted[g][0]
-        turned_back.append(
-            rowwise(
-                comb_back_kernel, g, quarter,
-                [
-                    (part, 0), (swap(part[quarter:]), 0), (crowned[g][2], 0), (combined, None),
-                    (attn_proj, None), (laurel_mid, None),
-                ],
-                [full_left, full_right, gain_pre[None], gain_attn[None], gain_laurel[None]],
-                [(width, bf16), (width, f32), (width, f32)],
-            )
-        )
-    grad_inputs = jnp.concatenate([turned_back[0][1], turned_back[1][1]], axis=0)
-    grad_normed = jnp.concatenate([turned_back[0][2], turned_back[1][2]], axis=0)
-    grad_attn_b = in_order(
-        jnp.concatenate([turned_back[0][0], turned_back[1][0]], axis=0),
-        jnp.concatenate([swap(turned_back[0][0]), swap(turned_back[1][0])], axis=0),
-    )
-    output_own = jnp.concatenate([crowned[0][0], crowned[1][0]], axis=0)
+    grad_attn_b, early, output_own, grad_inputs, grad_normed = aft(
+        (full_gate, full_up, full_down), (gate_b, up_b),
+        (
+            down_part, combined, own_half(layer_input[0]), own_half(cotangent[0]), full_layer_gate, full_layer_proj,
+            code_ffn, code_down, ffn_b, pick_down_in.T, pick_down_out, pick_gu_out, pick_ffn_in.T,
+            attn_proj, laurel_mid, full_left, full_right, mark,
+            gain_post[None], gain_layer[None], gain_pre[None], gain_attn[None], gain_laurel[None],
+        ),
+        shards,
+    )
     layer_output = in_order(output_own, swap(output_own))
     code_out_back = matmul_t(grad_attn_b, pick_out_out)
     term_out_out = outer(code_out, grad_attn_b)
@@ -991,39 +1388,16 @@
         (grad_query.reshape(count, heads, head_size), grad_kv_own[0], grad_kv_own[1])
     )
     grad_qlin_b = low(grad_qlin)
-    early, grad_qlin_b = lax.optimization_barrier((early, grad_qlin_b))
     grad_klin_b = low(grad_klin)
     grad_vlin_b = low(grad_vlin)
-    code_attn_back = jnp.concatenate(
-        [
-            matmul_t(grad_qlin_b, pick_query_out),
-            matmul_t(grad_klin_b, pick_kv_out[0]),
-            matmul_t(grad_vlin_b, pick_kv_out[1]),
-        ],
-        axis=1,
-    )
-    term_query_out = outer(code_attn[:, :rank], grad_qlin_b)
-    term_key_out = outer(code_attn[:, rank : 2 * rank], grad_klin_b)
-    term_value_out = outer(code_attn[:, 2 * rank :], grad_vlin_b)
-    term_attn_in = outer(code_attn_back, normed_b)
-    late = share(
-        jnp.concatenate(
-            [
-                term_out_in, term_out_out, term_query_out, term_key_out, term_value_out,
-                term_attn_in[:rank], term_attn_in[rank : 2 * rank], term_attn_in[2 * rank :],
-            ],
-            axis=1,
-        )
-    )
-    grad_normed_part = low(
-        matmul_t(grad_qlin_b, full_query)
-        + matmul_t(grad_klin_b, full_key)
-        + matmul_t(grad_vlin_b, full_value)
-        + matmul_t(code_attn_back, pick_attn_in)
-    )
-    grad_normed = grad_normed + wide(own_half(grad_normed_part)) + wide(swap(other_half(grad_normed_part)))
-    grad_own = low(grad_inputs + normed_back(grad_normed)[0])
-    input_grad = in_order(grad_own, swap(grad_own))
+    input_grad, late = tail(
+        (
+            grad_qlin_b, grad_klin_b, grad_vlin_b, full_query, full_key, full_value, low(code_attn), normed_b,
+            pick_query_out, pick_kv_out, pick_attn_in.T, term_out_in, term_out_out,
+            own_half(tokens[0]), gain_in[None], grad_inputs, grad_normed,
+        ),
+        shards,
+    )
 
     at = 0
 

time: 773 us -> 698 us (0.903)
  Pallas kernels: 404 us -> 544 us
  waiting for transfers between devices: 120 us -> 0.01 us
  local copies, waits for them, and re-layouts: 68.9 us -> 35.6 us
  matrix products: 66.9 us -> 39.9 us
  starting transfers between devices: 19.9 us -> 5.67 us
  between operations: 16.8 us -> 2.87 us
  other arithmetic: 70.6 us -> 61.1 us
    pallas_call x6 -> x2, Pallas kernels: 69.3 us -> 209 us  [the longest x1 136 us: aft(): pl.pallas_call(functools.partial(aft_kernel, shards, block, strip), out_s...]
    ppermute x11 -> x1, waiting for transfers between devices: 86.6 us -> 0.01 us  [swap(): return lax.ppermute(array, 'tensor', [(0, 1), (1, 0)])]
    all_gather x2 -> x0, waiting for transfers between devices: 28.6 us -> none  [share(): lax.all_gather(low(part), ('shard', 'context', 'tensor'), axis=0, tiled=F...]
    dot_general x11 -> x4, matrix products: 28.1 us -> 5.34 us  [matmul_t(): lax.dot_general(low(left_op), low(right_op), (((1,), (1,)), ((), ())), pr...]
    reshape x3 -> x0, local copies, waits for them, and re-layouts: 16 us -> none  [the longest x2 11.3 us: share(): whole.transpose(2, 0, 3, 1, 4)]
    ppermute x11 -> x1, starting transfers between devices: 14.6 us -> 0.53 us  [swap(): return lax.ppermute(array, 'tensor', [(0, 1), (1, 0)])]
    unnamed x258 -> x137, local copies, waits for them, and re-layouts: 22.8 us -> 12.2 us
  transfers between devices with their start and end apart: 17 -> 3, of which waited for: 12 -> 0; matrix products, arithmetic and copies ran while one was open for 15% -> 9% of each run, Pallas kernels for 6% -> 11%
where the time goes in v3:
time: 698 us; the launch traced here: 689 us
  Pallas kernels  544 us (78%)
  other arithmetic  61.1 us (9%)
  matrix products  39.9 us (6%)
  local copies, waits for them, and re-layouts  35.6 us (5%)
    pallas_call x1, Pallas kernels, fore(): pl.pallas_call(functools.partial(fore_kernel, shards, block), out_shape=f...  290 us
    pallas_call x1, Pallas kernels, aft(): pl.pallas_call(functools.partial(aft_kernel, shards, block, strip), out_s...  136 us
    pallas_call x1, Pallas kernels, tail(): pl.pallas_call(functools.partial(tail_kernel, shards), out_shape=[jax.Sha...  73.2 us
    pallas_call x1, Pallas kernels, gather(): pl.pallas_call(functools.partial(gather_kernel, axes, shards), out_shape=...  44.3 us
    add x7, other arithmetic, tables(): sum((marks[s].reshape((adapters,) + (1,) * (terms.ndim - 1)) * terms[s][N...  16.2 us
    dot_general x7, matrix products, matmul(): jnp.dot(low(left_op), low(right_op), preferred_element_type=jnp.float32)  15.9 us
  transfers between devices with their start and end apart: 3, of which 0 were waited for; matrix products, arithmetic and copies ran while one was open for 9% of the time, Pallas kernels for 11%

profile of v3, /device:TPU:0, one launch (start us, length us, event | category | flops | bytes accessed | tf_op | source)
XLA Modules:
  0.0 689.1 jit_solution(632848530821985084)
XLA Ops:
  2.0 2.1 fusion.7
  4.1 3.5 fusion.9.normed
  7.5 2.5 fusion.41.code_attn
  11.2 44.3 %shard_map.392 = (bf16[2048,1024]{1,0:T(8,128)(2,1)S(1)}, bf16[2048,256]{1,0:T(8,128)(2,1)S(1)}, bf16[2048,256]{1,0:T(8,128)(2,1)S(1)}, bf16[64,2048]{1,0:T(8,128)(2,1)S(1)}) custom-call(bf16[512,1024]{1,0:T(8,128)(2,1)S(1)} %copy-done.5, bf16[512,256]{1,0:T(8,128)(2,1)S(1)} %copy-done.6, bf16[512,256]{1,0:T(8,128)(2,1)S(1)} %copy-done.7, ...), custom_call_target="tpu_custom_call" | custom-call | tf_op jit(solution)/shard_map/pallas_call | solution.py:928
  55.6 2.0 multiply_reduce_fusion.3
  59.2 1.4 constant_dynamic-slice_fusion
  62.9 2.4 multiply_reduce_fusion.2
  67.8 3.7 collective-permute-start
  71.6 1.8 multiply_cosine_fusion
  74.6 1.6 dynamic-slice_bitcast_fusion.3.attn_in
  76.2 1.3 dynamic-slice_bitcast_fusion.11.kv_out
  78.3 5.2 fusion.139
  83.5 1.7 convolution_add_fusion
  85.2 3.2 reshape.585
  88.3 2.2 multiply_reduce_fusion
  90.7 1.6 fusion.19
  92.3 1.9 dynamic-slice_bitcast_fusion.5.down_in
  94.2 1.5 dynamic-slice_bitcast_fusion.6.ffn_in
  95.8 1.4 dynamic-slice_bitcast_fusion.10.out_in
  98.9 1.5 dynamic-slice_bitcast_fusion.7
  104.0 1.7 dynamic-slice_bitcast_fusion.2.gu_out
  106.9 1.6 fusion.138
  109.6 2.2 copy-done.10
  111.8 1.5 fusion.33
  113.4 1.3 copy.187.attended
  114.7 290.4 %shard_map.393 = (bf16[1024,2048]{1,0:T(8,128)(2,1)}, bf16[64,2048]{1,0:T(8,128)(2,1)}, bf16[2048,256]{1,0:T(8,128)(2,1)}, bf16[256,2048]{1,0:T(8,128)(2,1)}, bf...) custom-call(bf16[1024,512]{1,0:T(8,128)(2,1)} %w_output.1, ...), custom_call_target="tpu_custom_call" | custom-call | tf_op jit(solution)/shard_map/pallas_call | solution.py:1165
  405.7 135.9 %shard_map.394 = (bf16[512,2048]{1,0:T(8,128)(2,1)}, bf16[2,4,16,18944]{3,2,1,0:T(8,128)(2,1)}, bf16[256,2048]{1,0:T(8,128)(2,1)}, f32[256,2048]{1,0:T(8,128)}, f32[256,2048]{1,0:T(8,128)}) custom-call(bf16[2048,4096]{1,0:T(8,128)(2,1)} %get-tuple-element.42.full_gate, bf16[2048,4096]{1,0:T(8,128)(2,1)} %get-tuple-element.43.full_up, ...), custom_call_target="tpu_custom_call" | custom-call | flops 25769803776 | bytes 67108864 | tf_op jit(solution)/shard_map/pallas_call | solution.py:659
  541.7 4.8 slice_convert_fusion
  547.2 3.3 slice_convert_fusion.3
  552.2 2.4 fusion.140
  555.8 1.5 copy.191
  557.3 5.1 fusion.36
  562.5 5.3 fusion
  567.8 2.4 fusion.15
  571.6 1.8 multiply_bitcast_fusion
  573.5 1.4 copy-done.17
  575.1 1.4 copy-done.16
  579.3 1.4 collective-permute-start.2
  585.5 3.0 multiply_add_fusion.1
  588.6 4.4 multiply_add_fusion
  593.0 1.9 multiply_add_fusion.3
  599.4 73.2 %shard_map.395 = (bf16[512,2048]{1,0:T(8,128)(2,1)}, bf16[2,4,16,10752]{3,2,1,0:T(8,128)(2,1)}) custom-call(bf16[512,1024]{1,0:T(8,128)(2,1)} %bitcast.381, bf16[512,256]{1,0:T(8,128)(2,1)} %fusion.89.grad_key, bf16[512,256]{1,0:T(8,128)(2,1)} %fusion.59.grad_value, bf16[2048,1024]{1,0:T(8,128)(2,1)} %copy-done.2, bf16[2048,256]{1,0:T(8,128)(2,1)} %copy-done.3, ...), custom_call_target="tpu_custom_call" | custom-call | tf_op jit(solution)/shard_map/pallas_call | solution.py:427
  674.6 1.9 slice_convert_fusion.6
  678.3 2.5 multiply_add_fusion.2
  680.8 1.3 multiply_add_fusion.6
  682.1 2.1 multiply_add_fusion.4
  684.2 2.3 maximum_select_fusion
  686.5 1.3 copy.201
  (222 shorter events, 40.1 us)
Async XLA Ops:
  0.6 96.5 %copy-start = (bf16[1,512,2048]{2,1,0:T(8,128)(2,1)S(1)}, bf16[1,512,2048]{2,1,0:T(8,128)(2,1)}, u32[]{:S(2)}) copy-start(bf16[1,512,2048]{2,1,0:T(8,128)(2,1)} %param.37) | copy-start | bytes 6291460
  0.7 3.4 copy-start.47
  7.5 3.6 copy-start.5
  7.5 3.7 copy-start.6
  7.5 3.7 copy-start.7
  7.5 3.7 copy-start.8
  10.0 73.4 %copy-start.37 = (bf16[512,48]{1,0:T(8,128)(2,1)}, bf16[512,48]{1,0:T(8,128)(2,1)S(1)}, u32[]{:S(2)}) copy-start(bf16[512,48]{1,0:T(8,128)(2,1)S(1)} %fusion.41.code_attn) | copy-start | bytes 147460
  10.0 45.6 %copy-start.14 = (bf16[512,2048]{1,0:T(8,128)(2,1)S(1)}, bf16[512,2048]{1,0:T(8,128)(2,1)}, u32[]{:S(2)}) copy-start(bf16[512,2048]{1,0:T(8,128)(2,1)} %fusion.9.normed) | copy-start | bytes 6291460
  55.5 2.5 copy-start.3
  55.5 7.3 %copy-start.4 = (bf16[2048,256]{1,0:T(8,128)(2,1)}, bf16[2048,256]{1,0:T(8,128)(2,1)S(1)}, u32[]{:S(2)}) copy-start(bf16[2048,256]{1,0:T(8,128)(2,1)S(1)} %get-tuple-element.39.w_value) | copy-start | bytes 3145732
  55.6 46.2 %copy-start.9 = (bf16[64,2048]{1,0:T(8,128)(2,1)}, bf16[64,2048]{1,0:T(8,128)(2,1)S(1)}, u32[]{:S(2)}) copy-start(bf16[64,2048]{1,0:T(8,128)(2,1)S(1)} %get-tuple-element.41.left) | copy-start | bytes 786436
  62.8 2.5 copy-start.19
  62.9 2.5 copy-start.49
  62.9 2.5 copy-start.53
  62.9 2.7 copy-start.62
  65.3 2.5 copy-start.21
  65.3 2.5 copy-start.59
  65.4 2.5 copy-start.51
  66.8 6.6 copy-start.33
  66.9 4.6 copy-start.31
  67.8 37.9 %collective-permute-start = (bf16[2,512,1,256]{3,1,2,0:T(8,128)(2,1)}, bf16[2,512,1,256]{3,1,2,0:T(8,128)(2,1)}, u32[]{:S(2)}, u32[]{:S(2)}) collective-permute-start(bf16[2,512,1,256]{3,1,2,0:T(8,128)(2,1)} %pad_maximum_fusion.7), channel_id=1, source_target_pairs={{0,2},{2,4},{4,6},{1,3},{3,5},{5,7},{8,10},{10,12},{12,14},{9,11},... | collective-permute-start | bytes 1572872 | tf_op jit(solution)/shard_map/ppermute | solution.py:23
  78.3 5.2 copy-start.45
  88.3 2.4 copy-start.61
  90.7 7.5 %copy-start.48 = (bf16[1,512,256]{2,1,0:T(8,128)(2,1)S(1)}, bf16[1,512,256]{2,1,0:T(8,128)(2,1)}, u32[]{:S(2)}) copy-start(bf16[1,512,256]{2,1,0:T(8,128)(2,1)} %param.34) | copy-start | bytes 786436
  92.3 9.5 %copy-start.13 = (bf16[256,2048]{1,0:T(8,128)(2,1)}, bf16[256,2048]{1,0:T(8,128)(2,1)S(1)}, u32[]{:S(2)}) copy-start(bf16[256,2048]{1,0:T(8,128)(2,1)S(1)} %get-tuple-element.66.tokens) | copy-start | bytes 3145732
  92.3 8.1 %copy-start.11 = (f32[512,1024]{1,0:T(8,128)S(1)}, f32[512,1024]{1,0:T(8,128)}, u32[]{:S(2)}) copy-start(f32[512,1024]{1,0:T(8,128)} %convolution_add_fusion) | copy-start | bytes 6291460
  92.3 8.1 %copy-start.55 = (f32[256]{0:T(256)S(1)}, f32[256]{0:T(256)}, u32[]{:S(2)}) copy-start(f32[256]{0:T(256)} %param.55) | copy-start | bytes 3076
  101.7 5.1 copy-start.41
  101.7 5.1 copy-start.43
  101.8 3.9 copy-start.32
  101.8 3.9 copy-start.34
  106.8 2.8 copy-start.35
  108.4 3.4 copy-start.10
  547.2 3.3 copy-start.15
  547.2 3.3 copy-start.40
  547.2 5.0 copy-start.65
  557.2 5.2 copy-start.26
  557.3 5.2 copy-start.36
  557.3 10.5 %slice-start = ((s8[8388608]{0:T(1024)(128)(4,1)}), s8[4194304]{0:T(1024)(128)(4,1)S(1)}, s32[]{:S(2)}) async-start(s8[8388608]{0:T(1024)(128)(4,1)} %bitcast.376), calls=%async_computation | async-start | bytes 8388608
  562.4 5.4 slice-start.1
  567.8 2.5 copy-start.42
  567.8 2.5 copy-start.44
  578.2 2.6 copy-start.28
  578.2 2.6 copy-start.30
  579.3 15.5 %collective-permute-start.2 = (bf16[2,512,1,256]{3,1,2,0:T(8,128)(2,1)S(1)}, bf16[2,512,1,256]{3,1,2,0:T(8,128)(2,1)S(1)}, u32[]{:S(2)}, u32[]{:S(2)}) collective-permute-start(bf16[2,512,1,256]{3,1,2,0:T(8,128)(2,1)S(1)} %fusion.54), channel_id=1, source_target_pairs={{2,0},{4,2},{6,4},{3,1},{5,3},{7,5},{10,8},{12,10},{14,12},{11,9},... | collective-permute-start | bytes 1572872 | tf_op jit(solution)/shard_map/ppermute | solution.py:23
  584.2 99.9 %collective-permute-start.1 = (bf16[256,2048]{1,0:T(8,128)(2,1)S(1)}, bf16[256,2048]{1,0:T(8,128)(2,1)S(1)}, u32[]{:S(2)}, u32[]{:S(2)}) collective-permute-start(bf16[256,2048]{1,0:T(8,128)(2,1)S(1)} %copy-done.39), channel_id=1, source_target_pairs={{0,1},{1,0},{2,3},{3,2},{4,5},{5,4},{6,7},{7,6},{8,9},{9,8},{10,11... | collective-permute-start | bytes 3145736 | tf_op jit(solution)/shard_map/ppermute | solution.py:27
  596.1 2.4 copy-start.58
  596.1 2.4 copy-start.50
  (23 other events, 35.5 us)

commit v4 on v3

--- a/solution.py
+++ b/solution.py
@@ -27,23 +27,6 @@
     return lax.ppermute(array, "tensor", [(0, 1), (1, 0)])
 
 
-def rms_norm(values, scaling):
-    return values * lax.rsqrt(jnp.mean(values * values, axis=-1, keepdims=True) + EPSILON) * scaling
-
-
-def gelu_tanh(values):
-    return jax.nn.gelu(values, approximate=True)
-
-
-def rotate_half(values, cosine, sine_table):
-    middle = values.shape[-1] // 2
-    former = values[..., :middle]
-    latter = values[..., middle:]
-    return jnp.concatenate(
-        [former * cosine - latter * sine_table, latter * cosine + former * sine_table], axis=-1
-    )
-
-
 def rope_tables(positions, head_size):
     frequency = jnp.exp(
         jnp.arange(head_size // 2, dtype=jnp.float32) * (-2.0 * math.log(10000.0) / head_size)
@@ -58,22 +41,6 @@
 
 def wide(values):
     return values.astype(jnp.float32)
-
-
-def matmul(left_op, right_op):
-    return jnp.dot(low(left_op), low(right_op), preferred_element_type=jnp.float32)
-
-
-def matmul_t(left_op, right_op):
-    return lax.dot_general(
-        low(left_op), low(right_op), (((1,), (1,)), ((), ())), preferred_element_type=jnp.float32
-    )
-
-
-def outer(left_op, right_op):
-    return lax.dot_general(
-        low(left_op), low(right_op), (((0,), (0,)), ((), ())), preferred_element_type=jnp.float32
-    )
 
 
 def dot(left, right):
@@ -328,10 +295,11 @@
 
 def tail_kernel(
     shards,
-    grad_query, grad_key, grad_value, w_query, w_key, w_value, code_attn, normed, query_out, kv_out, attn_in,
+    grad_query, w_query, w_key, w_value, code_attn, normed, query_out, kv_out, attn_in,
     out_in_term, out_out_term, tokens, gain_in, grad_comb, grad_normed,
+    own_kv, came_kv, lin_kv, cosine, sine, gain_key,
     input_grad_out, whole,
-    pack, mine, sent, got, result, send_sem, recv_sem, keep_sem, *shared,
+    pack, mine, sent, got, result, grad_key, grad_value, send_sem, recv_sem, keep_sem, *shared,
 ):
     side = lax.axis_index("tensor")
     partner = {"tensor": 1 - side}
@@ -344,6 +312,12 @@
         pack, whole, shared[0], shared[1], shared[2], shared[3], shared[4:], shards
     )
     greet_all(shards, [partner, {"context": across}, {"context": beside}], True)
+    keys = grad_key.shape[1]
+    values = lin_kv[:, :keys]
+    turned = unrotate(own_kv[0] + wide(came_kv[0]), cosine[...], sine[...]) * gain_key[...]
+    grad_key[...] = low(rms_back(values, inverse_rms(values), turned))
+    values = lin_kv[:, keys:]
+    grad_value[...] = low(rms_back(values, inverse_rms(values), own_kv[1] + wide(came_kv[1])))
     parts = ((grad_query, w_query, query_out[...]), (grad_key, w_key, kv_out[0]), (grad_value, w_value, kv_out[1]))
     at = 0
 
@@ -392,6 +366,7 @@
         mine[rows(k), :] = product(rows_of(side, k))
         if k == 0:
             settle()
+    hop(1)
     ends = []
     for k in range(2):
         swaps[k].wait_recv()
@@ -403,8 +378,7 @@
         ends.append(send(result.at[there, :], result.at[there, :], 2 + k))
         ends[k].start()
         if k == 0:
-            hop(1)
-    hops(2)
+            hops(2)
     cross_over()
     spread()
     for end in ends:
@@ -418,10 +392,11 @@
 
 
 def tail(arrays, shards):
-    count, width = arrays[7].shape
-    rank = arrays[8].shape[0]
+    count, width = arrays[5].shape
+    rank = arrays[6].shape[0]
     half = count // 2
-    columns = sum(a.shape[1] for a in arrays[:3]) + arrays[11].shape[1] + arrays[12].shape[1] + 3 * width
+    queries, keys = arrays[0].shape[1], arrays[2].shape[1]
+    columns = 2 * queries + 2 * keys + 4 * width
     bf16, f32 = jnp.bfloat16, jnp.float32
     anywhere, vmem = pl.BlockSpec(memory_space=pl.ANY), pl.BlockSpec(memory_space=pltpu.VMEM)
     return pl.pallas_call(
@@ -438,15 +413,307 @@
             pltpu.VMEM((half, width), bf16),
             pltpu.VMEM((half, width), bf16),
             pltpu.VMEM((count, width), bf16),
+            pltpu.VMEM((count, keys), bf16),
+            pltpu.VMEM((count, keys), bf16),
             pltpu.SemaphoreType.DMA((4,)),
             pltpu.SemaphoreType.DMA((4,)),
             pltpu.SemaphoreType.DMA,
         ]
         + sharer_scratch(rank, columns, shards),
         compiler_params=pltpu.CompilerParams(
-            collective_id=3, has_side_effects=True, vmem_limit_bytes=56 * 2**20
+            collective_id=3, has_side_effects=True, vmem_limit_bytes=60 * 2**20
         ),
     )(*arrays)
+
+
+def allowed_bias(seg_rows, seg_cols, keys):
+    count = seg_rows.shape[0]
+    shape = (count, keys)
+    distance = lax.broadcasted_iota(jnp.int32, shape, 0) + (keys - count) - lax.broadcasted_iota(jnp.int32, shape, 1)
+    seen = (seg_rows[...] == seg_cols[...]) & (distance >= 0) & (distance < WINDOW)
+    return jnp.where(seen, 0.0, -1e30)
+
+
+def attend_kernel(scale, query, prior, own, seg_rows, seg_cols, attended, log_total, bias):
+    count = query.shape[0]
+
+    @pl.when(pl.program_id(0) == 0)
+    def _():
+        bias[...] = allowed_bias(seg_rows, seg_cols, 2 * count)
+
+    early = dot_t(query[...], prior[0]) * scale + bias[:, :count]
+    later = dot_t(query[...], own[0]) * scale + bias[:, count:]
+    top = jnp.maximum(jnp.max(early, axis=-1, keepdims=True), jnp.max(later, axis=-1, keepdims=True))
+    early, later = jnp.exp(early - top), jnp.exp(later - top)
+    total = jnp.sum(early, axis=-1, keepdims=True) + jnp.sum(later, axis=-1, keepdims=True)
+    log_total[...] = top + jnp.log(total)
+    attended[...] = low(dot(low(early / total), prior[1]) + dot(low(later / total), own[1]))
+
+
+def attend(query, prior, own, seg_rows, seg_cols, head, scale):
+    count, inner = query.shape
+    heads = inner // head
+    return pl.pallas_call(
+        functools.partial(attend_kernel, scale),
+        grid=(heads,),
+        in_specs=[
+            pl.BlockSpec((count, head), lambda h: (0, h)),
+            pl.BlockSpec((2, count, head), lambda h: (0, 0, 0)),
+            pl.BlockSpec((2, count, head), lambda h: (0, 0, 0)),
+            pl.BlockSpec((count, 1), lambda h: (0, 0)),
+            pl.BlockSpec((1, 2 * count), lambda h: (0, 0)),
+        ],
+        out_specs=[
+            pl.BlockSpec((count, head), lambda h: (0, h)),
+            pl.BlockSpec((None, count, 1), lambda h: (h, 0, 0)),
+        ],
+        out_shape=[
+            jax.ShapeDtypeStruct((count, inner), jnp.bfloat16),
+            jax.ShapeDtypeStruct((heads, count, 1), jnp.float32),
+        ],
+        scratch_shapes=[pltpu.VMEM((count, 2 * count), jnp.float32)],
+        compiler_params=pltpu.CompilerParams(vmem_limit_bytes=56 * 2**20),
+    )(query, prior, own, seg_rows, seg_cols)
+
+
+def unrotate(grad, cosine, sine):
+    middle = grad.shape[1] // 2
+    former, latter = grad[:, :middle], grad[:, middle:]
+    return jnp.concatenate([former * cosine + latter * sine, latter * cosine - former * sine], axis=1)
+
+
+def attend_back_kernel(
+    scale, grad, w_out, out_in, out_out, code_out, attended, query, prior, own, log_total, seg_rows, seg_cols, lin,
+    cosine, sine, gain_query,
+    grad_query, sent_kv, own_kv, term_in, term_out, bias, back, grad_k, grad_v,
+):
+    count = query.shape[0]
+    head = pl.program_id(0)
+
+    @pl.when(head == 0)
+    def _():
+        bias[...] = allowed_bias(seg_rows, seg_cols, 2 * count)
+        back[...] = low(dot_t(grad[...], out_out[...]))
+        term_out[...] = dot_o(code_out[...], grad[...])
+        grad_k[...] = jnp.zeros_like(grad_k)
+        grad_v[...] = jnp.zeros_like(grad_v)
+
+    top = low(dot_t(grad[...], w_out[...]) + dot(back[...], out_in[...]))
+    term_in[...] = dot_o(back[...], attended[...])
+    probs, slopes, mean = [], [], 0.0
+    for i, kv in enumerate((prior, own)):
+        score = dot_t(query[...], kv[0]) * scale + bias[:, i * count : (i + 1) * count]
+        probs.append(jnp.exp(score - log_total[...]))
+        slopes.append(dot_t(top, kv[1]))
+        mean += jnp.sum(probs[i] * slopes[i], axis=-1, keepdims=True)
+    turned = 0.0
+    for i, kv in enumerate((prior, own)):
+        grad_score = low(probs[i] * (slopes[i] - mean))
+        turned += dot(grad_score, kv[0])
+        grad_k[i] += dot_o(grad_score, query[...]) * scale
+        grad_v[i] += dot_o(low(probs[i]), top)
+    values = lin[...]
+    turned = unrotate(turned * scale, cosine[...], sine[...]) * gain_query[...]
+    grad_query[...] = low(rms_back(values, inverse_rms(values), turned))
+
+    @pl.when(head == pl.num_programs(0) - 1)
+    def _():
+        sent_kv[0] = low(grad_k[0])
+        sent_kv[1] = low(grad_v[0])
+        own_kv[0] = grad_k[1]
+        own_kv[1] = grad_v[1]
+
+
+def attend_back(
+    grad, w_out, out_in, out_out, code_out, attended, query, prior, own, log_total, seg_rows, seg_cols, lin,
+    cosine, sine, gain_query, scale,
+):
+    count, inner = query.shape
+    width = grad.shape[1]
+    head = gain_query.shape[1]
+    rank = out_in.shape[0]
+    bf16, f32 = jnp.bfloat16, jnp.float32
+    whole = lambda *shape: pl.BlockSpec(shape, lambda h: (0,) * len(shape))
+    column = lambda rows: pl.BlockSpec((rows, head), lambda h: (0, h))
+    return pl.pallas_call(
+        functools.partial(attend_back_kernel, scale),
+        grid=(inner // head,),
+        in_specs=[
+            whole(count, width),
+            pl.BlockSpec((head, width), lambda h: (h, 0)),
+            column(rank),
+            whole(rank, width),
+            whole(count, rank),
+            column(count),
+            column(count),
+            whole(2, count, head),
+            whole(2, count, head),
+            pl.BlockSpec((None, count, 1), lambda h: (h, 0, 0)),
+            whole(count, 1),
+            whole(1, 2 * count),
+            column(count),
+            whole(count, head // 2),
+            whole(count, head // 2),
+            whole(1, head),
+        ],
+        out_specs=[column(count), whole(2, count, head), whole(2, count, head), column(rank), whole(rank, width)],
+        out_shape=[
+            jax.ShapeDtypeStruct((count, inner), bf16),
+            jax.ShapeDtypeStruct((2, count, head), bf16),
+            jax.ShapeDtypeStruct((2, count, head), f32),
+            jax.ShapeDtypeStruct((rank, inner), f32),
+            jax.ShapeDtypeStruct((rank, width), f32),
+        ],
+        scratch_shapes=[
+            pltpu.VMEM((count, 2 * count), f32),
+            pltpu.VMEM((count, rank), bf16),
+            pltpu.VMEM((2, count, head), f32),
+            pltpu.VMEM((2, count, head), f32),
+        ],
+        compiler_params=pltpu.CompilerParams(vmem_limit_bytes=56 * 2**20),
+    )(
+        grad, w_out, out_in, out_out, code_out, attended, query, prior, own, log_total, seg_rows, seg_cols, lin,
+        cosine, sine, gain_query,
+    )
+
+
+def tables_kernel(
+    queries, keys, early, late, output_own, output_other,
+    output, out_attn, out_query, out_kv, out_out_in, out_out_out, out_ffn, out_gu, out_down_in, out_down_out,
+    marks, drawn, laid, mark_sem, drawn_sem, laid_sem, output_sem,
+):
+    side = lax.axis_index("tensor")
+    shards, rank = early.shape[1], early.shape[2]
+    half, width = output_own.shape
+    puts = []
+    for i, (rows, owner) in enumerate(((output_own, side), (output_other, 1 - side))):
+        there = output.at[pl.ds(pl.multiple_of(owner * half, half), half), :]
+        puts.append(pltpu.make_async_copy(rows, there, output_sem.at[i]))
+        puts[i].start()
+    adapters, hidden = out_gu.shape[0], out_gu.shape[3] // 2
+    wide_at = early.shape[3] - 512
+    get_marks = pltpu.make_async_copy(early.at[0, :, :, pl.ds(wide_at, 128)], marks, mark_sem)
+    get_marks.start()
+    span = drawn.shape[4]
+    def both(source, at, columns, table, inner):
+        found = []
+        for first in range(0, columns, span):
+            size = min(span, columns - first)
+            found.append(
+                (source, at + first, size, [table(t * inner + first, size) for t in range(2)])
+            )
+        return found
+
+    def gu_table(i):
+        return lambda at, size: out_gu.at[:, i, :, pl.ds(at, size)]
+
+    def kv_table(i):
+        return lambda at, size: out_kv.at[:, i, :, pl.ds(at, size)]
+
+    def plain(out, row=0):
+        return lambda at, size: out.at[:, pl.ds(row, rank), pl.ds(at, size)]
+
+    def single(source, at, out, row=0):
+        return [
+            (source, at + first, span, [plain(out, row)(first, span)]) for first in range(0, width, span)
+        ]
+
+    early_units = both(early, 0, hidden, gu_table(0), hidden) + both(early, hidden, hidden, gu_table(1), hidden)
+    early_units += both(early, 2 * hidden, hidden, plain(out_down_in), hidden)
+    early_units += single(early, 3 * hidden, out_ffn) + single(early, 3 * hidden + width, out_ffn, rank)
+    early_units += single(early, 3 * hidden + 2 * width, out_down_out)
+    late_units = both(late, 0, queries, plain(out_out_in), queries) + single(late, queries, out_out_out)
+    late_units += both(late, queries + width, queries, plain(out_query), queries)
+    late_units += both(late, 2 * queries + width, keys, kv_table(0), keys)
+    late_units += both(late, 2 * queries + width + keys, keys, kv_table(1), keys)
+    for i in range(3):
+        late_units += single(late, 2 * queries + (1 + i) * width + 2 * keys, out_attn, i * rank)
+    units = early_units + late_units
+
+    def draw(u):
+        source, at, size, _ = units[u]
+        return pltpu.make_async_copy(
+            source.at[:, :, :, pl.ds(at, size)], drawn.at[u % 2, :, :, :, pl.ds(0, size)], drawn_sem.at[u % 2]
+        )
+
+    def lays(u):
+        _, _, size, targets = units[u]
+        return [
+            pltpu.make_async_copy(laid.at[u % 2, t, :, :, pl.ds(0, size)], target, laid_sem.at[u % 2, t])
+            for t, target in enumerate(targets)
+        ]
+
+    def lay_out(u, last):
+        if u + 1 < last:
+            draw(u + 1).start()
+        draw(u).wait()
+        if u >= 2:
+            for lay in lays(u - 2):
+                lay.wait()
+        _, _, size, targets = units[u]
+        lanes = min(256, size)
+        slot = u % 2
+
+        def one(i, carry):
+            at = pl.ds(pl.multiple_of(i * lanes, lanes), lanes)
+            for t in range(len(targets)):
+                terms = []
+                for q in range(shards):
+                    term = wide(drawn[slot, t, q, :, at])
+                    if len(targets) == 1:
+                        term += wide(drawn[slot, 1, q, :, at])
+                    terms.append(term)
+                for k in range(adapters):
+                    total = terms[0] * wide(marks[0])[:, k : k + 1]
+                    for q in range(1, shards):
+                        total += terms[q] * wide(marks[q])[:, k : k + 1]
+                    laid[slot, t, k, :, at] = total
+            return carry
+
+        lax.fori_loop(0, size // lanes, one, 0)
+        for lay in lays(u):
+            lay.start()
+
+    draw(0).start()
+    get_marks.wait()
+    for u in range(len(units)):
+        lay_out(u, len(units))
+    for u in (len(units) - 2, len(units) - 1):
+        for lay in lays(u):
+            lay.wait()
+    for put in puts:
+        put.wait()
+
+
+def tables(early, late, output_own, output_other, queries, keys, adapters, hidden):
+    half, width = output_own.shape
+    shards, rank = early.shape[1], early.shape[2]
+    span = 2048
+    bf16, f32 = jnp.bfloat16, jnp.float32
+    anywhere, vmem = pl.BlockSpec(memory_space=pl.ANY), pl.BlockSpec(memory_space=pltpu.VMEM)
+    return pl.pallas_call(
+        functools.partial(tables_kernel, queries, keys),
+        out_shape=[jax.ShapeDtypeStruct((2 * half, width), bf16)]
+        + [
+            jax.ShapeDtypeStruct((adapters,) + rest, f32)
+            for rest in (
+                (3 * rank, width), (rank, 2 * queries), (2, rank, 2 * keys), (rank, 2 * queries), (rank, width),
+                (2 * rank, width), (2, rank, 2 * hidden), (rank, 2 * hidden), (rank, width),
+            )
+        ],
+        in_specs=[anywhere] * 2 + [vmem] * 2,
+        out_specs=[anywhere] * 10,
+        scratch_shapes=[
+            pltpu.VMEM((shards, rank, 128), bf16),
+            pltpu.VMEM((2, 2, shards, rank, span), bf16),
+            pltpu.VMEM((2, 2, adapters, rank, span), f32),
+            pltpu.SemaphoreType.DMA,
+            pltpu.SemaphoreType.DMA((2,)),
+            pltpu.SemaphoreType.DMA((2, 2)),
+            pltpu.SemaphoreType.DMA((2,)),
+        ],
+        compiler_params=pltpu.CompilerParams(vmem_limit_bytes=60 * 2**20),
+    )(early, late, output_own, output_other)
 
 
 def aft_kernel(
@@ -891,52 +1158,146 @@
     return shapes
 
 
-def gather_kernel(axes, shards, *refs):
-    count = len(axes)
-    sources, fulls, held = refs[:count], refs[count : 2 * count], refs[2 * count : 3 * count]
-    load_sem, store_sem = refs[3 * count : 3 * count + 2]
-    greet, begin, relay, spread, finish, flush, own_place = mover(
-        sources, fulls, refs[3 * count + 2 :], shards
-    )
+def pick_kernel(chosen, *refs):
+    count = len(refs) // 2
+    for source, target in zip(refs[:count], refs[count:]):
+        if len(source.shape) > len(target.shape):
+            target[...] = source[0]
+        else:
+            target[...] = source[...]
+
+
+def pick_rows(chosen, side, tables, arrays):
+    in_specs, out_specs, shapes = [], [], []
+    for t in tables:
+        rest = t.shape[1:]
+        in_specs.append(pl.BlockSpec((1,) + rest, lambda i, at, n=len(rest): (at[0],) + (0,) * n))
+        out_specs.append(pl.BlockSpec(rest, lambda i, at, n=len(rest): (0,) * n))
+        shapes.append(jax.ShapeDtypeStruct(rest, t.dtype))
+    for a in arrays:
+        part = (a.shape[0] // 2, a.shape[1])
+        in_specs.append(pl.BlockSpec(part, lambda i, at: (at[1], 0)))
+        out_specs.append(pl.BlockSpec(part, lambda i, at: (0, 0)))
+        shapes.append(jax.ShapeDtypeStruct(part, a.dtype))
+    return pl.pallas_call(
+        pick_kernel,
+        grid_spec=pltpu.PrefetchScalarGridSpec(
+            num_scalar_prefetch=1, grid=(1,), in_specs=in_specs, out_specs=out_specs
+        ),
+        out_shape=shapes,
+        compiler_params=pltpu.CompilerParams(vmem_limit_bytes=61 * 2**20),
+    )(jnp.stack([chosen, side]), *tables, *arrays)
+
+
+FRONT_AXES = (0, 0, 0, 1)
+
+
+def front_kernel(
+    shards, w_query, w_key, w_value, w_left, tokens, attn_in, query_out, kv_out, cosine, sine, gain_in, gain_query, gain_key,
+    full_query, full_key, full_value, full_left,
+    normed, code_attn, lin, lin_kv, query_rot, kv_rot,
+    held_query, held_key, held_value, held_left, query_w, key_w, value_w, load_sem, store_sem, weight_sem, *semaphores,
+):
+    sources, fulls = (w_query, w_key, w_value, w_left), (full_query, full_key, full_value, full_left)
+    held = (held_query, held_key, held_value, held_left)
+    greet, begin, relay, spread, finish, flush, own_place = mover(sources, fulls, semaphores, shards)
     pieces = [
-        [(i, i, axes[i], 0, sources[i].shape[0], 0, sources[i].shape[1])] for i in range(count)
+        [(i, i, FRONT_AXES[i], 0, sources[i].shape[0], 0, sources[i].shape[1])] for i in range(4)
     ]
     greet()
     for piece in pieces:
         begin(piece)
-    loads = [pltpu.make_async_copy(sources[i], held[i], load_sem.at[i]) for i in range(count)]
-    stores = [pltpu.make_async_copy(held[i], own_place(i, axes[i]), store_sem.at[i]) for i in range(count)]
+    loads = [pltpu.make_async_copy(sources[i], held[i], load_sem.at[i]) for i in range(4)]
+    stores = [pltpu.make_async_copy(held[i], own_place(i, FRONT_AXES[i]), store_sem.at[i]) for i in range(4)]
     for load in loads:
         load.start()
     for load, store in zip(loads, stores):
         load.wait()
         store.start()
-    for piece in pieces:
+    count = tokens.shape[0]
+    rows = 64
+
+    def norm(i, carry):
+        at = pl.ds(pl.multiple_of(i * rows, rows), rows)
+        token = wide(tokens[at, :])
+        normed[at, :] = low(token * inverse_rms(token) * gain_in[...])
+        return carry
+
+    for k, piece in enumerate(pieces):
         relay(piece)
+        if k == 0:
+            lax.fori_loop(0, count // rows, norm, 0)
+            code_attn[...] = low(dot_t(normed[...], attn_in[...]))
     for piece in pieces:
         spread(piece)
     for piece in pieces:
         finish(piece)
+    for store in stores:
+        store.wait()
+    bring = [
+        pltpu.make_async_copy(full, w, weight_sem.at[i])
+        for i, (full, w) in enumerate(zip(fulls[:3], (query_w, key_w, value_w)))
+    ]
+    for copy in bring:
+        copy.start()
+    head = gain_query.shape[1]
+    middle = head // 2
+    rank = query_out.shape[0]
+    queries, keys = query_w.shape[1], key_w.shape[1]
+
+    def rotate(values, target, at):
+        former, latter = values[:, :middle], values[:, middle:]
+        target[:, at : at + middle] = low(former * cosine[...] - latter * sine[...])
+        target[:, at + middle : at + head] = low(latter * cosine[...] + former * sine[...])
+
+    bring[0].wait()
+    for h in range(queries // head):
+        at = slice(h * head, (h + 1) * head)
+        values = dot(normed[...], query_w[:, at]) + dot(code_attn[:, :rank], query_out[:, at])
+        lin[:, at] = values
+        rotate(values * inverse_rms(values) * gain_query[...], query_rot, h * head)
+    bring[1].wait()
+    bring[2].wait()
+    for h in range(keys // head):
+        at = slice(h * head, (h + 1) * head)
+        values = dot(normed[...], key_w[:, at]) + dot(code_attn[:, rank : 2 * rank], kv_out[0, :, at])
+        lin_kv[:, at] = values
+        rotate(values * inverse_rms(values) * gain_key[...], kv_rot.at[0], h * head)
+        values = dot(normed[...], value_w[:, at]) + dot(code_attn[:, 2 * rank :], kv_out[1, :, at])
+        lin_kv[:, keys + h * head : keys + (h + 1) * head] = values
+        kv_rot[1, :, at] = low(values * inverse_rms(values))
     for piece in pieces:
         flush(piece)
-    for store in stores:
-        store.wait()
-
-
-def gather(weights, axes, shards):
-    count = len(weights)
+
+
+def front(weights, arrays, shards):
+    count, width = arrays[0].shape
+    queries, keys = weights[0].shape[1], weights[1].shape[1]
+    rank = arrays[2].shape[0]
+    bf16, f32 = jnp.bfloat16, jnp.float32
+    shape = jax.ShapeDtypeStruct
+    anywhere, vmem = pl.BlockSpec(memory_space=pl.ANY), pl.BlockSpec(memory_space=pltpu.VMEM)
     return pl.pallas_call(
-        functools.partial(gather_kernel, axes, shards),
-        out_shape=full_shapes(weights, axes, shards),
-        in_specs=[pl.BlockSpec(memory_space=pl.ANY)] * count,
-        out_specs=[pl.BlockSpec(memory_space=pl.ANY)] * count,
+        functools.partial(front_kernel, shards),
+        out_shape=full_shapes(weights, FRONT_AXES, shards)
+        + [
+            shape((count, width), bf16),
+            shape((count, 3 * rank), bf16),
+            shape((count, queries), f32),
+            shape((count, 2 * keys), f32),
+            shape((count, queries), bf16),
+            shape((2, count, keys), bf16),
+        ],
+        in_specs=[anywhere] * 4 + [vmem] * len(arrays),
+        out_specs=[anywhere] * 4 + [vmem] * 6,
         scratch_shapes=[pltpu.VMEM(w.shape, w.dtype) for w in weights]
-        + [pltpu.SemaphoreType.DMA((count,)), pltpu.SemaphoreType.DMA((count,))]
-        + mover_semaphores(count, shards),
+        + [pltpu.VMEM((width, n), bf16) for n in (queries, keys, keys)]
+        + [pltpu.SemaphoreType.DMA((4,)), pltpu.SemaphoreType.DMA((4,)), pltpu.SemaphoreType.DMA((3,))]
+        + mover_semaphores(4, shards),
         compiler_params=pltpu.CompilerParams(
-            collective_id=0, has_side_effects=True, vmem_limit_bytes=32 * 2**20
+            collective_id=0, has_side_effects=True, vmem_limit_bytes=60 * 2**20
         ),
-    )(*weights)
+    )(*weights, *arrays)
 
 
 FORE_AXES = (1, 1, 0, 1, 0, 0, 1)
@@ -945,10 +1306,10 @@
 def fore_kernel(
     shards, block,
     w_output, w_right, w_lgate, w_lproj, w_gate, w_up, w_down,
-    attended, tokens, laurel_mid, out_in, out_out, ffn_in, gu_out, down_in, down_out,
+    attended, tokens, left, out_in, out_out, ffn_in, gu_out, down_in, down_out,
     gain_in, gain_attn, gain_laurel, gain_pre,
     full_output, full_right, full_lgate, full_lproj, full_gate, full_up, full_down, gate_out, up_out, ffn_out,
-    attn_proj, combined, code_out, code_ffn, code_down, part,
+    attn_proj, combined, laurel_mid, code_out, code_ffn, code_down, part,
     stage_a, stage_b, stage_c, stage_d, stage_e, stage_f, stage_g, out_w, right_w, gate_w, up_w, down_w, sent, got, ffn, total, codes, hidden,
     gate_keep, up_keep,
     load_sem, store_sem, weight_sem, keep_sem, ffn_sem, swap_send, swap_recv, *semaphores,
@@ -1025,7 +1386,9 @@
         attn_proj[at, :] = proj
         token = wide(tokens[at, :])
         normed = token * inverse_rms(token) * gain_in[...]
-        end = dot(laurel_mid[at, :], right_w[...])
+        mid = low(dot_t(low(normed), left[...]))
+        laurel_mid[at, :] = mid
+        end = dot(mid, right_w[...])
         comb = (
             token + proj * inverse_rms(proj) * gain_attn[...] + normed + end * inverse_rms(end) * gain_laurel[...]
         ) * ROOT_HALF
@@ -1150,7 +1513,7 @@
 
 
 def fore(
-    weights, attended, tokens, laurel_mid, out_in, out_out, ffn_in, gu_out, down_in, down_out, gains, shards
+    weights, attended, tokens, left, out_in, out_out, ffn_in, gu_out, down_in, down_out, gains, shards
 ):
     count = attended.shape[0]
     width = tokens.shape[1]
@@ -1171,13 +1534,14 @@
             shape((count, width), bf16),
             shape((half, width), f32),
             shape((half, width), f32),
+            shape((half, left.shape[0]), bf16),
             shape((count, rank), bf16),
             shape((count, 2 * rank), bf16),
             shape((count, rank), bf16),
             shape((count, width), bf16),
         ],
         in_specs=[anywhere] * 7 + [vmem] * 13,
-        out_specs=[anywhere] * 10 + [vmem] * 6,
+        out_specs=[anywhere] * 10 + [vmem] * 7,
         scratch_shapes=[
             *[pltpu.VMEM(w.shape, bf16) for w in weights],
             pltpu.VMEM((weights[0].shape[0], width), bf16),
@@ -1205,7 +1569,7 @@
         compiler_params=pltpu.CompilerParams(
             collective_id=1, has_side_effects=True, vmem_limit_bytes=60 * 2**20
         ),
-    )(*weights, attended, tokens, laurel_mid, out_in, out_out, ffn_in, gu_out, down_in, down_out, *gains)
+    )(*weights, attended, tokens, left, out_in, out_out, ffn_in, gu_out, down_in, down_out, *gains)
 
 
 def body(
@@ -1250,34 +1614,28 @@
     rank = adapt_query_out.shape[1]
     heads = adapt_query_out.shape[2] // head_size
     kv_heads = adapt_kv_out.shape[3] // head_size
-    group = heads // kv_heads
+    assert kv_heads == 1
     side = lax.axis_index("tensor")
     place = lax.axis_index("context")
     shards = lax.axis_size("shard")
 
-    full_query, full_key, full_value, full_left = gather(
-        (w_query, w_key, w_value, laurel_left.T), (0, 0, 0, 1), shards
-    )
     hidden_here = w_gate.shape[1]
     chosen = adapter_ids[0]
 
-    def pick(table):
-        return lax.dynamic_index_in_dim(table, chosen, 0, keepdims=False)
-
-    pick_attn_in, pick_query_out, pick_kv_out = pick(adapt_attn_in), pick(adapt_query_out), pick(adapt_kv_out)
-    pick_out_in, pick_out_out, pick_ffn_in = pick(adapt_out_in), pick(adapt_out_out), pick(adapt_ffn_in)
-    pick_gu_out, pick_down_in, pick_down_out = pick(adapt_gu_out), pick(adapt_down_in), pick(adapt_down_out)
-
-    def own_half(array):
-        return lax.dynamic_slice_in_dim(array, side * half, half, 0)
-
-    def other_half(array):
-        return lax.dynamic_slice_in_dim(array, (1 - side) * half, half, 0)
-
-    def in_order(own, other):
-        return jnp.where(
-            side == 0, jnp.concatenate([own, other], axis=0), jnp.concatenate([other, own], axis=0)
-        )
+    def turned(table):
+        return table.transpose(0, 2, 1)
+
+    (
+        pick_attn_in, pick_query_out, pick_kv_out, pick_out_in, pick_out_out, pick_ffn_in, pick_gu_out,
+        pick_down_in, pick_down_out, tokens_own, per_layer_own, cotangent_own,
+    ) = pick_rows(
+        chosen, side,
+        [
+            turned(adapt_attn_in), adapt_query_out, adapt_kv_out, turned(adapt_out_in), adapt_out_out,
+            turned(adapt_ffn_in), adapt_gu_out, turned(adapt_down_in), adapt_down_out,
+        ],
+        [tokens[0], layer_input[0], cotangent[0]],
+    )
 
     start_pos = place * count
     seg_all = segments[0]
@@ -1285,65 +1643,29 @@
     before = jnp.sum((seg_all[None, :] < seg_query[:, None]).astype(jnp.int32), axis=1)
     own_pos = start_pos + jnp.arange(count, dtype=jnp.int32) - before
     cosine, sine_table = rope_tables(own_pos, head_size)
-    cosine = cosine[:, None, :]
-    sine_table = sine_table[:, None, :]
-    tokens_f = wide(tokens[0])
-    normed_b = low(rms_norm(tokens_f, gain_in))
-    tokens_h = wide(own_half(tokens[0]))
-    normed_h = rms_norm(tokens_h, gain_in)
-    code_attn = matmul(normed_b, pick_attn_in)
-    query_lin = matmul(normed_b, full_query) + matmul(code_attn[:, :rank], pick_query_out)
-    key_lin = matmul(normed_b, full_key) + matmul(code_attn[:, rank : 2 * rank], pick_kv_out[0])
-    value_lin = matmul(normed_b, full_value) + matmul(code_attn[:, 2 * rank :], pick_kv_out[1])
-
-    def prepare(query_in, key_in, value_in):
-        query_rot = rotate_half(
-            rms_norm(query_in.reshape(count, heads, head_size), gain_query), cosine, sine_table
-        )
-        key_rot = rotate_half(
-            rms_norm(key_in.reshape(count, kv_heads, head_size), gain_key), cosine, sine_table
-        )
-        value_nrm = rms_norm(value_in.reshape(count, kv_heads, head_size), 1.0)
-        return (query_rot, key_rot, value_nrm)
-
-    (query_rot, key_rot, value_nrm), prepare_back = jax.vjp(prepare, query_lin, key_lin, value_lin)
-    query_b = low(query_rot).reshape(count, kv_heads, group, head_size)
-    kv_own = low(jnp.stack([key_rot, value_nrm]))
+    (
+        full_query, full_key, full_value, full_left, normed_b, code_attn, lin, lin_kv, query_rot, kv_own,
+    ) = front(
+        (w_query, w_key, w_value, laurel_left.T),
+        (
+            tokens[0], pick_attn_in, pick_query_out, pick_kv_out, cosine, sine_table,
+            gain_in[None], gain_query[None], gain_key[None],
+        ),
+        shards,
+    )
     kv_prior = shifted(kv_own, "context", 1)
-    kv_all = jnp.concatenate([kv_prior, kv_own], axis=1)
-    query_pos = start_pos + jnp.arange(count, dtype=jnp.int32)
-    key_pos = start_pos - count + jnp.arange(2 * count, dtype=jnp.int32)
     seg_prior = lax.dynamic_slice_in_dim(seg_all, jnp.maximum(start_pos - count, 0), count, 0)
-    seg_keys = jnp.concatenate([seg_prior, seg_query], axis=0)
-    distance = query_pos[:, None] - key_pos[None, :]
-    window_ok = (distance >= 0) & (distance < WINDOW) & (key_pos >= 0)[None, :]
-    allowed = (seg_query[:, None] == seg_keys[None, :]) & window_ok
-    allowed = allowed[None, None]
+    seg_cols = jnp.concatenate([jnp.where(place > 0, seg_prior, -1), seg_query])[None, :]
+    seg_rows = seg_query[:, None]
     score_scale = 1.0 / math.sqrt(head_size)
-
-    def masked_scores():
-        raw_scores = (
-            jnp.einsum("lkgd,mkd->kglm", query_b, kv_all[0], preferred_element_type=jnp.float32)
-            * score_scale
-        )
-        return jnp.where(allowed, raw_scores, -1e30)
-
-    scores = masked_scores()
-    row_max = jnp.max(scores, axis=-1, keepdims=True)
-    exponent = jnp.exp(scores - row_max)
-    row_total = jnp.sum(exponent, axis=-1, keepdims=True)
-    log_total = row_max + jnp.log(row_total)
-    attn_probs = low(exponent / row_total)
-    attended = jnp.einsum("kglm,mkd->lkgd", attn_probs, kv_all[1], preferred_element_type=jnp.float32)
-    attended_b = low(attended.reshape(count, heads * head_size))
-    laurel_mid = low(matmul_t(normed_h, full_left))
+    attended_b, log_total = attend(query_rot, kv_prior, kv_own, seg_rows, seg_cols, head_size, score_scale)
     (
         full_output, full_right, full_layer_gate, full_layer_proj, full_gate, full_up, full_down,
-        gate_b, up_b, ffn_b, attn_proj, combined, code_out, code_ffn, code_down, down_part,
+        gate_b, up_b, ffn_b, attn_proj, combined, laurel_mid, code_out, code_ffn, code_down, down_part,
     ) = fore(
         (w_output, laurel_right, input_gate, input_proj, w_gate, w_up, w_down),
-        attended_b, own_half(tokens[0]), laurel_mid,
-        pick_out_in.T, pick_out_out, pick_ffn_in.T, pick_gu_out, pick_down_in.T, pick_down_out,
+        attended_b, tokens_own, full_left,
+        pick_out_in, pick_out_out, pick_ffn_in, pick_gu_out, pick_down_in, pick_down_out,
         (gain_in[None], gain_attn[None], gain_laurel[None], gain_pre[None]), shards,
     )
     mark = jnp.where(
@@ -1352,100 +1674,36 @@
     grad_attn_b, early, output_own, grad_inputs, grad_normed = aft(
         (full_gate, full_up, full_down), (gate_b, up_b),
         (
-            down_part, combined, own_half(layer_input[0]), own_half(cotangent[0]), full_layer_gate, full_layer_proj,
-            code_ffn, code_down, ffn_b, pick_down_in.T, pick_down_out, pick_gu_out, pick_ffn_in.T,
+            down_part, combined, per_layer_own, cotangent_own, full_layer_gate, full_layer_proj,
+            code_ffn, code_down, ffn_b, pick_down_in, pick_down_out, pick_gu_out, pick_ffn_in,
             attn_proj, laurel_mid, full_left, full_right, mark,
             gain_post[None], gain_layer[None], gain_pre[None], gain_attn[None], gain_laurel[None],
         ),
         shards,
     )
-    layer_output = in_order(output_own, swap(output_own))
-    code_out_back = matmul_t(grad_attn_b, pick_out_out)
-    term_out_out = outer(code_out, grad_attn_b)
-    term_out_in = outer(code_out_back, attended_b)
-    grad_attended = low(matmul_t(grad_attn_b, full_output) + matmul_t(code_out_back, pick_out_in))
-    grad_heads = grad_attended.reshape(count, kv_heads, group, head_size)
-    recomputed = jnp.exp(masked_scores() - log_total)
-    grad_probs = jnp.einsum("lkgd,mkd->kglm", grad_heads, kv_all[1], preferred_element_type=jnp.float32)
-    grad_scores = low(
-        recomputed * (grad_probs - jnp.sum(recomputed * grad_probs, axis=-1, keepdims=True))
+    output_other = swap(output_own)
+    grad_query, sent_kv, own_kv, term_out_in, term_out_out = attend_back(
+        grad_attn_b, full_output, pick_out_in, pick_out_out, code_out, attended_b, query_rot, kv_prior, kv_own,
+        log_total, seg_rows, seg_cols, lin, cosine, sine_table, gain_query[None], score_scale,
     )
-    grad_query = (
-        jnp.einsum("kglm,mkd->lkgd", grad_scores, kv_all[0], preferred_element_type=jnp.float32)
-        * score_scale
-    )
-    grad_keys = (
-        jnp.einsum("kglm,lkgd->mkd", grad_scores, query_b, preferred_element_type=jnp.float32)
-        * score_scale
-    )
-    grad_values = jnp.einsum(
-        "kglm,lkgd->mkd", low(recomputed), grad_heads, preferred_element_type=jnp.float32
-    )
-    grad_kv = jnp.stack([grad_keys, grad_values])
-    grad_kv_later = wide(shifted(low(grad_kv[:, :count]), "context", -1))
-    grad_kv_own = grad_kv[:, count:] + grad_kv_later
-    grad_qlin, grad_klin, grad_vlin = prepare_back(
-        (grad_query.reshape(count, heads, head_size), grad_kv_own[0], grad_kv_own[1])
-    )
-    grad_qlin_b = low(grad_qlin)
-    grad_klin_b = low(grad_klin)
-    grad_vlin_b = low(grad_vlin)
     input_grad, late = tail(
         (
-            grad_qlin_b, grad_klin_b, grad_vlin_b, full_query, full_key, full_value, low(code_attn), normed_b,
-            pick_query_out, pick_kv_out, pick_attn_in.T, term_out_in, term_out_out,
-            own_half(tokens[0]), gain_in[None], grad_inputs, grad_normed,
+            grad_query, full_query, full_key, full_value, code_attn, normed_b,
+            pick_query_out, pick_kv_out, pick_attn_in, term_out_in, term_out_out,
+            tokens_own, gain_in[None], grad_inputs, grad_normed,
+            own_kv, shifted(sent_kv, "context", -1), lin_kv, cosine, sine_table, gain_key[None],
         ),
         shards,
     )
-
-    at = 0
-
-    def take(packed, columns):
-        nonlocal at
-        at += columns
-        return wide(packed[..., at - columns : at])
-
-    def joined(packed, columns):
-        both = take(packed, columns)
-        return jnp.concatenate([both[0], both[1]], axis=-1)
-
-    def added(packed, columns):
-        both = take(packed, columns)
-        return both[0] + both[1]
-
-    gate_out, up_out, down_in = (joined(early, hidden_here) for _ in range(3))
-    ffn_in = [added(early, width) for _ in range(2)]
-    down_out = added(early, width)
-    adapters = adapt_attn_in.shape[0]
-    marks = wide(early[0, :, 0, at : at + adapters])
-    at = 0
-    out_in = joined(late, heads * head_size)
-    out_out = added(late, width)
-    query_out = joined(late, heads * head_size)
-    key_out, value_out = (joined(late, kv_heads * head_size) for _ in range(2))
-    attn_in = [added(late, width) for _ in range(3)]
-
-    def tables(terms):
-        return sum(
-            marks[s].reshape((adapters,) + (1,) * (terms.ndim - 1)) * terms[s][None] for s in range(shards)
-        )
-
-    def turned(terms):
-        return tables(terms).transpose(0, 2, 1)
-
+    (
+        layer_output, table_attn_in, table_query_out, table_kv_out, table_out_in, table_out_out, table_ffn_in,
+        table_gu_out, table_down_in, table_down_out,
+    ) = tables(
+        early, late, output_own, output_other, heads * head_size, kv_heads * head_size, adapt_attn_in.shape[0], hidden_here
+    )
     return (
-        layer_output[None],
-        input_grad[None],
-        turned(jnp.concatenate(attn_in, axis=1)),
-        tables(query_out),
-        tables(jnp.stack([key_out, value_out], axis=1)),
-        turned(out_in),
-        tables(out_out),
-        turned(jnp.concatenate(ffn_in, axis=1)),
-        tables(jnp.stack([gate_out, up_out], axis=1)),
-        turned(down_in),
-        tables(down_out),
+        layer_output[None], input_grad[None], turned(table_attn_in), table_query_out, table_kv_out,
+        turned(table_out_in), table_out_out, turned(table_ffn_in), table_gu_out, turned(table_down_in), table_down_out,
     )
 
 

time: 698 us -> 646 us (0.926)
  Pallas kernels: 544 us -> 619 us
  other arithmetic: 61.1 us -> 5.09 us
  matrix products: 39.9 us -> 0 us
  local copies, waits for them, and re-layouts: 35.6 us -> 5.35 us
    pallas_call x1 -> x5, Pallas kernels: 44.3 us -> 111 us  [the longest x1 56.2 us: front(): pl.pallas_call(functools.partial(front_kernel, shards), out_shape=full_sh...]
    dot_general x19 -> x0, matrix products: 39.9 us -> none  [the longest x7 15.9 us: matmul(): jnp.dot(low(left_op), low(right_op), preferred_element_type=jnp.float32)]
    convert_element_type x9 -> x0, other arithmetic: 17.9 us -> none  [the longest x6 12.7 us: wide(): return values.astype(jnp.float32)]
    add x17 -> x0, other arithmetic: 17.3 us -> none  [the longest x7 16.2 us: tables(): sum((marks[s].reshape((adapters,) + (1,) * (terms.ndim - 1)) * terms[s][N...]
    unnamed x137 -> x9, local copies, waits for them, and re-layouts: 12.2 us -> 3.87 us
    reduce_sum x7 -> x0, other arithmetic: 7.79 us -> none  [the longest x3 5.86 us: rms_norm(): jnp.mean(values * values, axis=-1, keepdims=True) + EPSILON]
  transfers between devices with their start and end apart: 3 -> 3, of which waited for: 0 -> 2; matrix products, arithmetic and copies ran while one was open for 9% -> 0% of each run, Pallas kernels for 11% -> 15%
where the time goes in v4:
time: 646 us; the launch traced here: 639 us
  Pallas kernels  619 us (96%)
    pallas_call x1, Pallas kernels, fore(): pl.pallas_call(functools.partial(fore_kernel, shards, block), out_shape=f...  296 us
    pallas_call x1, Pallas kernels, aft(): pl.pallas_call(functools.partial(aft_kernel, shards, block, strip), out_s...  137 us
    pallas_call x1, Pallas kernels, tail(): pl.pallas_call(functools.partial(tail_kernel, shards), out_shape=[jax.Sha...  75.5 us
    pallas_call x1, Pallas kernels, front(): pl.pallas_call(functools.partial(front_kernel, shards), out_shape=full_sh...  56.2 us
    pallas_call x1, Pallas kernels, tables(): pl.pallas_call(functools.partial(tables_kernel, queries, keys), out_shape...  22.7 us
    pallas_call x1, Pallas kernels, attend_back(): pl.pallas_call(functools.partial(attend_back_kernel, scale), grid=(inner...  19.1 us
  transfers between devices with their start and end apart: 3, of which 2 were waited for; matrix products, arithmetic and copies ran while one was open for 0% of the time, Pallas kernels for 15%

profile of v4, /device:TPU:0, one launch (start us, length us, event | category | flops | bytes accessed | tf_op | source)
XLA Modules:
  0.0 639.3 jit_solution(3294047965630249564)
XLA Ops:
  1.3 0.8 broadcast_select_fusion
  2.2 1.3 convert_reduce_fusion
  3.4 0.6 pad_add_fusion.1.chosen
  4.0 1.8 multiply_sine_fusion
  5.8 4.3 shard_map.392
  10.1 56.2 %shard_map.393 = (bf16[2048,1024]{1,0:T(8,128)(2,1)}, bf16[2048,256]{1,0:T(8,128)(2,1)}, bf16[2048,256]{1,0:T(8,128)(2,1)}, bf16[64,2048]{1,0:T(8,128)(2,1)}, bf...) custom-call(bf16[512,1024]{1,0:T(8,128)(2,1)} %w_query.1, ...), custom_call_target="tpu_custom_call" | custom-call | tf_op jit(solution)/shard_map/pallas_call | solution.py:1280
  66.3 3.4 collective-permute-start
  69.7 0.9 copy.46.seg_rows
  70.5 0.6 pad_add_fusion
  71.1 0.2 collective-permute-done.prior
  71.4 0.0 copy-start.1
  71.4 0.8 copy-done.1
  72.2 8.8 %shard_map.394 = (bf16[512,1024]{1,0:T(8,128)(2,1)}, f32[4,512,1]{2,1,0:T(8,128)}) custom-call(bf16[512,1024]{1,0:T(8,128)(2,1)} %get-tuple-element.77.query, bf16[2,512,256]{2,1,0:T(8,128)(2,1)} %copy-done.1, bf16[2,512,256]{2,1,0:T(8,128)(2,1)} %get-tuple-element.78.own, s32[512,1]{1,0:T(8,128)} %copy.46.seg_rows, s32[1,1024]{1,0:T(1,128)} %bitcast.43), custom_call_target="tpu_custom_call" | custom-call | tf_op jit(solution)/shard_map/pallas_call | solution.py:456
  81.0 295.9 %shard_map.395 = (bf16[1024,2048]{1,0:T(8,128)(2,1)}, bf16[64,2048]{1,0:T(8,128)(2,1)}, bf16[2048,256]{1,0:T(8,128)(2,1)}, bf16[256,2048]{1,0:T(8,128)(2,1)}, bf...) custom-call(bf16[1024,512]{1,0:T(8,128)(2,1)} %w_output.1, ...), custom_call_target="tpu_custom_call" | custom-call | tf_op jit(solution)/shard_map/pallas_call | solution.py:1528
  376.9 0.6 iota.19.mark
  377.5 136.9 %shard_map.396 = (bf16[512,2048]{1,0:T(8,128)(2,1)}, bf16[2,4,16,18944]{3,2,1,0:T(8,128)(2,1)}, bf16[256,2048]{1,0:T(8,128)(2,1)}, f32[256,2048]{1,0:T(8,128)}, f32[256,2048]{1,0:T(8,128)}) custom-call(bf16[2048,4096]{1,0:T(8,128)(2,1)} %get-tuple-element.88.full_gate, bf16[2048,4096]{1,0:T(8,128)(2,1)} %get-tuple-element.89.full_up, ...), custom_call_target="tpu_custom_call" | custom-call | flops 25769803776 | bytes 67108864 | tf_op jit(solution)/shard_map/pallas_call | solution.py:926
  514.4 0.1 collective-permute-start.2
  514.5 19.1 %shard_map.397 = (bf16[512,1024]{1,0:T(8,128)(2,1)}, bf16[2,512,256]{2,1,0:T(8,128)(2,1)}, f32[2,512,256]{2,1,0:T(8,128)}, f32[16,1024]{1,0:T(8,128)}, f32[16,2048]{1,0:T(8,128)}) custom-call(bf16[512,2048]{1,0:T(8,128)(2,1)} %get-tuple-element.106.grad, bf16[1024,2048]{1,0:T(8,128)(2,1)} %get-tuple-element.107.w_out, ...), custom_call_target="tpu_custom_call" | custom-call | tf_op jit(solution)/shard_map/pallas_call | solution.py:538
  533.6 1.3 collective-permute-start.1
  534.9 2.7 collective-permute-done.1.came_kv
  537.6 0.0 copy-start.3
  537.6 0.8 copy-done.3
  538.4 75.5 %shard_map.398 = (bf16[512,2048]{1,0:T(8,128)(2,1)}, bf16[2,4,16,10752]{3,2,1,0:T(8,128)(2,1)}) custom-call(bf16[512,1024]{1,0:T(8,128)(2,1)} %get-tuple-element.111.grad_query, bf16[2048,1024]{1,0:T(8,128)(2,1)} %get-tuple-element.112.w_query, bf16[2048,256]{1,0:T(8,128)(2,1)} %get-tuple-element.113.w_key, bf16[2048,256]{1,0:T(8,128)(2,1)} %get-tuple-element.114.w_value, ...), custom_call_target="tpu_custom_call" | custom-call | tf_op jit(solution)/shard_map/pallas_call | solution.py:402
  613.9 0.0 collective-permute-done.2.output_other
  613.9 0.0 copy-start.2
  613.9 1.0 copy-done.2
  614.8 0.0 copy-start
  614.8 22.7 %shard_map.399 = (bf16[512,2048]{1,0:T(8,128)(2,1)}, f32[8,48,2048]{2,1,0:T(8,128)}, f32[8,16,2048]{2,1,0:T(8,128)}, f32[8,2,16,512]{3,2,1,0:T(8,128)}, f32[8,16...) custom-call(bf16[2,4,16,18944]{3,2,1,0:T(8,128)(2,1)} %get-tuple-ele, ...), custom_call_target="tpu_custom_call" | custom-call | tf_op jit(solution)/shard_map/pallas_call | solution.py:694
  637.6 0.0 copy-done
  637.6 1.3 copy.50
  (3 shorter events, 0.0 us)
Async XLA Ops:
  66.3 5.1 collective-permute-start
  71.4 0.8 copy-start.1
  514.4 99.5 %collective-permute-start.2 = (bf16[256,2048]{1,0:T(8,128)(2,1)}, bf16[256,2048]{1,0:T(8,128)(2,1)S(1)}, u32[]{:S(2)}, u32[]{:S(2)}) collective-permute-start(bf16[256,2048]{1,0:T(8,128)(2,1)} %get-tuple-element.125.output_own), channel_id=1, source_target_pairs={{0,1},{1,0},{2,3},{3,2},{4,5},{5,4},{6,7},{7,6},{8,9},{9,8},{10,11... | collective-permute-start | bytes 3145736 | tf_op jit(solution)/shard_map/ppermute | solution.py:27
  533.6 4.0 collective-permute-start.1
  537.6 0.8 copy-start.3
  613.9 1.0 copy-start.2
  614.8 22.7 %copy-start = (bf16[512,2048]{1,0:T(8,128)(2,1)S(1)}, bf16[512,2048]{1,0:T(8,128)(2,1)}, u32[]{:S(2)}) copy-start(bf16[512,2048]{1,0:T(8,128)(2,1)} %get-tuple-element.127) | copy-start | bytes 6291460

commit v5 on v4

--- a/solution.py
+++ b/solution.py
@@ -132,14 +132,14 @@
     def turned():
         return copy(turn_out, turn_in, pre_send.at[2], pre_recv.at[2], {"context": across})
 
-    def z_copy(s, source, sender, by):
-        return copy(source, region(side, s, c), z_send.at[sender], z_recv.at[s], {"shard": z + by})
-
-    def passed(s, by):
-        return z_copy(s, region(side, s, c), s, by)
-
-    def x_copy(s, source, t):
-        return copy(source, region(t, s, c), x_send.at[s], x_recv.at[s], {"tensor": 1 - side})
+    def z_copy(t, s, source, sender, by):
+        return copy(source, region(t, s, c), z_send.at[t, sender], z_recv.at[t, s], {"shard": z + by})
+
+    def passed(t, s, by):
+        return z_copy(t, s, region(t, s, c), s, by)
+
+    def x_copy(source, t):
+        return copy(source, region(t, z, c), x_send, x_recv, {"tensor": 1 - side})
 
     def y_copy(t, s, source, q):
         return copy(source, region(t, s, q), y_send.at[t, s], y_recv.at[t, s], {"context": across})
@@ -168,60 +168,50 @@
         turned().wait_recv()
         piece[...] = low(pack[:, cols(c)] + inbox[0] + wide(turn_in[...]))
         keep().start()
-
+        x_copy(piece, side).start()
+        set_out(side, piece)
+
+    def set_out(t, source):
         @pl.when(z < shards - 1)
         def _():
-            z_copy(z, piece, z, 1).start()
+            z_copy(t, z, source, z, 1).start()
 
         @pl.when(z > 0)
         def _():
-            z_copy(z, piece, shards, -1).start()
-
-        x_copy(z, piece, side).start()
-        y_copy(side, z, piece, c).start()
-        near_copy(side, z, piece, c).start()
-
-    def hand_on(s):
-        at = region(side, s, c)
-        x_copy(s, at, side).start()
-        y_copy(side, s, at, c).start()
-        near_copy(side, s, at, c).start()
+            z_copy(t, z, source, shards, -1).start()
+
+        y_copy(t, z, source, c).start()
+        near_copy(t, z, source, c).start()
+
+    def cross_over():
+        at = region(1 - side, z, c)
+        x_copy(at, 1 - side).wait_recv()
+        set_out(1 - side, at)
 
     def hop(d):
+        def one(t, s, by, last):
+            passed(t, s, by).wait_recv()
+
+            @pl.when(z != last)
+            def _():
+                passed(t, s, by).start()
+
+            at = region(t, s, c)
+            y_copy(t, s, at, c).start()
+            near_copy(t, s, at, c).start()
+
         @pl.when(z >= d)
         def _():
-            s = z - d
-            passed(s, 1).wait_recv()
-
-            @pl.when(z < shards - 1)
-            def _():
-                passed(s, 1).start()
-
-            hand_on(s)
+            for t in (side, 1 - side):
+                one(t, z - d, 1, shards - 1)
 
         @pl.when(z + d <= shards - 1)
         def _():
-            s = z + d
-            passed(s, -1).wait_recv()
-
-            @pl.when(z > 0)
-            def _():
-                passed(s, -1).start()
-
-            hand_on(s)
+            for t in (side, 1 - side):
+                one(t, z + d, -1, 0)
 
     def hops(first):
         lax.fori_loop(first, shards, lambda d, carry: (hop(d), carry)[1], 0)
-
-    def cross_over():
-        def one(s, carry):
-            at = region(1 - side, s, c)
-            x_copy(s, at, 1 - side).wait_recv()
-            y_copy(1 - side, s, at, c).start()
-            near_copy(1 - side, s, at, c).start()
-            return carry
-
-        lax.fori_loop(0, shards, one, 0)
 
     def every(act):
         def one(s, carry):
@@ -248,28 +238,23 @@
 
         every(act)
 
-        def one(s, carry):
-            x_copy(s, region(side, s, c), side).wait_send()
-
-            @pl.when((s < z) & (z < shards - 1))
+        def sent(t, s):
+            @pl.when((s <= z) & (z < shards - 1))
             def _():
-                passed(s, 1).wait_send()
+                passed(t, s, 1).wait_send()
 
             @pl.when((s > z) & (z > 0))
             def _():
-                passed(s, -1).wait_send()
-
-            return carry
-
-        lax.fori_loop(0, shards, one, 0)
-
-        @pl.when(z < shards - 1)
-        def _():
-            z_copy(z, piece, z, 1).wait_send()
+                passed(t, s, -1).wait_send()
+
+        every(sent)
 
         @pl.when(z > 0)
         def _():
-            z_copy(z, piece, shards, -1).wait_send()
+            for t in range(2):
+                z_copy(t, z, piece, shards, -1).wait_send()
+
+        x_copy(piece, side).wait_send()
 
         for k in range(2):
             halves(k).wait_send()
@@ -287,7 +272,7 @@
         pltpu.VMEM((rows, part), jnp.bfloat16),
         pltpu.VMEM((rows, part), jnp.bfloat16),
         pltpu.VMEM((rows, part), jnp.bfloat16),
-        dma((3,)), dma((3,)), dma((shards + 1,)), dma((shards,)), dma((shards,)), dma((shards,)),
+        dma((3,)), dma((3,)), dma((2, shards + 1)), dma((2, shards)), dma, dma,
         dma((2, shards)), dma((2, shards)), dma((2, shards)), dma((2, shards)), dma((2, shards)), dma((2, shards)),
         dma,
     ]
@@ -366,7 +351,7 @@
         mine[rows(k), :] = product(rows_of(side, k))
         if k == 0:
             settle()
-    hop(1)
+    cross_over()
     ends = []
     for k in range(2):
         swaps[k].wait_recv()
@@ -378,8 +363,8 @@
         ends.append(send(result.at[there, :], result.at[there, :], 2 + k))
         ends[k].start()
         if k == 0:
-            hops(2)
-    cross_over()
+            hop(1)
+    hops(2)
     spread()
     for end in ends:
         end.wait()
@@ -432,48 +417,6 @@
     distance = lax.broadcasted_iota(jnp.int32, shape, 0) + (keys - count) - lax.broadcasted_iota(jnp.int32, shape, 1)
     seen = (seg_rows[...] == seg_cols[...]) & (distance >= 0) & (distance < WINDOW)
     return jnp.where(seen, 0.0, -1e30)
-
-
-def attend_kernel(scale, query, prior, own, seg_rows, seg_cols, attended, log_total, bias):
-    count = query.shape[0]
-
-    @pl.when(pl.program_id(0) == 0)
-    def _():
-        bias[...] = allowed_bias(seg_rows, seg_cols, 2 * count)
-
-    early = dot_t(query[...], prior[0]) * scale + bias[:, :count]
-    later = dot_t(query[...], own[0]) * scale + bias[:, count:]
-    top = jnp.maximum(jnp.max(early, axis=-1, keepdims=True), jnp.max(later, axis=-1, keepdims=True))
-    early, later = jnp.exp(early - top), jnp.exp(later - top)
-    total = jnp.sum(early, axis=-1, keepdims=True) + jnp.sum(later, axis=-1, keepdims=True)
-    log_total[...] = top + jnp.log(total)
-    attended[...] = low(dot(low(early / total), prior[1]) + dot(low(later / total), own[1]))
-
-
-def attend(query, prior, own, seg_rows, seg_cols, head, scale):
-    count, inner = query.shape
-    heads = inner // head
-    return pl.pallas_call(
-        functools.partial(attend_kernel, scale),
-        grid=(heads,),
-        in_specs=[
-            pl.BlockSpec((count, head), lambda h: (0, h)),
-            pl.BlockSpec((2, count, head), lambda h: (0, 0, 0)),
-            pl.BlockSpec((2, count, head), lambda h: (0, 0, 0)),
-            pl.BlockSpec((count, 1), lambda h: (0, 0)),
-            pl.BlockSpec((1, 2 * count), lambda h: (0, 0)),
-        ],
-        out_specs=[
-            pl.BlockSpec((count, head), lambda h: (0, h)),
-            pl.BlockSpec((None, count, 1), lambda h: (h, 0, 0)),
-        ],
-        out_shape=[
-            jax.ShapeDtypeStruct((count, inner), jnp.bfloat16),
-            jax.ShapeDtypeStruct((heads, count, 1), jnp.float32),
-        ],
-        scratch_shapes=[pltpu.VMEM((count, 2 * count), jnp.float32)],
-        compiler_params=pltpu.CompilerParams(vmem_limit_bytes=56 * 2**20),
-    )(query, prior, own, seg_rows, seg_cols)
 
 
 def unrotate(grad, cosine, sine):
@@ -580,7 +523,7 @@
 def tables_kernel(
     queries, keys, early, late, output_own, output_other,
     output, out_attn, out_query, out_kv, out_out_in, out_out_out, out_ffn, out_gu, out_down_in, out_down_out,
-    marks, drawn, laid, mark_sem, drawn_sem, laid_sem, output_sem,
+    marks, drawn, laid, spots, placing, mark_sem, drawn_sem, laid_sem, output_sem,
 ):
     side = lax.axis_index("tensor")
     shards, rank = early.shape[1], early.shape[2]
@@ -651,31 +594,25 @@
             for lay in lays(u - 2):
                 lay.wait()
         _, _, size, targets = units[u]
-        lanes = min(256, size)
         slot = u % 2
-
-        def one(i, carry):
-            at = pl.ds(pl.multiple_of(i * lanes, lanes), lanes)
-            for t in range(len(targets)):
-                terms = []
-                for q in range(shards):
-                    term = wide(drawn[slot, t, q, :, at])
-                    if len(targets) == 1:
-                        term += wide(drawn[slot, 1, q, :, at])
-                    terms.append(term)
-                for k in range(adapters):
-                    total = terms[0] * wide(marks[0])[:, k : k + 1]
-                    for q in range(1, shards):
-                        total += terms[q] * wide(marks[q])[:, k : k + 1]
-                    laid[slot, t, k, :, at] = total
-            return carry
-
-        lax.fori_loop(0, size // lanes, one, 0)
+        for t in range(len(targets)):
+            terms = drawn[slot, t, :, :, :size].reshape(shards * rank, size)
+            total = dot(placing[...], terms)
+            if len(targets) == 1:
+                total += dot(placing[...], drawn[slot, 1, :, :, :size].reshape(shards * rank, size))
+            laid[slot, t, :, :, :size] = total.reshape(adapters, rank, size)
         for lay in lays(u):
             lay.start()
 
     draw(0).start()
     get_marks.wait()
+    same = lax.broadcasted_iota(jnp.int32, (rank, rank), 0) == lax.broadcasted_iota(jnp.int32, (rank, rank), 1)
+    same = same.astype(jnp.float32)
+    for q in range(shards):
+        mark = wide(marks[q])
+        for k in range(adapters):
+            spots[k * rank : (k + 1) * rank, q * rank : (q + 1) * rank] = same * mark[:, k : k + 1]
+    placing[...] = low(spots[...])
     for u in range(len(units)):
         lay_out(u, len(units))
     for u in (len(units) - 2, len(units) - 1):
@@ -707,6 +644,8 @@
             pltpu.VMEM((shards, rank, 128), bf16),
             pltpu.VMEM((2, 2, shards, rank, span), bf16),
             pltpu.VMEM((2, 2, adapters, rank, span), f32),
+            pltpu.VMEM((adapters * rank, shards * rank), f32),
+            pltpu.VMEM((adapters * rank, shards * rank), bf16),
             pltpu.SemaphoreType.DMA,
             pltpu.SemaphoreType.DMA((2,)),
             pltpu.SemaphoreType.DMA((2, 2)),
@@ -864,12 +803,14 @@
         sent[k] = low(result[half:])
         strip_send(k).start()
         mine[:, at] = result[:half]
-        for when, act in ((1, turn), (2, settle), (3, lambda: hop(1)), (4, lambda: hop(2)), (5, lambda: hops(3))):
+        for when, act in (
+            (1, turn), (2, settle), (4, cross_over), (7, lambda: hop(1)),
+        ):
             pl.when(k == when)(act)
         return carry
 
     lax.fori_loop(0, strips, cross, 0)
-    cross_over()
+    hop(2)
 
     def add(k, carry):
         at = pl.ds(pl.multiple_of(k * strip, strip), strip)
@@ -878,6 +819,7 @@
         return carry
 
     lax.fori_loop(0, strips, add, 0)
+    hops(3)
     attn_swaps = []
     for k in range(2):
         at = rows(k)
@@ -973,7 +915,7 @@
     across = lax.rem(c + 2, 4)
     beside = c + 1 - 2 * lax.rem(c, 2)
 
-    def greet(also=()):
+    def greet(also=(), row=False):
         barrier = pltpu.get_barrier_semaphore()
 
         def signal(place):
@@ -993,6 +935,17 @@
             signal({"shard": z + 1})
 
         peers = 2 + len(also) + lax.div(z + shards - 1, shards) + lax.div(2 * shards - 2 - z, shards)
+        if row:
+
+            @pl.when(c > 0)
+            def _():
+                signal({"context": c - 1})
+
+            @pl.when(c < 3)
+            def _():
+                signal({"context": c + 1})
+
+            peers = peers + lax.div(c + 3, 4) + lax.div(6 - c, 4)
         pl.semaphore_wait(barrier, peers)
 
     def region(piece, s, q):
@@ -1189,26 +1142,28 @@
     )(jnp.stack([chosen, side]), *tables, *arrays)
 
 
-FRONT_AXES = (0, 0, 0, 1)
+FRONT_AXES = (0, 0, 0, 1, 1, 1, 0, 1)
 
 
 def front_kernel(
-    shards, w_query, w_key, w_value, w_left, tokens, attn_in, query_out, kv_out, cosine, sine, gain_in, gain_query, gain_key,
-    full_query, full_key, full_value, full_left,
-    normed, code_attn, lin, lin_kv, query_rot, kv_rot,
-    held_query, held_key, held_value, held_left, query_w, key_w, value_w, load_sem, store_sem, weight_sem, *semaphores,
+    shards, *refs
 ):
-    sources, fulls = (w_query, w_key, w_value, w_left), (full_query, full_key, full_value, full_left)
-    held = (held_query, held_key, held_value, held_left)
+    sources, rest = refs[:8], refs[8:]
+    (tokens, attn_in, query_out, kv_out, cosine, sine, seg_rows, seg_cols, gain_in, gain_query, gain_key), rest = (
+        rest[:11], rest[11:]
+    )
+    fulls, rest = rest[:8], rest[8:]
+    (normed, code_attn, lin, lin_kv, query_rot, kv_rot, prior_out, attended, log_total), rest = rest[:9], rest[9:]
+    held, rest = rest[:8], rest[8:]
+    query_w, key_w, value_w, own, prior, bias, load_sem, store_sem, weight_sem, shift_sem, *semaphores = rest
+    c = lax.axis_index("context")
     greet, begin, relay, spread, finish, flush, own_place = mover(sources, fulls, semaphores, shards)
-    pieces = [
-        [(i, i, FRONT_AXES[i], 0, sources[i].shape[0], 0, sources[i].shape[1])] for i in range(4)
-    ]
-    greet()
-    for piece in pieces:
-        begin(piece)
-    loads = [pltpu.make_async_copy(sources[i], held[i], load_sem.at[i]) for i in range(4)]
-    stores = [pltpu.make_async_copy(held[i], own_place(i, FRONT_AXES[i]), store_sem.at[i]) for i in range(4)]
+    pieces = [(i, i, FRONT_AXES[i], 0, sources[i].shape[0], 0, sources[i].shape[1]) for i in range(8)]
+    needed, further = pieces[:4], pieces[4:]
+    greet(row=True)
+    begin(needed)
+    loads = [pltpu.make_async_copy(sources[i], held[i], load_sem.at[i]) for i in range(8)]
+    stores = [pltpu.make_async_copy(held[i], own_place(i, FRONT_AXES[i]), store_sem.at[i]) for i in range(8)]
     for load in loads:
         load.start()
     for load, store in zip(loads, stores):
@@ -1223,15 +1178,20 @@
         normed[at, :] = low(token * inverse_rms(token) * gain_in[...])
         return carry
 
-    for k, piece in enumerate(pieces):
-        relay(piece)
-        if k == 0:
-            lax.fori_loop(0, count // rows, norm, 0)
-            code_attn[...] = low(dot_t(normed[...], attn_in[...]))
-    for piece in pieces:
-        spread(piece)
-    for piece in pieces:
-        finish(piece)
+    relay(needed, 1, 1)
+    begin(further)
+    lax.fori_loop(0, count // rows, norm, 0)
+    code_attn[...] = low(dot_t(normed[...], attn_in[...]))
+    relay(needed, 2)
+    bias[...] = allowed_bias(seg_rows, seg_cols, 2 * count)
+
+    @pl.when(c == 0)
+    def _():
+        prior[...] = jnp.zeros_like(prior)
+
+    relay(further, 1, 1)
+    spread(needed)
+    finish(needed)
     for store in stores:
         store.wait()
     bring = [
@@ -1250,24 +1210,62 @@
         target[:, at : at + middle] = low(former * cosine[...] - latter * sine[...])
         target[:, at + middle : at + head] = low(latter * cosine[...] + former * sine[...])
 
+    bring[1].wait()
+    bring[2].wait()
+    values = dot(normed[...], key_w[...]) + dot(code_attn[:, rank : 2 * rank], kv_out[0])
+    lin_kv[:, :keys] = values
+    rotate(values * inverse_rms(values) * gain_key[...], own.at[0], 0)
+    values = dot(normed[...], value_w[...]) + dot(code_attn[:, 2 * rank :], kv_out[1])
+    lin_kv[:, keys:] = values
+    own[1] = low(values * inverse_rms(values))
+    shift = pltpu.make_async_remote_copy(
+        src_ref=own, dst_ref=prior, send_sem=shift_sem.at[0], recv_sem=shift_sem.at[1],
+        device_id={"context": c + 1}, device_id_type=MESH,
+    )
+    shifted_in = pltpu.make_async_remote_copy(
+        src_ref=own, dst_ref=prior, send_sem=shift_sem.at[0], recv_sem=shift_sem.at[1],
+        device_id={"context": c - 1}, device_id_type=MESH,
+    )
+
+    @pl.when(c < 3)
+    def _():
+        shift.start()
+
+    kv_rot[...] = own[...]
+    relay(further, 2, 2)
     bring[0].wait()
-    for h in range(queries // head):
+    heads = queries // head
+    for h in range(heads):
         at = slice(h * head, (h + 1) * head)
         values = dot(normed[...], query_w[:, at]) + dot(code_attn[:, :rank], query_out[:, at])
         lin[:, at] = values
         rotate(values * inverse_rms(values) * gain_query[...], query_rot, h * head)
-    bring[1].wait()
-    bring[2].wait()
-    for h in range(keys // head):
+    relay(further, 3)
+
+    @pl.when(c > 0)
+    def _():
+        shifted_in.wait_recv()
+
+    prior_out[...] = prior[...]
+    scale = 1.0 / math.sqrt(head)
+    for h in range(heads):
+        if h == 2:
+            spread(further)
         at = slice(h * head, (h + 1) * head)
-        values = dot(normed[...], key_w[:, at]) + dot(code_attn[:, rank : 2 * rank], kv_out[0, :, at])
-        lin_kv[:, at] = values
-        rotate(values * inverse_rms(values) * gain_key[...], kv_rot.at[0], h * head)
-        values = dot(normed[...], value_w[:, at]) + dot(code_attn[:, 2 * rank :], kv_out[1, :, at])
-        lin_kv[:, keys + h * head : keys + (h + 1) * head] = values
-        kv_rot[1, :, at] = low(values * inverse_rms(values))
-    for piece in pieces:
-        flush(piece)
+        early = dot_t(query_rot[:, at], prior[0]) * scale + bias[:, :count]
+        later = dot_t(query_rot[:, at], own[0]) * scale + bias[:, count:]
+        top = jnp.maximum(jnp.max(early, axis=-1, keepdims=True), jnp.max(later, axis=-1, keepdims=True))
+        early, later = jnp.exp(early - top), jnp.exp(later - top)
+        total = jnp.sum(early, axis=-1, keepdims=True) + jnp.sum(later, axis=-1, keepdims=True)
+        log_total[h] = top + jnp.log(total)
+        attended[:, at] = low(dot(low(early / total), prior[1]) + dot(low(later / total), own[1]))
+
+    @pl.when(c < 3)
+    def _():
+        shift.wait_send()
+
+    finish(further)
+    flush(pieces)
 
 
 def front(weights, arrays, shards):
@@ -1287,35 +1285,39 @@
             shape((count, 2 * keys), f32),
             shape((count, queries), bf16),
             shape((2, count, keys), bf16),
+            shape((2, count, keys), bf16),
+            shape((count, queries), bf16),
+            shape((queries // keys, count, 1), f32),
         ],
-        in_specs=[anywhere] * 4 + [vmem] * len(arrays),
-        out_specs=[anywhere] * 4 + [vmem] * 6,
+        in_specs=[anywhere] * 8 + [vmem] * len(arrays),
+        out_specs=[anywhere] * 8 + [vmem] * 9,
         scratch_shapes=[pltpu.VMEM(w.shape, w.dtype) for w in weights]
         + [pltpu.VMEM((width, n), bf16) for n in (queries, keys, keys)]
-        + [pltpu.SemaphoreType.DMA((4,)), pltpu.SemaphoreType.DMA((4,)), pltpu.SemaphoreType.DMA((3,))]
-        + mover_semaphores(4, shards),
+        + [pltpu.VMEM((2, count, keys), bf16), pltpu.VMEM((2, count, keys), bf16), pltpu.VMEM((count, 2 * count), f32)]
+        + [pltpu.SemaphoreType.DMA((n,)) for n in (8, 8, 3, 2)]
+        + mover_semaphores(8, shards),
         compiler_params=pltpu.CompilerParams(
             collective_id=0, has_side_effects=True, vmem_limit_bytes=60 * 2**20
         ),
     )(*weights, *arrays)
 
 
-FORE_AXES = (1, 1, 0, 1, 0, 0, 1)
+FORE_AXES = (0, 0, 1)
 
 
 def fore_kernel(
     shards, block,
-    w_output, w_right, w_lgate, w_lproj, w_gate, w_up, w_down,
-    attended, tokens, left, out_in, out_out, ffn_in, gu_out, down_in, down_out,
+    w_gate, w_up, w_down,
+    out_w, right_w, attended, tokens, left, out_in, out_out, ffn_in, gu_out, down_in, down_out,
     gain_in, gain_attn, gain_laurel, gain_pre,
-    full_output, full_right, full_lgate, full_lproj, full_gate, full_up, full_down, gate_out, up_out, ffn_out,
+    full_gate, full_up, full_down, gate_out, up_out, ffn_out,
     attn_proj, combined, laurel_mid, code_out, code_ffn, code_down, part,
-    stage_a, stage_b, stage_c, stage_d, stage_e, stage_f, stage_g, out_w, right_w, gate_w, up_w, down_w, sent, got, ffn, total, codes, hidden,
+    stage_a, stage_b, stage_c, gate_w, up_w, down_w, sent, got, ffn, total, codes, hidden,
     gate_keep, up_keep,
     load_sem, store_sem, weight_sem, keep_sem, ffn_sem, swap_send, swap_recv, *semaphores,
 ):
-    sources = (w_output, w_right, w_lgate, w_lproj, w_gate, w_up, w_down)
-    fulls = (full_output, full_right, full_lgate, full_lproj, full_gate, full_up, full_down)
+    sources = (w_gate, w_up, w_down)
+    fulls = (full_gate, full_up, full_down)
     side = lax.axis_index("tensor")
     partner = {"tensor": 1 - side}
     greet, begin, relay, spread, finish, flush, own_place = mover(sources, fulls, semaphores, shards)
@@ -1325,47 +1327,27 @@
     quarter = half // 2
     groups = w_gate.shape[1] // block
 
-    def whole(i):
-        return (i, i, FORE_AXES[i], 0, sources[i].shape[0], 0, sources[i].shape[1])
-
-    first = [whole(0), whole(1)]
-    small = [whole(2), whole(3)]
-
     def group(g):
-        base = 4 + 3 * g
+        base = 3 * g
         return [
-            (base, 4, 0, 0, sources[4].shape[0], g * block, block),
-            (base + 1, 5, 0, 0, sources[5].shape[0], g * block, block),
-            (base + 2, 6, 1, g * block, block, 0, sources[6].shape[1]),
+            (base, 0, 0, 0, sources[0].shape[0], g * block, block),
+            (base + 1, 1, 0, 0, sources[1].shape[0], g * block, block),
+            (base + 2, 2, 1, g * block, block, 0, sources[2].shape[1]),
         ]
 
     greet([partner])
-    begin(first)
     begin(group(0))
-    begin(small)
     begin(group(1))
-    stages = (stage_a, stage_b, stage_c, stage_d, stage_e, stage_f, stage_g)
-    loads = [pltpu.make_async_copy(sources[i], stages[i], load_sem.at[i]) for i in range(7)]
-    stores = [pltpu.make_async_copy(stages[i], own_place(i, FORE_AXES[i]), store_sem.at[i]) for i in range(7)]
+    stages = (stage_a, stage_b, stage_c)
+    loads = [pltpu.make_async_copy(sources[i], stages[i], load_sem.at[i]) for i in range(3)]
+    stores = [pltpu.make_async_copy(stages[i], own_place(i, FORE_AXES[i]), store_sem.at[i]) for i in range(3)]
     for load in loads:
         load.start()
     for load, store in zip(loads, stores):
         load.wait()
         store.start()
-    for store in stores:
-        store.wait()
-
-    relay(first)
-    spread(first)
-    finish(first)
-    load_out = pltpu.make_async_copy(full_output, out_w, weight_sem.at[0])
-    load_right = pltpu.make_async_copy(full_right, right_w, weight_sem.at[1])
-    load_out.start()
-    load_right.start()
     code = low(dot_t(attended[...], out_in[...]))
     code_out[...] = code
-    load_out.wait()
-    load_right.wait()
     mine = pl.ds(pl.multiple_of(side * half, half), half)
     theirs = pl.ds(pl.multiple_of((1 - side) * half, half), half)
     sent[...] = low(dot(attended[theirs, :], out_w[...]) + dot(code_out[theirs, :], out_out[...]))
@@ -1377,6 +1359,8 @@
     attn_proj[...] = dot(attended[mine, :], out_w[...]) + dot(code_out[mine, :], out_out[...])
 
     relay(group(0))
+    for store in stores:
+        store.wait()
     swap_attn.wait()
     rows = 64
 
@@ -1407,8 +1391,6 @@
             )
         )
         swaps[k].start()
-    relay(small)
-    spread(small)
     total[...] = jnp.zeros_like(total)
     codes[...] = jnp.zeros_like(codes)
 
@@ -1422,9 +1404,9 @@
     def weights(g):
         at = pl.ds(pl.multiple_of(g * block, block), block)
         return (
-            pltpu.make_async_copy(full_gate.at[:, at], gate_w, weight_sem.at[2]),
-            pltpu.make_async_copy(full_up.at[:, at], up_w, weight_sem.at[3]),
-            pltpu.make_async_copy(full_down.at[at, :], down_w, weight_sem.at[4]),
+            pltpu.make_async_copy(full_gate.at[:, at], gate_w, weight_sem.at[0]),
+            pltpu.make_async_copy(full_up.at[:, at], up_w, weight_sem.at[1]),
+            pltpu.make_async_copy(full_down.at[at, :], down_w, weight_sem.at[2]),
         )
 
     def climb(g):
@@ -1497,13 +1479,10 @@
     descend(groups - 1)
     code_down[...] = low(codes[...])
     part[...] = low(total[...] + dot(code_down[...], down_out[...]))
-    finish(small)
     for g in (groups - 2, groups - 1):
         for keep in keeps(g, g % 2):
             keep.wait()
     pltpu.make_async_copy(ffn, ffn_out, ffn_sem).wait()
-    flush(first)
-    flush(small)
 
     def flush_group(g, carry):
         flush(group(g))
@@ -1513,11 +1492,11 @@
 
 
 def fore(
-    weights, attended, tokens, left, out_in, out_out, ffn_in, gu_out, down_in, down_out, gains, shards
+    weights, out_w, right_w, attended, tokens, left, out_in, out_out, ffn_in, gu_out, down_in, down_out, gains, shards
 ):
     count = attended.shape[0]
     width = tokens.shape[1]
-    hidden = weights[4].shape[1]
+    hidden = weights[0].shape[1]
     half = count // 2
     rank = out_in.shape[0]
     block = min(512, hidden)
@@ -1540,12 +1519,10 @@
             shape((count, rank), bf16),
             shape((count, width), bf16),
         ],
-        in_specs=[anywhere] * 7 + [vmem] * 13,
-        out_specs=[anywhere] * 10 + [vmem] * 7,
+        in_specs=[anywhere] * 3 + [vmem] * 15,
+        out_specs=[anywhere] * 6 + [vmem] * 7,
         scratch_shapes=[
             *[pltpu.VMEM(w.shape, bf16) for w in weights],
-            pltpu.VMEM((weights[0].shape[0], width), bf16),
-            pltpu.VMEM((weights[1].shape[0], width), bf16),
             pltpu.VMEM((width, block), bf16),
             pltpu.VMEM((width, block), bf16),
             pltpu.VMEM((block, width), bf16),
@@ -1557,19 +1534,19 @@
             pltpu.VMEM((count, block), bf16),
             pltpu.VMEM((2, count, block), bf16),
             pltpu.VMEM((2, count, block), bf16),
-            pltpu.SemaphoreType.DMA((7,)),
-            pltpu.SemaphoreType.DMA((7,)),
-            pltpu.SemaphoreType.DMA((5,)),
+            pltpu.SemaphoreType.DMA((3,)),
+            pltpu.SemaphoreType.DMA((3,)),
+            pltpu.SemaphoreType.DMA((3,)),
             pltpu.SemaphoreType.DMA((2, 2)),
             pltpu.SemaphoreType.DMA,
             pltpu.SemaphoreType.DMA((3,)),
             pltpu.SemaphoreType.DMA((3,)),
         ]
-        + mover_semaphores(4 + 3 * groups, shards),
+        + mover_semaphores(3 * groups, shards),
         compiler_params=pltpu.CompilerParams(
             collective_id=1, has_side_effects=True, vmem_limit_bytes=60 * 2**20
         ),
-    )(*weights, attended, tokens, left, out_in, out_out, ffn_in, gu_out, down_in, down_out, *gains)
+    )(*weights, out_w, right_w, attended, tokens, left, out_in, out_out, ffn_in, gu_out, down_in, down_out, *gains)
 
 
 def body(
@@ -1643,27 +1620,26 @@
     before = jnp.sum((seg_all[None, :] < seg_query[:, None]).astype(jnp.int32), axis=1)
     own_pos = start_pos + jnp.arange(count, dtype=jnp.int32) - before
     cosine, sine_table = rope_tables(own_pos, head_size)
-    (
-        full_query, full_key, full_value, full_left, normed_b, code_attn, lin, lin_kv, query_rot, kv_own,
-    ) = front(
-        (w_query, w_key, w_value, laurel_left.T),
-        (
-            tokens[0], pick_attn_in, pick_query_out, pick_kv_out, cosine, sine_table,
-            gain_in[None], gain_query[None], gain_key[None],
-        ),
-        shards,
-    )
-    kv_prior = shifted(kv_own, "context", 1)
     seg_prior = lax.dynamic_slice_in_dim(seg_all, jnp.maximum(start_pos - count, 0), count, 0)
     seg_cols = jnp.concatenate([jnp.where(place > 0, seg_prior, -1), seg_query])[None, :]
     seg_rows = seg_query[:, None]
     score_scale = 1.0 / math.sqrt(head_size)
-    attended_b, log_total = attend(query_rot, kv_prior, kv_own, seg_rows, seg_cols, head_size, score_scale)
     (
-        full_output, full_right, full_layer_gate, full_layer_proj, full_gate, full_up, full_down,
+        full_query, full_key, full_value, full_left, full_output, full_right, full_layer_gate, full_layer_proj, normed_b,
+        code_attn, lin, lin_kv, query_rot, kv_own, kv_prior, attended_b, log_total,
+    ) = front(
+        (w_query, w_key, w_value, laurel_left.T, w_output, laurel_right, input_gate, input_proj),
+        (
+            tokens[0], pick_attn_in, pick_query_out, pick_kv_out, cosine, sine_table, seg_rows, seg_cols,
+            gain_in[None], gain_query[None], gain_key[None],
+        ),
+        shards,
+    )
+    (
+        full_gate, full_up, full_down,
         gate_b, up_b, ffn_b, attn_proj, combined, laurel_mid, code_out, code_ffn, code_down, down_part,
     ) = fore(
-        (w_output, laurel_right, input_gate, input_proj, w_gate, w_up, w_down),
+        (w_gate, w_up, w_down), full_output, full_right,
         attended_b, tokens_own, full_left,
         pick_out_in, pick_out_out, pick_ffn_in, pick_gu_out, pick_down_in, pick_down_out,
         (gain_in[None], gain_attn[None], gain_laurel[None], gain_pre[None]), shards,

time: 646 us -> 605 us (0.937)
  Pallas kernels: 619 us -> 583 us
    pallas_call x1, Pallas kernels: 296 us -> 254 us  [fore(): pl.pallas_call(functools.partial(fore_kernel, shards, block), out_shape=f...]
    pallas_call x1, Pallas kernels: 56.2 us -> 86.9 us  [front(): pl.pallas_call(functools.partial(front_kernel, shards), out_shape=full_sh...]
    pallas_call x1 -> x0, Pallas kernels: 8.84 us -> none  [attend(): pl.pallas_call(functools.partial(attend_kernel, scale), grid=(heads,), in...]
  transfers between devices with their start and end apart: 3 -> 2, of which waited for: 2 -> 1; matrix products, arithmetic and copies ran while one was open for 0% -> 0% of each run, Pallas kernels for 15% -> 15%
where the time goes in v5:
time: 605 us; the launch traced here: 599 us
  Pallas kernels  583 us (96%)
    pallas_call x1, Pallas kernels, fore(): pl.pallas_call(functools.partial(fore_kernel, shards, block), out_shape=f...  254 us
    pallas_call x1, Pallas kernels, aft(): pl.pallas_call(functools.partial(aft_kernel, shards, block, strip), out_s...  132 us
    pallas_call x1, Pallas kernels, front(): pl.pallas_call(functools.partial(front_kernel, shards), out_shape=full_sh...  86.9 us
    pallas_call x1, Pallas kernels, tail(): pl.pallas_call(functools.partial(tail_kernel, shards), out_shape=[jax.Sha...  69.6 us
    pallas_call x1, Pallas kernels, attend_back(): pl.pallas_call(functools.partial(attend_back_kernel, scale), grid=(inner...  19.1 us
    pallas_call x1, Pallas kernels, tables(): pl.pallas_call(functools.partial(tables_kernel, queries, keys), out_shape...  16.8 us
  transfers between devices with their start and end apart: 2, of which 1 were waited for; matrix products, arithmetic and copies ran while one was open for 0% of the time, Pallas kernels for 15%

profile of v5, /device:TPU:0, one launch (start us, length us, event | category | flops | bytes accessed | tf_op | source)
XLA Modules:
  0.0 598.8 jit_solution(9357567161881705847)
XLA Ops:
  1.3 0.8 broadcast_select_fusion
  2.2 0.6 pad_add_fusion
  2.8 1.3 convert_reduce_fusion
  4.0 0.9 copy.46.refs_14_.seg_rows
  4.9 0.6 pad_add_fusion.1.chosen
  5.5 1.8 multiply_sine_fusion
  7.3 4.3 shard_map.392
  11.6 86.9 %shard_map.393 = (bf16[2048,1024]{1,0:T(8,128)(2,1)}, bf16[2048,256]{1,0:T(8,128)(2,1)}, bf16[2048,256]{1,0:T(8,128)(2,1)}, bf16[64,2048]{1,0:T(8,128)(2,1)}, bf...) custom-call(bf16[512,1024]{1,0:T(8,128)(2,1)} %refs_0_.1, ...), custom_call_target="tpu_custom_call" | custom-call | tf_op jit(solution)/shard_map/pallas_call | solution.py:1278
  98.5 254.2 %shard_map.394 = (bf16[2048,4096]{1,0:T(8,128)(2,1)}, bf16[2048,4096]{1,0:T(8,128)(2,1)}, bf16[4096,2048]{1,0:T(8,128)(2,1)}, bf16[512,4096]{1,0:T(8,128)(2,1)},...) custom-call(bf16[512,4096]{1,0:T(8,128)(2,1)} %w_gate.1, ...), custom_call_target="tpu_custom_call" | custom-call | tf_op jit(solution)/shard_map/pallas_call | solution.py:1507
  352.7 0.6 iota.19.mark
  353.3 131.8 %shard_map.395 = (bf16[512,2048]{1,0:T(8,128)(2,1)}, bf16[2,4,16,18944]{3,2,1,0:T(8,128)(2,1)}, bf16[256,2048]{1,0:T(8,128)(2,1)}, f32[256,2048]{1,0:T(8,128)}, f32[256,2048]{1,0:T(8,128)}) custom-call(bf16[2048,4096]{1,0:T(8,128)(2,1)} %get-tuple-element.89.full_gate, bf16[2048,4096]{1,0:T(8,128)(2,1)} %get-tuple-element.90.full_up, ...), custom_call_target="tpu_custom_call" | custom-call | flops 25769803776 | bytes 67108864 | tf_op jit(solution)/shard_map/pallas_call | solution.py:868
  485.1 1.0 collective-permute-start.1
  486.1 19.1 %shard_map.396 = (bf16[512,1024]{1,0:T(8,128)(2,1)}, bf16[2,512,256]{2,1,0:T(8,128)(2,1)}, f32[2,512,256]{2,1,0:T(8,128)}, f32[16,1024]{1,0:T(8,128)}, f32[16,2048]{1,0:T(8,128)}) custom-call(bf16[512,2048]{1,0:T(8,128)(2,1)} %get-tuple-element.106.grad, bf16[1024,2048]{1,0:T(8,128)(2,1)} %get-tuple-element.78.out_w.w_out, ...), custom_call_target="tpu_custom_call" | custom-call | tf_op jit(solution)/shard_map/pallas_call | solution.py:481
  505.2 1.3 collective-permute-start
  506.5 2.7 collective-permute-done.came_kv
  509.2 0.0 copy-start.2
  509.2 0.8 copy-done.2
  510.0 69.6 %shard_map.397 = (bf16[512,2048]{1,0:T(8,128)(2,1)}, bf16[2,4,16,10752]{3,2,1,0:T(8,128)(2,1)}) custom-call(bf16[512,1024]{1,0:T(8,128)(2,1)} %get-tuple-element.113.grad_query, bf16[2048,1024]{1,0:T(8,128)(2,1)} %get-tuple-element.114.w_query, bf16[2048,256]{1,0:T(8,128)(2,1)} %get-tuple-element.115.w_key, bf16[2048,256]{1,0:T(8,128)(2,1)} %get-tuple-element.116.w_value, ...), custom_call_target="tpu_custom_call" | custom-call | tf_op jit(solution)/shard_map/pallas_call | solution.py:387
  579.5 0.0 collective-permute-done.1.output_other
  579.6 0.0 copy-start.1
  579.6 1.0 copy-done.1
  580.5 0.0 copy-start
  580.5 16.8 %shard_map.398 = (bf16[512,2048]{1,0:T(8,128)(2,1)}, f32[8,48,2048]{2,1,0:T(8,128)}, f32[8,16,2048]{2,1,0:T(8,128)}, f32[8,2,16,512]{3,2,1,0:T(8,128)}, f32[8,16...) custom-call(bf16[2,4,16,18944]{3,2,1,0:T(8,128)(2,1)} %get-tuple-ele, ...), custom_call_target="tpu_custom_call" | custom-call | tf_op jit(solution)/shard_map/pallas_call | solution.py:631
  597.3 0.0 copy-done
  597.3 1.3 copy.50
  (3 shorter events, 0.0 us)
Async XLA Ops:
  485.1 94.5 %collective-permute-start.1 = (bf16[256,2048]{1,0:T(8,128)(2,1)}, bf16[256,2048]{1,0:T(8,128)(2,1)S(1)}, u32[]{:S(2)}, u32[]{:S(2)}) collective-permute-start(bf16[256,2048]{1,0:T(8,128)(2,1)} %get-tuple-element.127.output_own), channel_id=1, source_target_pairs={{0,1},{1,0},{2,3},{3,2},{4,5},{5,4},{6,7},{7,6},{8,9},{9,8},{10,11... | collective-permute-start | bytes 3145736 | tf_op jit(solution)/shard_map/ppermute | solution.py:27
  505.2 4.0 collective-permute-start
  509.2 0.8 copy-start.2
  579.6 1.0 copy-start.1
  580.5 16.8 %copy-start = (bf16[512,2048]{1,0:T(8,128)(2,1)S(1)}, bf16[512,2048]{1,0:T(8,128)(2,1)}, u32[]{:S(2)}) copy-start(bf16[512,2048]{1,0:T(8,128)(2,1)} %get-tuple-element.129) | copy-start | bytes 6291460

commit v6 on v5

--- a/solution.py
+++ b/solution.py
@@ -810,8 +810,6 @@
         return carry
 
     lax.fori_loop(0, strips, cross, 0)
-    hop(2)
-
     def add(k, carry):
         at = pl.ds(pl.multiple_of(k * strip, strip), strip)
         strip_send(k).wait_recv()
@@ -819,7 +817,6 @@
         return carry
 
     lax.fori_loop(0, strips, add, 0)
-    hops(3)
     attn_swaps = []
     for k in range(2):
         at = rows(k)
@@ -831,6 +828,10 @@
         attn[there, :] = low(rms_back(proj, inverse_rms(proj), top * gain_attn[...]))
         attn_swaps.append(send(attn.at[there, :], attn.at[there, :], 4 + strips + k))
         attn_swaps[k].start()
+        if k == 0:
+            hop(2)
+        else:
+            hops(3)
         end = dot(laurel_mid[at, :], right[...])
         grad_end = low(rms_back(end, inverse_rms(end), top * gain_laurel[...]))
         grad_normed[at, :] = top + dot(low(dot_t(grad_end, right[...])), left[...])

time: 605 us -> 600 us (level)
    pallas_call x1, Pallas kernels: 132 us -> 125 us  [aft(): pl.pallas_call(functools.partial(aft_kernel, shards, block, strip), out_s...]
where the time goes in v6:
time: 600 us; the launch traced here: 594 us
  Pallas kernels  577 us (96%)
    pallas_call x1, Pallas kernels, fore(): pl.pallas_call(functools.partial(fore_kernel, shards, block), out_shape=f...  254 us
    pallas_call x1, Pallas kernels, aft(): pl.pallas_call(functools.partial(aft_kernel, shards, block, strip), out_s...  125 us
    pallas_call x1, Pallas kernels, front(): pl.pallas_call(functools.partial(front_kernel, shards), out_shape=full_sh...  86.9 us
    pallas_call x1, Pallas kernels, tail(): pl.pallas_call(functools.partial(tail_kernel, shards), out_shape=[jax.Sha...  71.3 us
    pallas_call x1, Pallas kernels, attend_back(): pl.pallas_call(functools.partial(attend_back_kernel, scale), grid=(inner...  19.1 us
    pallas_call x1, Pallas kernels, tables(): pl.pallas_call(functools.partial(tables_kernel, queries, keys), out_shape...  16.8 us
  transfers between devices with their start and end apart: 2, of which 1 were waited for; matrix products, arithmetic and copies ran while one was open for 0% of the time, Pallas kernels for 15%

profile of v6, /device:TPU:0, one launch (start us, length us, event | category | flops | bytes accessed | tf_op | source)
XLA Modules:
  0.0 593.9 jit_solution(13312810713442529850)
XLA Ops:
  1.3 0.8 broadcast_select_fusion
  2.2 0.6 pad_add_fusion
  2.8 1.3 convert_reduce_fusion
  4.0 0.9 copy.46.refs_14_.seg_rows
  4.9 0.6 pad_add_fusion.1.chosen
  5.5 1.8 multiply_sine_fusion
  7.3 4.3 shard_map.392
  11.6 86.9 %shard_map.393 = (bf16[2048,1024]{1,0:T(8,128)(2,1)}, bf16[2048,256]{1,0:T(8,128)(2,1)}, bf16[2048,256]{1,0:T(8,128)(2,1)}, bf16[64,2048]{1,0:T(8,128)(2,1)}, bf...) custom-call(bf16[512,1024]{1,0:T(8,128)(2,1)} %refs_0_.1, ...), custom_call_target="tpu_custom_call" | custom-call | tf_op jit(solution)/shard_map/pallas_call | solution.py:1279
  98.5 254.2 %shard_map.394 = (bf16[2048,4096]{1,0:T(8,128)(2,1)}, bf16[2048,4096]{1,0:T(8,128)(2,1)}, bf16[4096,2048]{1,0:T(8,128)(2,1)}, bf16[512,4096]{1,0:T(8,128)(2,1)},...) custom-call(bf16[512,4096]{1,0:T(8,128)(2,1)} %w_gate.1, ...), custom_call_target="tpu_custom_call" | custom-call | tf_op jit(solution)/shard_map/pallas_call | solution.py:1508
  352.7 0.6 iota.19.mark
  353.3 124.7 %shard_map.395 = (bf16[512,2048]{1,0:T(8,128)(2,1)}, bf16[2,4,16,18944]{3,2,1,0:T(8,128)(2,1)}, bf16[256,2048]{1,0:T(8,128)(2,1)}, f32[256,2048]{1,0:T(8,128)}, f32[256,2048]{1,0:T(8,128)}) custom-call(bf16[2048,4096]{1,0:T(8,128)(2,1)} %get-tuple-element.89.full_gate, bf16[2048,4096]{1,0:T(8,128)(2,1)} %get-tuple-element.90.full_up, ...), custom_call_target="tpu_custom_call" | custom-call | flops 25769803776 | bytes 67108864 | tf_op jit(solution)/shard_map/pallas_call | solution.py:869
  477.9 1.2 collective-permute-start.1
  479.1 19.1 %shard_map.396 = (bf16[512,1024]{1,0:T(8,128)(2,1)}, bf16[2,512,256]{2,1,0:T(8,128)(2,1)}, f32[2,512,256]{2,1,0:T(8,128)}, f32[16,1024]{1,0:T(8,128)}, f32[16,2048]{1,0:T(8,128)}) custom-call(bf16[512,2048]{1,0:T(8,128)(2,1)} %get-tuple-element.106.grad, bf16[1024,2048]{1,0:T(8,128)(2,1)} %get-tuple-element.78.out_w.w_out, ...), custom_call_target="tpu_custom_call" | custom-call | tf_op jit(solution)/shard_map/pallas_call | solution.py:481
  498.2 1.3 collective-permute-start
  499.5 2.7 collective-permute-done.came_kv
  502.2 0.0 copy-start.2
  502.2 0.8 copy-done.2
  503.0 71.3 %shard_map.397 = (bf16[512,2048]{1,0:T(8,128)(2,1)}, bf16[2,4,16,10752]{3,2,1,0:T(8,128)(2,1)}) custom-call(bf16[512,1024]{1,0:T(8,128)(2,1)} %get-tuple-element.113.grad_query, bf16[2048,1024]{1,0:T(8,128)(2,1)} %get-tuple-element.114.w_query, bf16[2048,256]{1,0:T(8,128)(2,1)} %get-tuple-element.115.w_key, bf16[2048,256]{1,0:T(8,128)(2,1)} %get-tuple-element.116.w_value, ...), custom_call_target="tpu_custom_call" | custom-call | tf_op jit(solution)/shard_map/pallas_call | solution.py:387
  574.4 0.0 collective-permute-done.1.output_other
  574.4 0.0 copy-start.1
  574.4 1.0 copy-done.1
  575.4 0.0 copy-start
  575.4 16.8 %shard_map.398 = (bf16[512,2048]{1,0:T(8,128)(2,1)}, f32[8,48,2048]{2,1,0:T(8,128)}, f32[8,16,2048]{2,1,0:T(8,128)}, f32[8,2,16,512]{3,2,1,0:T(8,128)}, f32[8,16...) custom-call(bf16[2,4,16,18944]{3,2,1,0:T(8,128)(2,1)} %get-tuple-ele, ...), custom_call_target="tpu_custom_call" | custom-call | tf_op jit(solution)/shard_map/pallas_call | solution.py:631
  592.1 0.0 copy-done
  592.1 1.3 copy.50
  (3 shorter events, 0.0 us)
Async XLA Ops:
  477.9 96.4 %collective-permute-start.1 = (bf16[256,2048]{1,0:T(8,128)(2,1)}, bf16[256,2048]{1,0:T(8,128)(2,1)S(1)}, u32[]{:S(2)}, u32[]{:S(2)}) collective-permute-start(bf16[256,2048]{1,0:T(8,128)(2,1)} %get-tuple-element.127.output_own), channel_id=1, source_target_pairs={{0,1},{1,0},{2,3},{3,2},{4,5},{5,4},{6,7},{7,6},{8,9},{9,8},{10,11... | collective-permute-start | bytes 3145736 | tf_op jit(solution)/shard_map/ppermute | solution.py:27
  498.2 4.0 collective-permute-start
  502.2 0.8 copy-start.2
  574.4 1.0 copy-start.1
  575.4 16.8 %copy-start = (bf16[512,2048]{1,0:T(8,128)(2,1)S(1)}, bf16[512,2048]{1,0:T(8,128)(2,1)}, u32[]{:S(2)}) copy-start(bf16[512,2048]{1,0:T(8,128)(2,1)} %get-tuple-element.129) | copy-start | bytes 6291460
